TPU v7x, 32 devices: a whole 2x2x4 slice. The times are simulated.
32 devices in a mesh: expert: 4 (over y, x), context: 4 (over z), dp: 2 (over core).
Axes of the slice: x: 2, y: 2, z: 4, core: 2. Of those that a mesh axis runs over, the one named last changes fastest.
Arguments:
- tokens: bfloat16 [8, 1024, 2048], P('expert', ('context', 'dp')), may hold values from -6 to 6
- block_ids: int32 [8, 1024], P('expert', ('context', 'dp')), may hold values from 0 to 7, never falling along the last dimension, each value on 1 to 256 neighbouring positions
- routes: int32 [8, 1024, 8], P('expert', ('context', 'dp')), may hold values from 0 to 15, all different within a row
- norm_gains: bfloat16 [2048, 4], P(('expert', 'context', 'dp')), may hold values from 0.099609375 to 1.8984375
- w_query: bfloat16 [2048, 2048], P(('expert', 'context', 'dp')), may hold values from -0.125 to 0.125
- w_key: bfloat16 [2048, 2048], P(('expert', 'context', 'dp')), may hold values from -0.125 to 0.125
- w_value: bfloat16 [2048, 2048], P(('expert', 'context', 'dp')), may hold values from -0.125 to 0.125
- w_output: bfloat16 [2048, 2048], P(('expert', 'context', 'dp')), may hold values from -3 to 3
- router: bfloat16 [2048, 16], P(('expert', 'context', 'dp')), may hold values from -0.0625 to 0.0625
- expert_gate: bfloat16 [16, 2048, 1024], P(('expert', 'context')), may hold values from -0.125 to 0.125
- expert_up: bfloat16 [16, 2048, 1024], P(('expert', 'context')), may hold values from -0.125 to 0.125
- expert_down: bfloat16 [16, 1024, 2048], P(('expert', 'context')), may hold values from -1 to 1
- cotangent: bfloat16 [8, 1024, 2048], P('expert', ('context', 'dp')), may hold values from -6 to 6
Outputs:
- activations: bfloat16 [8, 1024, 2048], P('expert', ('context', 'dp'))
- input_grad: float32 [8, 1024, 2048], P('expert', ('context', 'dp'))
- grad_gains: float32 [2048, 4], P(('expert', 'context', 'dp'))
- grad_query: float32 [2048, 2048], P(('expert', 'context', 'dp'))
- grad_key: float32 [2048, 2048], P(('expert', 'context', 'dp'))
- grad_value: float32 [2048, 2048], P(('expert', 'context', 'dp'))
- grad_output: float32 [2048, 2048], P(('expert', 'context', 'dp'))
- grad_router: float32 [2048, 16], P(('expert', 'context', 'dp'))
- grad_gate: float32 [16, 2048, 1024], P(('expert', 'context'), None, 'dp')
- grad_up: float32 [16, 2048, 1024], P(('expert', 'context'), None, 'dp')
- grad_down: float32 [16, 1024, 2048], P(('expert', 'context'), 'dp')
Inputs may be any that keep to these rules, and one draw needn't show every extreme that they name: `block_ids`: block ids never fall along a sequence; one block holds at most 256 tokens. `routes`: each token names 8 different experts; a smaller position is a higher priority for slots.
All inputs are finite; a program needn't handle non-finite values.
Results may differ from a plain program's by a relative error of at most 0.017.
Values may be sent and summed in bfloat16 or wider, within the bound.
A program may use at most 200 MiB of HBM per device.

v0:
```python
import jax
import jax.numpy as jnp
from jax import lax
from jax.sharding import PartitionSpec as P

HEADS = 16
HEAD = 128


epsilon = 1e-05
masked_value = -1e30


def rms_factor(values):
    return lax.rsqrt(jnp.mean(values * values, axis=-1, keepdims=True) + epsilon)


def norm_back(grad_hat, hatted, factor):
    return factor * (grad_hat - hatted * jnp.mean(grad_hat * hatted, axis=-1, keepdims=True))


def contract_rows(first_array, second_array):
    return lax.dot_general(
        first_array, second_array, (((0,), (0,)), ((), ())), preferred_element_type=jnp.float32
    )


def contract_last(first_array, second_array):
    return lax.dot_general(
        first_array, second_array, (((1,), (1,)), ((), ())), preferred_element_type=jnp.float32
    )


def block_slots(route_block, experts, capacity):
    pair_expert = route_block.T.reshape(-1)
    pair_count = pair_expert.shape[0]
    onehot = (pair_expert[:, None] == jnp.arange(experts, dtype=jnp.int32)[None, :]).astype(
        jnp.int32
    )
    earlier = jnp.cumsum(onehot, axis=0) - onehot
    slot_index = jnp.sum(earlier * onehot, axis=1)
    kept_pair = slot_index < capacity
    target = jnp.where(kept_pair, pair_expert * capacity + slot_index, 0)
    cell_index = jnp.arange(experts * capacity, dtype=jnp.int32)
    matches = jnp.logical_and(target[None, :] == cell_index[:, None], kept_pair[None, :])
    filled = jnp.any(matches, axis=1)
    source = jnp.sum(
        jnp.where(matches, jnp.arange(pair_count, dtype=jnp.int32)[None, :], 0), axis=1
    )
    return (kept_pair, target, filled, source)


def send_inputs(buffer):
    return lax.all_to_all(buffer, ("expert", "context"), split_axis=0, concat_axis=0, tiled=True)


def return_outputs(buffer):
    return lax.all_to_all(buffer, ("expert", "context"), split_axis=0, concat_axis=0, tiled=True)


def send_grads(buffer):
    return lax.all_to_all(buffer, ("expert", "context"), split_axis=0, concat_axis=0, tiled=True)


def return_grads(buffer):
    return lax.all_to_all(buffer, ("expert", "context"), split_axis=0, concat_axis=0, tiled=True)


def body(
    tokens,
    block_ids,
    routes,
    norm_gains,
    w_query,
    w_key,
    w_value,
    w_output,
    router,
    expert_gate,
    expert_up,
    expert_down,
    cotangent,
):
    batches, seq_dev, model_width = tokens.shape
    top_choices = routes.shape[2]
    local_experts = expert_gate.shape[0]
    hidden_units = expert_gate.shape[2]
    experts = local_experts * lax.axis_size(("expert", "context"))
    capacity = max(2, seq_dev * top_choices // experts)
    pair_count = top_choices * seq_dev
    score_scale = HEAD ** (-0.5)
    expert_ids = jnp.arange(experts, dtype=jnp.int32)
    sum_gate = jnp.zeros((local_experts, model_width, hidden_units), jnp.float32)
    sum_up = jnp.zeros((local_experts, model_width, hidden_units), jnp.float32)
    sum_down = jnp.zeros((local_experts, model_width, hidden_units), jnp.float32)
    kept_operands = []
    layer_outputs = []
    input_grads = []
    for batch_index in range(batches):
        full_query, full_key, full_value, full_output, full_router, full_gains = (
            lax.all_gather(w_query, ("expert", "context", "dp"), axis=0, tiled=True),
            lax.all_gather(w_key, ("expert", "context", "dp"), axis=0, tiled=True),
            lax.all_gather(w_value, ("expert", "context", "dp"), axis=0, tiled=True),
            lax.all_gather(w_output, ("expert", "context", "dp"), axis=0, tiled=True),
            lax.all_gather(router, ("expert", "context", "dp"), axis=0, tiled=True),
            lax.all_gather(norm_gains, ("expert", "context", "dp"), axis=0, tiled=True),
        )
        gain_cols = full_gains.astype(jnp.float32)
        inputs = tokens[batch_index].astype(jnp.float32)
        first_factor = rms_factor(inputs)
        first_hat = inputs * first_factor
        normed = (first_hat * gain_cols[:, 0]).astype(jnp.bfloat16)
        query_raw = jnp.dot(normed, full_query, preferred_element_type=jnp.float32)
        key_raw = jnp.dot(normed, full_key, preferred_element_type=jnp.float32)
        value_low = jnp.dot(normed, full_value, preferred_element_type=jnp.float32).astype(
            jnp.bfloat16
        )
        query_factor = rms_factor(query_raw)
        query_hat = query_raw * query_factor
        query_low = (query_hat * gain_cols[:, 1]).astype(jnp.bfloat16)
        key_factor = rms_factor(key_raw)
        key_hat = key_raw * key_factor
        key_low = (key_hat * gain_cols[:, 2]).astype(jnp.bfloat16)
        block_local = block_ids[batch_index]
        key_all, value_all, block_all = (
            lax.all_gather(key_low, ("context", "dp"), axis=0, tiled=True),
            lax.all_gather(value_low, ("context", "dp"), axis=0, tiled=True),
            lax.all_gather(block_local, ("context", "dp"), axis=0, tiled=True),
        )
        seq_len = key_all.shape[0]
        query_heads = query_low.reshape(seq_dev, HEADS, HEAD)
        key_heads = key_all.reshape(seq_len, HEADS, HEAD)
        value_heads = value_all.reshape(seq_len, HEADS, HEAD)
        allowed = block_all[None, None, :] <= block_local[None, :, None]

        def masked_scores():
            raw_scores = (
                jnp.einsum(
                    "qhd,khd->hqk", query_heads, key_heads, preferred_element_type=jnp.float32
                )
                * score_scale
            )
            return jnp.where(allowed, raw_scores, masked_value)

        scores = masked_scores()
        row_peak = jnp.max(scores, axis=-1, keepdims=True)
        exponent = jnp.exp(scores - row_peak)
        row_total = jnp.sum(exponent, axis=-1, keepdims=True)
        log_total = row_peak + jnp.log(row_total)
        attn_probs = (exponent / row_total).astype(jnp.bfloat16)
        mixed_low = jnp.einsum(
            "hqk,khd->qhd", attn_probs, value_heads, preferred_element_type=jnp.float32
        )
        mixed_low = mixed_low.reshape(seq_dev, model_width).astype(jnp.bfloat16)
        resid = inputs + jnp.dot(mixed_low, full_output, preferred_element_type=jnp.float32)
        second_factor = rms_factor(resid)
        second_hat = resid * second_factor
        second_low = (second_hat * gain_cols[:, 3]).astype(jnp.bfloat16)
        logits = jnp.dot(second_low, full_router, preferred_element_type=jnp.float32)
        router_probs = jax.nn.softmax(logits, axis=-1)
        route_local = routes[batch_index]
        gate_vals = jnp.take_along_axis(router_probs, route_local, axis=1)
        kept_pair, target, filled, source = block_slots(route_local, experts, capacity)
        kept_float = kept_pair.astype(jnp.float32)
        filled_low = filled.astype(jnp.bfloat16)[:, None]
        token_of_slot = source % seq_dev
        send_rows = (jnp.take(second_low, token_of_slot, axis=0) * filled_low).reshape(
            experts, capacity, model_width
        )
        received = send_inputs(send_rows)
        shaped_in = received.reshape(-1, local_experts, capacity, model_width)
        gate_pre = jnp.einsum(
            "secd,edf->secf", shaped_in, expert_gate, preferred_element_type=jnp.float32
        )
        up_pre = jnp.einsum(
            "secd,edf->secf", shaped_in, expert_up, preferred_element_type=jnp.float32
        )
        sigmoid_gate = jax.nn.sigmoid(gate_pre)
        silu_gate = gate_pre * sigmoid_gate
        act_low = (silu_gate * up_pre).astype(jnp.bfloat16)
        expert_low = jnp.einsum(
            "secf,efd->secd", act_low, expert_down, preferred_element_type=jnp.float32
        )
        expert_low = expert_low.astype(jnp.bfloat16).reshape(experts, capacity, model_width)
        returned = return_outputs(expert_low).reshape(experts * capacity, model_width)
        pair_out = (
            jnp.take(returned, target, axis=0)
            .astype(jnp.float32)
            .reshape(top_choices, seq_dev, model_width)
        )
        pair_weight = (gate_vals.T.reshape(-1) * kept_float).reshape(top_choices, seq_dev)
        mixture = jnp.sum(pair_weight[:, :, None] * pair_out, axis=0)
        layer_outputs.append((resid + mixture).astype(jnp.bfloat16))
        upstream = cotangent[batch_index].astype(jnp.float32)
        gate_grad = kept_float.reshape(top_choices, seq_dev) * jnp.sum(
            pair_out * upstream[None], axis=-1
        )
        pair_grad = (
            (pair_weight[:, :, None] * upstream[None])
            .astype(jnp.bfloat16)
            .reshape(pair_count, model_width)
        )
        grad_rows = (jnp.take(pair_grad, source, axis=0) * filled_low).reshape(
            experts, capacity, model_width
        )
        grad_recv = send_grads(grad_rows).reshape(-1, local_experts, capacity, model_width)
        act_grad = jnp.einsum(
            "secd,efd->secf", grad_recv, expert_down, preferred_element_type=jnp.float32
        )
        gate_grad_pre = (
            act_grad * up_pre * sigmoid_gate * (1.0 + gate_pre * (1.0 - sigmoid_gate))
        ).astype(jnp.bfloat16)
        up_grad_pre = (act_grad * silu_gate).astype(jnp.bfloat16)
        input_back = jnp.einsum(
            "secf,edf->secd", gate_grad_pre, expert_gate, preferred_element_type=jnp.float32
        )
        input_back = input_back + jnp.einsum(
            "secf,edf->secd", up_grad_pre, expert_up, preferred_element_type=jnp.float32
        )
        input_back = input_back.astype(jnp.bfloat16).reshape(experts, capacity, model_width)
        sum_gate = sum_gate + jnp.einsum(
            "secd,secf->edf", shaped_in, gate_grad_pre, preferred_element_type=jnp.float32
        )
        sum_up = sum_up + jnp.einsum(
            "secd,secf->edf", shaped_in, up_grad_pre, preferred_element_type=jnp.float32
        )
        sum_down = sum_down + jnp.einsum(
            "secd,secf->edf", grad_recv, act_low, preferred_element_type=jnp.float32
        )
        back_rows = return_grads(input_back).reshape(experts * capacity, model_width)
        pair_back = jnp.take(back_rows, target, axis=0).astype(jnp.float32) * kept_float[:, None]
        second_grad = jnp.sum(pair_back.reshape(top_choices, seq_dev, model_width), axis=0)
        route_match = (route_local[:, :, None] == expert_ids[None, None, :]).astype(jnp.float32)
        prob_grad = jnp.sum(gate_grad.T[:, :, None] * route_match, axis=1)
        logit_grad = router_probs * (
            prob_grad - jnp.sum(router_probs * prob_grad, axis=-1, keepdims=True)
        )
        logit_grad = logit_grad.astype(jnp.bfloat16)
        second_grad = second_grad + contract_last(logit_grad, full_router)
        gain_second = jnp.sum(second_grad * second_hat, axis=0)
        resid_grad = upstream + norm_back(second_grad * gain_cols[:, 3], second_hat, second_factor)
        attn_grad = resid_grad.astype(jnp.bfloat16)
        mixed_grad = contract_last(attn_grad, full_output).astype(jnp.bfloat16)
        mixed_heads = mixed_grad.reshape(seq_dev, HEADS, HEAD)
        probs_again = jnp.exp(masked_scores() - log_total)
        probs_again_low = probs_again.astype(jnp.bfloat16)
        value_prod = jnp.einsum(
            "qhd,khd->hqk", mixed_heads, value_heads, preferred_element_type=jnp.float32
        )
        row_delta = jnp.sum(probs_again * value_prod, axis=-1, keepdims=True)
        score_grad = (probs_again * (value_prod - row_delta)).astype(jnp.bfloat16)
        query_grad = jnp.einsum(
            "hqk,khd->qhd", score_grad, key_heads, preferred_element_type=jnp.float32
        )
        query_grad = query_grad.reshape(seq_dev, model_width) * score_scale
        row_count = seq_dev * lax.axis_size(("context", "dp"))
        key_part = (
            jnp.einsum("hqk,qhd->khd", score_grad, query_heads, preferred_element_type=jnp.float32)
            * score_scale
        )
        value_part = jnp.einsum(
            "hqk,qhd->khd", probs_again_low, mixed_heads, preferred_element_type=jnp.float32
        )
        key_value_grad = lax.psum_scatter(
            jnp.concatenate(
                [
                    key_part.reshape(row_count, model_width),
                    value_part.reshape(row_count, model_width),
                ],
                axis=1,
            ),
            ("context", "dp"),
            scatter_dimension=0,
            tiled=True,
        )
        key_grad = key_value_grad[:, :model_width]
        value_grad = key_value_grad[:, model_width:]
        gain_query = jnp.sum(query_grad * query_hat, axis=0)
        gain_key = jnp.sum(key_grad * key_hat, axis=0)
        query_raw_grad = norm_back(query_grad * gain_cols[:, 1], query_hat, query_factor).astype(
            jnp.bfloat16
        )
        key_raw_grad = norm_back(key_grad * gain_cols[:, 2], key_hat, key_factor).astype(
            jnp.bfloat16
        )
        value_raw_grad = value_grad.astype(jnp.bfloat16)
        first_grad = contract_last(query_raw_grad, full_query) + contract_last(
            key_raw_grad, full_key
        )
        first_grad = first_grad + contract_last(value_raw_grad, full_value)
        gain_first = jnp.sum(first_grad * first_hat, axis=0)
        input_grads.append(
            resid_grad + norm_back(first_grad * gain_cols[:, 0], first_hat, first_factor)
        )
        gain_stack = jnp.stack([gain_first, gain_query, gain_key, gain_second], axis=1)
        kept_operands.append(
            (
                normed,
                query_raw_grad,
                key_raw_grad,
                value_raw_grad,
                mixed_low,
                attn_grad,
                second_low,
                logit_grad,
                gain_stack,
            )
        )
    stacked = tuple(
        (jnp.concatenate([entry[index] for entry in kept_operands], axis=0) for index in range(8))
    )
    gain_total = kept_operands[0][8]
    for entry in kept_operands[1:]:
        gain_total = gain_total + entry[8]
    all_grads = (
        contract_rows(stacked[0], stacked[1]),
        contract_rows(stacked[0], stacked[2]),
        contract_rows(stacked[0], stacked[3]),
        contract_rows(stacked[4], stacked[5]),
        contract_rows(stacked[6], stacked[7]),
        gain_total,
    )
    weight_shares = (
        lax.psum_scatter(
            all_grads[0], ("expert", "context", "dp"), scatter_dimension=0, tiled=True
        ),
        lax.psum_scatter(
            all_grads[1], ("expert", "context", "dp"), scatter_dimension=0, tiled=True
        ),
        lax.psum_scatter(
            all_grads[2], ("expert", "context", "dp"), scatter_dimension=0, tiled=True
        ),
        lax.psum_scatter(
            all_grads[3], ("expert", "context", "dp"), scatter_dimension=0, tiled=True
        ),
        lax.psum_scatter(
            all_grads[4], ("expert", "context", "dp"), scatter_dimension=0, tiled=True
        ),
        lax.psum_scatter(
            all_grads[5], ("expert", "context", "dp"), scatter_dimension=0, tiled=True
        ),
    )
    gate_share, up_share, down_share = (
        lax.psum_scatter(
            sum_gate.astype(jnp.bfloat16), "dp", scatter_dimension=2, tiled=True
        ).astype(jnp.float32),
        lax.psum_scatter(sum_up.astype(jnp.bfloat16), "dp", scatter_dimension=2, tiled=True).astype(
            jnp.float32
        ),
        lax.psum_scatter(
            sum_down.astype(jnp.bfloat16), "dp", scatter_dimension=2, tiled=True
        ).astype(jnp.float32),
    )
    down_share = jnp.swapaxes(down_share, 1, 2)
    return (
        jnp.stack(layer_outputs, axis=0),
        jnp.stack(input_grads, axis=0),
        weight_shares[5],
        weight_shares[0],
        weight_shares[1],
        weight_shares[2],
        weight_shares[3],
        weight_shares[4],
        gate_share,
        up_share,
        down_share,
    )


def solution(mesh):
    return jax.shard_map(
        body,
        mesh=mesh,
        in_specs=(
            P("expert", ("context", "dp"), None),
            P("expert", ("context", "dp")),
            P("expert", ("context", "dp"), None),
            P(("expert", "context", "dp"), None),
            P(("expert", "context", "dp"), None),
            P(("expert", "context", "dp"), None),
            P(("expert", "context", "dp"), None),
            P(("expert", "context", "dp"), None),
            P(("expert", "context", "dp"), None),
            P(("expert", "context"), None, None),
            P(("expert", "context"), None, None),
            P(("expert", "context"), None, None),
            P("expert", ("context", "dp"), None),
        ),
        out_specs=(
            P("expert", ("context", "dp"), None),
            P("expert", ("context", "dp"), None),
            P(("expert", "context", "dp"), None),
            P(("expert", "context", "dp"), None),
            P(("expert", "context", "dp"), None),
            P(("expert", "context", "dp"), None),
            P(("expert", "context", "dp"), None),
            P(("expert", "context", "dp"), None),
            P(("expert", "context"), None, "dp"),
            P(("expert", "context"), None, "dp"),
            P(("expert", "context"), "dp", None),
        ),
        check_vma=False,
    )
```

profile of v0, /device:TPU:1, one launch (start us, length us, event | category | flops | bytes accessed | tf_op | source)
XLA Modules:
  0.0 3076.3 jit_solution(10201825135469429739)
XLA Ops:
  9.4 43.5 %all-gather.2 = bf16[32,64,4]{1,2,0:T(4,128)(2,1)S(1)} all-gather(bf16[1,64,4]{1,2,0:T(4,128)(2,1)} %bitcast.601), channel_id=1, replica_groups=mesh['expert'=4,'context'=4,'dp'=2] {'expert','context','dp'}, dimensions={0}, use_global_device_ids=true | all-gather | bytes 16896 | tf_op jit(solution)/shard_map/all_gather | solution.py:106
  56.2 34.8 %all-gather.19.cloned.1.call-done = bf16[2048,2048]{1,0:T(8,128)(2,1)} async-done(((bf16[64,2048]{1,0:T(8,128)(2,1)}), bf16[2048,2048]{1,0:T(8,128)(2,1)}) %all-gather.19.cloned.1.call-update) | async-done | bytes 8388624 | tf_op jit(solution)/shard_map/all_gather | solution.py:102
  99.6 70.3 %all-gather.13.cloned.1.call-done = bf16[2048,2048]{1,0:T(8,128)(2,1)} async-done(((bf16[64,2048]{1,0:T(8,128)(2,1)}), bf16[2048,2048]{1,0:T(8,128)(2,1)}) %all-gather.13.cloned.1.call-update) | async-done | bytes 8388624 | tf_op jit(solution)/shard_map/all_gather | solution.py:103
  200.8 48.1 %all-gather.17.cloned.1.call-done = bf16[2048,2048]{1,0:T(8,128)(2,1)} async-done(((bf16[64,2048]{1,0:T(8,128)(2,1)}), bf16[2048,2048]{1,0:T(8,128)(2,1)}) %all-gather.17.cloned.1.call-update) | async-done | bytes 8388624 | tf_op jit(solution)/shard_map/all_gather | solution.py:101
  258.4 38.3 %all-gather.21.cloned.1.call-done = bf16[1024,2048]{1,0:T(8,128)(2,1)} async-done(((bf16[128,2048]{1,0:T(8,128)(2,1)}), bf16[1024,2048]{1,0:T(8,128)(2,1)}) %all-gather.21.cloned.1.call-update) | async-done | bytes 4194320 | tf_op jit(solution)/shard_map/all_gather | solution.py:126
  312.8 32.0 %all-gather.15.cloned.1.call-done = bf16[1024,2048]{1,0:T(8,128)(2,1)} async-done(((bf16[128,2048]{1,0:T(8,128)(2,1)}), bf16[1024,2048]{1,0:T(8,128)(2,1)}) %all-gather.15.cloned.1.call-update) | async-done | bytes 4194320 | tf_op jit(solution)/shard_map/all_gather | solution.py:127
  352.1 71.5 %all-gather.23.cloned.1.call-done = bf16[2048,2048]{1,0:T(8,128)(2,1)} async-done(((bf16[64,2048]{1,0:T(8,128)(2,1)}), bf16[2048,2048]{1,0:T(8,128)(2,1)}) %all-gather.23.cloned.1.call-update) | async-done | bytes 8388624 | tf_op jit(solution)/shard_map/all_gather | solution.py:104
  438.2 98.6 %all_to_all.40 = bf16[16,64,2048]{2,1,0:T(8,128)(2,1)S(1)} all-to-all(bf16[16,64,2048]{2,1,0:T(8,128)(2,1)S(1)} %bitcast.552), channel_id=1, replica_groups=mesh['expert'=4,'context'=4,'dp'=2] {'expert','context'}, dimensions={0} | all-to-all | bytes 8388608 | tf_op jit(solution)/shard_map/all_to_all | solution.py:54
  561.1 129.9 %all-gather.3 = bf16[32,64,16]{1,2,0:T(8,128)(2,1)S(1)} all-gather(bf16[1,64,16]{1,2,0:T(8,128)(2,1)S(1)} %bitcast.600), channel_id=1, replica_groups=mesh['expert'=4,'context'=4,'dp'=2] {'expert','context','dp'}, dimensions={0}, use_global_device_ids=true | all-gather | bytes 67584 | tf_op jit(solution)/shard_map/all_gather | solution.py:105
  744.9 151.3 %all-to-all-done.4 = bf16[16,64,2048]{2,1,0:T(8,128)(2,1)} async-done(((bf16[16,64,2048]{2,1,0:T(8,128)(2,1)}), bf16[16,64,2048]{2,1,0:T(8,128)(2,1)}, u32[]{:S(2)}, u32[]{:S(2)}) %all-to-all-start.4) | async-done | bytes 4194336 | tf_op jit(solution)/shard_map/all_to_all | solution.py:62
  928.1 75.6 %all-gather.1 = s32[1,1024]{1,0:T(1,128)S(1)} all-gather(s32[1,128]{1,0:T(1,128)S(1)} %copy-done.143), channel_id=3, replica_groups=mesh['expert'=4,'context'=4,'dp'=2] {'context','dp'}, dimensions={1}, use_global_device_ids=true | all-gather | bytes 4608 | tf_op jit(solution)/shard_map/all_gather | solution.py:128
  1068.1 126.1 %all_to_all.41 = bf16[16,64,2048]{2,1,0:T(8,128)(2,1)S(1)} all-to-all(bf16[16,64,2048]{2,1,0:T(8,128)(2,1)S(1)} %bitcast.553), channel_id=1, replica_groups=mesh['expert'=4,'context'=4,'dp'=2] {'expert','context'}, dimensions={0} | all-to-all | bytes 8388608 | tf_op jit(solution)/shard_map/all_to_all | solution.py:54
  1219.1 101.1 %all-to-all-done.3 = bf16[16,64,2048]{2,1,0:T(8,128)(2,1)} async-done(((bf16[16,64,2048]{2,1,0:T(8,128)(2,1)}), bf16[16,64,2048]{2,1,0:T(8,128)(2,1)}, u32[]{:S(2)}, u32[]{:S(2)}) %all-to-all-start.3) | async-done | bytes 4194336 | tf_op jit(solution)/shard_map/all_to_all | solution.py:58
  1359.5 97.3 %all_to_all.42 = bf16[16,64,2048]{2,1,0:T(8,128)(2,1)S(1)} all-to-all(bf16[16,64,2048]{2,1,0:T(8,128)(2,1)S(1)} %bitcast.551), channel_id=1, replica_groups=mesh['expert'=4,'context'=4,'dp'=2] {'expert','context'}, dimensions={0} | all-to-all | bytes 8388608 | tf_op jit(solution)/shard_map/all_to_all | solution.py:62
  1487.6 96.8 %all-to-all-done.7 = bf16[16,64,2048]{2,1,0:T(8,128)(2,1)} async-done(((bf16[16,64,2048]{2,1,0:T(8,128)(2,1)}), bf16[16,64,2048]{2,1,0:T(8,128)(2,1)}, u32[]{:S(2)}, u32[]{:S(2)}) %all-to-all-start.7) | async-done | bytes 4194336 | tf_op jit(solution)/shard_map/all_to_all | solution.py:66
  1821.3 17.3 reduce-scatter.16.cloned.1.call-done
  1840.2 167.2 %reduce-scatter.18.cloned.1.call-done = f32[128,4096]{1,0:T(8,128)} async-done(((f32[1024,4096]{1,0:T(8,128)}), f32[128,4096]{1,0:T(8,128)}) %reduce-scatter.18.cloned.1.call-update) | async-done | bytes 2097168 | tf_op jit(solution)/shard_map/reduce_scatter | solution.py:264
  2075.4 64.4 %reduce-scatter.36.cloned.1.call-done = f32[64,16]{1,0:T(8,128)} async-done(((f32[2048,16]{1,0:T(8,128)}), f32[64,16]{1,0:T(8,128)}) %reduce-scatter.36.cloned.1.call-update) | async-done | bytes 4112
  2141.3 15.3 reduce-scatter.32.cloned.1.call-done
  2196.4 124.0 %reduce-scatter.34.cloned.1.call-done = f32[64,4]{1,0:T(8,128)} async-done(((f32[2048,4]{1,0:T(8,128)}), f32[64,4]{1,0:T(8,128)}) %reduce-scatter.34.cloned.1.call-update) | async-done | bytes 1040
  2321.9 185.7 %reduce-scatter.26.cloned.1.call-done = f32[64,2048]{1,0:T(8,128)} async-done(((f32[2048,2048]{1,0:T(8,128)}), f32[64,2048]{1,0:T(8,128)}) %reduce-scatter.26.cloned.1.call-update) | async-done | bytes 524304 | tf_op jit(solution)/shard_map/reduce_scatter | solution.py:333
  2507.6 187.2 %reduce-scatter.20.cloned.1.call-done = f32[64,2048]{1,0:T(8,128)} async-done(((f32[2048,2048]{1,0:T(8,128)}), f32[64,2048]{1,0:T(8,128)}) %reduce-scatter.20.cloned.1.call-update) | async-done | bytes 524304 | tf_op jit(solution)/shard_map/reduce_scatter | solution.py:324
  2694.8 187.2 %reduce-scatter.24.cloned.1.call-done = f32[64,2048]{1,0:T(8,128)} async-done(((f32[2048,2048]{1,0:T(8,128)}), f32[64,2048]{1,0:T(8,128)}) %reduce-scatter.24.cloned.1.call-update) | async-done | bytes 524304 | tf_op jit(solution)/shard_map/reduce_scatter | solution.py:330
  2882.0 187.3 %reduce-scatter.22.cloned.1.call-done = f32[64,2048]{1,0:T(8,128)} async-done(((f32[2048,2048]{1,0:T(8,128)}), f32[64,2048]{1,0:T(8,128)}) %reduce-scatter.22.cloned.1.call-update) | async-done | bytes 524304 | tf_op jit(solution)/shard_map/reduce_scatter | solution.py:327
  (590 shorter events, 708.7 us)
Async XLA Ops:
  7.2 83.8 %all-gather.19.cloned.1.call-start = ((), (), s32[]{:S(2)}) async-start(), calls=%async_computation.22 | async-start | bytes 8650752 | tf_op jit(solution)/shard_map/all_gather | solution.py:102
  7.9 161.9 %all-gather.13.cloned.1.call-start = ((), (), s32[]{:S(2)}) async-start(), calls=%async_computation.19 | async-start | bytes 8650752 | tf_op jit(solution)/shard_map/all_gather | solution.py:103
  8.7 240.3 %all-gather.17.cloned.1.call-start = ((), (), s32[]{:S(2)}) async-start(), calls=%async_computation.21 | async-start | bytes 8650752 | tf_op jit(solution)/shard_map/all_gather | solution.py:101
  9.4 287.3 %all-gather.21.cloned.1.call-start = ((), (), s32[]{:S(2)}) async-start(), calls=%async_computation.23 | async-start | bytes 4718592 | tf_op jit(solution)/shard_map/all_gather | solution.py:126
  99.5 245.3 %all-gather.15.cloned.1.call-start = ((), (), s32[]{:S(2)}) async-start(), calls=%async_computation.20 | async-start | bytes 4718592 | tf_op jit(solution)/shard_map/all_gather | solution.py:127
  175.3 248.3 %all-gather.23.cloned.1.call-start = ((), (), s32[]{:S(2)}) async-start(), calls=%async_computation.24 | async-start | bytes 8650752 | tf_op jit(solution)/shard_map/all_gather | solution.py:104
  556.5 137.1 %all-to-all-start.1 = ((bf16[16,64,2048]{2,1,0:T(8,128)(2,1)}), bf16[16,64,2048]{2,1,0:T(8,128)(2,1)}, u32[]{:S(2)}, u32[]{:S(2)}) async-start(bf16[16,64,2048]{2,1,0:T(8,128)(2,1)} %fusion.71), calls=%async_computation.1 | async-start | bytes 8388608 | tf_op jit(solution)/shard_map/all_to_all | solution.py:58
  733.9 162.3 %all-to-all-start.4 = ((bf16[16,64,2048]{2,1,0:T(8,128)(2,1)}), bf16[16,64,2048]{2,1,0:T(8,128)(2,1)}, u32[]{:S(2)}, u32[]{:S(2)}) async-start(bf16[16,64,2048]{2,1,0:T(8,128)(2,1)} %bitcast.550), calls=%async_computation.4 | async-start | bytes 8388608 | tf_op jit(solution)/shard_map/all_to_all | solution.py:62
  738.4 266.6 %all-gather.27.cloned.1.call-start = ((), (), s32[]{:S(2)}) async-start(), calls=%async_computation.26 | async-start | bytes 4718592 | tf_op jit(solution)/shard_map/all_gather | solution.py:126
  739.2 282.0 %all-gather.25.cloned.1.call-start = ((), (), s32[]{:S(2)}) async-start(), calls=%async_computation.25 | async-start | bytes 4718592 | tf_op jit(solution)/shard_map/all_gather | solution.py:127
  922.6 110.9 %all-to-all-start.5 = ((bf16[16,64,2048]{2,1,0:T(8,128)(2,1)}), bf16[16,64,2048]{2,1,0:T(8,128)(2,1)}, u32[]{:S(2)}, u32[]{:S(2)}) async-start(bf16[16,64,2048]{2,1,0:T(8,128)(2,1)} %add_convert_fusion.1), calls=%async_computation.5 | async-start | bytes 8388608 | tf_op jit(solution)/shard_map/all_to_all | solution.py:66
  1213.9 106.3 %all-to-all-start.3 = ((bf16[16,64,2048]{2,1,0:T(8,128)(2,1)}), bf16[16,64,2048]{2,1,0:T(8,128)(2,1)}, u32[]{:S(2)}, u32[]{:S(2)}) async-start(bf16[16,64,2048]{2,1,0:T(8,128)(2,1)} %fusion.74), calls=%async_computation.3 | async-start | bytes 8388608 | tf_op jit(solution)/shard_map/all_to_all | solution.py:58
  1478.3 106.1 %all-to-all-start.7 = ((bf16[16,64,2048]{2,1,0:T(8,128)(2,1)}), bf16[16,64,2048]{2,1,0:T(8,128)(2,1)}, u32[]{:S(2)}, u32[]{:S(2)}) async-start(bf16[16,64,2048]{2,1,0:T(8,128)(2,1)} %add_convert_fusion), calls=%async_computation.8 | async-start | bytes 8388608 | tf_op jit(solution)/shard_map/all_to_all | solution.py:66
  1483.0 355.6 %reduce-scatter.16.cloned.1.call-start = ((), (), s32[]{:S(2)}) async-start(), calls=%async_computation.27 | async-start | bytes 18874368 | tf_op jit(solution)/shard_map/reduce_scatter | solution.py:264
  1675.3 332.1 %reduce-scatter.18.cloned.1.call-start = ((), (), s32[]{:S(2)}) async-start(), calls=%async_computation.28 | async-start | bytes 18874368 | tf_op jit(solution)/shard_map/reduce_scatter | solution.py:264
  1738.9 401.0 %reduce-scatter.36.cloned.1.call-start = ((), (), s32[]{:S(2)}) async-start(), calls=%async_computation.37 | async-start | bytes 1081344
  1751.5 405.1 %reduce-scatter.32.cloned.1.call-start = ((), (), s32[]{:S(2)}) async-start(), calls=%async_computation.35 | async-start | bytes 6291456 | tf_op jit(solution)/shard_map/reduce_scatter | solution.py:350
  1763.8 408.5 %reduce-scatter.28.cloned.1.call-start = ((), (), s32[]{:S(2)}) async-start(), calls=%async_computation.33 | async-start | bytes 6291456 | tf_op jit(solution)/shard_map/reduce_scatter | solution.py:344
  1778.1 409.7 %reduce-scatter.30.cloned.1.call-start = ((), (), s32[]{:S(2)}) async-start(), calls=%async_computation.34 | async-start | bytes 6291456 | tf_op jit(solution)/shard_map/reduce_scatter | solution.py:347
  1792.6 527.9 %reduce-scatter.34.cloned.1.call-start = ((), (), s32[]{:S(2)}) async-start(), calls=%async_computation.36 | async-start | bytes 1081344
  2031.9 475.7 %reduce-scatter.26.cloned.1.call-start = ((), (), s32[]{:S(2)}) async-start(), calls=%async_computation.32 | async-start | bytes 17301504 | tf_op jit(solution)/shard_map/reduce_scatter | solution.py:333
  2040.2 654.6 %reduce-scatter.20.cloned.1.call-start = ((), (), s32[]{:S(2)}) async-start(), calls=%async_computation.29 | async-start | bytes 17301504 | tf_op jit(solution)/shard_map/reduce_scatter | solution.py:324
  2049.9 832.2 %reduce-scatter.24.cloned.1.call-start = ((), (), s32[]{:S(2)}) async-start(), calls=%async_computation.31 | async-start | bytes 17301504 | tf_op jit(solution)/shard_map/reduce_scatter | solution.py:330
  2060.9 1008.4 %reduce-scatter.22.cloned.1.call-start = ((), (), s32[]{:S(2)}) async-start(), calls=%async_computation.30 | async-start | bytes 17301504 | tf_op jit(solution)/shard_map/reduce_scatter | solution.py:327
  (165 other events, 5677.4 us)
Sparse Core Ops, SparseCore 0:
  11.0 79.9 all-gather.18
  93.9 75.8 all-gather.12
  172.8 76.0 all-gather.16
  251.0 45.7 all-gather.20
  298.7 46.0 all-gather.14
  347.6 75.9 all-gather.22
  741.5 98.2 all-gather.26
  841.9 60.0 all-gather.24
  1675.4 163.1 reduce-scatter.15
  1840.8 166.5 reduce-scatter.17
  2009.7 130.1 reduce-scatter.35
  2142.1 14.4 reduce-scatter.31
  2158.9 13.3 reduce-scatter.27
  2174.5 13.3 reduce-scatter.29
  2190.0 130.4 reduce-scatter.33
  2323.3 184.2 reduce-scatter.25
  2510.4 184.3 reduce-scatter.19
  2697.6 184.3 reduce-scatter.23
  2885.0 184.3 reduce-scatter.21
where the time goes:
time: 3090 us; the launch traced here: 3080 us
  waiting for transfers between devices  1800 us (58%)
  blocking collectives  581 us (19%)
  matrix products  317 us (10%)
  local copies, waits for them, and re-layouts  193 us (6%)
  other arithmetic  143 us (5%)
    all_to_all x2, blocking collectives, send_inputs(): lax.all_to_all(buffer, ('expert', 'context'), split_axis=0, concat_axis=0...  225 us
    unnamed x21, waiting for transfers between devices  192 us
    reduce_scatter x1, waiting for transfers between devices, body(): lax.psum_scatter(all_grads[1], ('expert', 'context', 'dp'), scatter_dimen...  187 us
    reduce_scatter x1, waiting for transfers between devices, body(): lax.psum_scatter(all_grads[2], ('expert', 'context', 'dp'), scatter_dimen...  187 us
    reduce_scatter x1, waiting for transfers between devices, body(): lax.psum_scatter(all_grads[0], ('expert', 'context', 'dp'), scatter_dimen...  187 us
    reduce_scatter x1, waiting for transfers between devices, body(): lax.psum_scatter(all_grads[3], ('expert', 'context', 'dp'), scatter_dimen...  186 us
    reduce_scatter x2, waiting for transfers between devices, body(): lax.psum_scatter(jnp.concatenate([key_part.reshape(row_count, model_width...  185 us
    all_to_all x1, waiting for transfers between devices, send_grads(): lax.all_to_all(buffer, ('expert', 'context'), split_axis=0, concat_axis=0...  151 us
  transfers between devices with their start and end apart: 24, of which 20 were waited for; matrix products, arithmetic and copies ran while one was open for 12% of the time, Pallas kernels for 0%

commit v1 on v0

v1 whole, which is shorter than its diff:
```python
import functools

import jax
import jax.numpy as jnp
from jax import lax
from jax.experimental import pallas as pl
from jax.experimental.pallas import tpu as pltpu
from jax.sharding import PartitionSpec as P

HEAD = 128
EPSILON = 1e-05
MASKED = -1e30
UNUSED_SLOT = 4096.0
ALL_AXES = ("expert", "context", "dp")
MESH = pl.DeviceIdType.MESH
ANY = pl.BlockSpec(memory_space=pl.ANY)
VMEM = pl.BlockSpec(memory_space=pltpu.VMEM)
DMA = pltpu.SemaphoreType.DMA
MIB = 1 << 20
f32 = jnp.float32
bf16 = jnp.bfloat16


def call(kernel, operands, out_shapes, in_specs, out_specs, scratch, collective, name, vmem=32):
    return pl.pallas_call(
        kernel,
        out_shape=out_shapes,
        in_specs=in_specs,
        out_specs=out_specs,
        scratch_shapes=scratch,
        compiler_params=pltpu.CompilerParams(
            collective_id=collective, has_side_effects=True, vmem_limit_bytes=vmem * MIB
        ),
        name=name,
    )(*operands)


def position():
    return lax.axis_index("expert"), lax.axis_index("context"), lax.axis_index("dp")


def meet(devices):
    barrier = pltpu.get_barrier_semaphore()
    for device in devices:
        pl.semaphore_signal(barrier, inc=1, device_id=device, device_id_type=MESH)
    pl.semaphore_wait(barrier, len(devices))


def remote(source, target, send_sem, recv_sem, device):
    return pltpu.make_async_remote_copy(
        src_ref=source,
        dst_ref=target,
        send_sem=send_sem,
        recv_sem=recv_sem,
        device_id=device,
        device_id_type=MESH,
    )


def column_peers(E, C, G):
    e, c, d = position()
    me = c * G + d
    peers = []
    for offset in range(1, C * G):
        index = lax.rem(me + offset, C * G)
        peers.append((offset, index, (e, index // G, lax.rem(index, G))))
    return me, peers


def plane_peers(E):
    e, c, d = position()
    return [(i, lax.rem(e + i, E), (lax.rem(e + i, E), c, d)) for i in range(1, E)]


def level_peers(C):
    e, c, d = position()
    return [(i, lax.rem(c + i, C), (e, lax.rem(c + i, C), d)) for i in range(1, C)]


def start_kernel(E, C, G, tokens, weights, column, gathered, ws, wr, bs, br, hs, hr, ts, tr, ls):
    e, c, d = position()
    me, peers = column_peers(E, C, G)
    planes = plane_peers(E)
    batches = tokens.shape[0]
    rows = weights.shape[1]
    per_plane = C * G * rows
    meet([device for _, _, device in peers] + [device for _, _, device in planes])
    mine = gathered.at[pl.ds(pl.multiple_of(e * per_plane + me * rows, rows), rows)]
    weight_copies = []
    for offset, index, device in peers:
        copy = remote(weights.at[index], mine, ws.at[offset], wr.at[offset], device)
        copy.start()
        weight_copies.append(copy)
    local = [pltpu.make_async_copy(weights.at[me], mine, ls.at[batches])]
    for b in range(batches):
        local.append(pltpu.make_async_copy(tokens.at[b], column.at[b, me], ls.at[b]))
    for copy in local:
        copy.start()

    sibling = (e, c, 1 - d)

    def to_sibling(source, b, index, level):
        return remote(source, column.at[b, index], ts.at[b, level], tr.at[b, level], sibling)

    def step(hop, source, b, index, up):
        to = (e, c + 1, d) if up else (e, c - 1, d)
        way = 0 if up else 1
        return remote(source, column.at[b, index], hs.at[way, b, hop], hr.at[way, b, hop], to)

    for b in range(batches):

        @pl.when(c < C - 1)
        def _():
            step(0, tokens.at[b], b, me, True).start()

        @pl.when(c > 0)
        def _():
            step(0, tokens.at[b], b, me, False).start()

        if G > 1:
            to_sibling(tokens.at[b], b, me, 0).start()
    for copy in weight_copies:
        copy.wait_recv()
    local[0].wait()
    block = gathered.at[pl.ds(pl.multiple_of(e * per_plane, per_plane), per_plane)]
    block_copies = []
    for i, _, device in planes:
        copy = remote(block, block, bs.at[i], br.at[i], device)
        copy.start()
        block_copies.append(copy)
    for hop in range(1, C):
        for b in range(batches):
            for up in (True, False):
                origin = c - hop if up else c + hop
                index = origin * G + d
                level = hop if up else C - 1 + hop
                here = (c >= hop) if up else (c + hop < C)
                onward = (c < C - 1) if up else (c > 0)

                @pl.when(here)
                def _():
                    landed = column.at[b, index]
                    step(hop - 1, landed, b, index, up).wait_recv()
                    if hop < C - 1:

                        @pl.when(onward)
                        def _():
                            step(hop, landed, b, index, up).start()

                    if G > 1:
                        to_sibling(landed, b, index, level).start()

    for b in range(batches):
        if G > 1:
            to_sibling(tokens.at[b], b, me, 0).wait()
        for hop in range(C - 1):
            for up in (True, False):
                level = hop + 1 if up else C + hop
                origin = c - hop if up else c + hop
                sends = jnp.logical_and(origin >= 0, c < C - 1) if up else jnp.logical_and(origin < C, c > 0)
                arrives = (c >= hop + 1) if up else (c + hop + 1 < C)

                @pl.when(sends)
                def _():
                    step(hop, tokens.at[b], b, me, up).wait_send()

                if G > 1:

                    @pl.when(arrives)
                    def _():
                        to_sibling(tokens.at[b], b, me, level).wait()

    for copy in weight_copies:
        copy.wait_send()
    for copy in block_copies:
        copy.wait()
    for copy in local[1:]:
        copy.wait()


def start(E, C, G, tokens, weights):
    batches, run, width = tokens.shape
    rows, columns = weights.shape[1:]
    return call(
        functools.partial(start_kernel, E, C, G),
        (tokens, weights),
        (
            jax.ShapeDtypeStruct((batches, C * G, run, width), tokens.dtype),
            jax.ShapeDtypeStruct((E * C * G * rows, columns), weights.dtype),
        ),
        [ANY, ANY],
        (ANY, ANY),
        [
            DMA((C * G,)),
            DMA((C * G,)),
            DMA((E,)),
            DMA((E,)),
            DMA((2, batches, C)),
            DMA((2, batches, C)),
            DMA((batches, 2 * C)),
            DMA((batches, 2 * C)),
            DMA((batches + 1,)),
        ],
        1,
        "start",
    )


def share_kernel(E, C, G, part, parts, ss, rs):
    me, peers = column_peers(E, C, G)
    meet([device for _, _, device in peers])
    copies = []
    for offset, _, device in peers:
        copy = remote(part, parts.at[me], ss.at[offset], rs.at[offset], device)
        copy.start()
        copies.append(copy)
    parts[me] = part[...]
    for copy in copies:
        copy.wait()


def column_sum(E, C, G, part, collective, name):
    parts = call(
        functools.partial(share_kernel, E, C, G),
        (part,),
        jax.ShapeDtypeStruct((C * G,) + part.shape, part.dtype),
        [VMEM],
        VMEM,
        [DMA((C * G,)), DMA((C * G,))],
        collective,
        name,
    )
    return jnp.sum(parts, axis=0)


def to_tokens_kernel(E, C, G, heads, rows, ss, rs, ls):
    me, peers = column_peers(E, C, G)
    batches = rows.shape[0]
    size = heads.shape[3]
    meet([device for _, _, device in peers])
    mine = pl.ds(pl.multiple_of(me * size, size), size)
    copies = []
    for b in range(batches):
        for offset, index, device in peers:
            copies.append(
                remote(
                    heads.at[b, index], rows.at[b, :, mine], ss.at[b, offset], rs.at[b, offset], device
                )
            )
        copies.append(pltpu.make_async_copy(heads.at[b, me], rows.at[b, :, mine], ls.at[b]))
    for copy in copies:
        copy.start()
    for copy in copies:
        copy.wait()


def to_tokens(E, C, G, heads, collective, name):
    batches, count, run, size = heads.shape
    return call(
        functools.partial(to_tokens_kernel, E, C, G),
        (heads,),
        jax.ShapeDtypeStruct((batches, run, count * size), heads.dtype),
        [ANY],
        ANY,
        [DMA((batches, C * G)), DMA((batches, C * G)), DMA((batches,))],
        collective,
        name,
    )


def to_heads_kernel(E, C, G, rows, heads, ss, rs, ls):
    me, peers = column_peers(E, C, G)
    batches = rows.shape[0]
    size = heads.shape[3]
    meet([device for _, _, device in peers])

    def part(b, index):
        return rows.at[b, :, pl.ds(pl.multiple_of(index * size, size), size)]

    copies = []
    for b in range(batches):
        for offset, index, device in peers:
            copies.append(
                remote(part(b, index), heads.at[b, me], ss.at[b, offset], rs.at[b, offset], device)
            )
        copies.append(pltpu.make_async_copy(part(b, me), heads.at[b, me], ls.at[b]))
    for copy in copies:
        copy.start()
    for copy in copies:
        copy.wait()


def to_heads(E, C, G, rows, collective, name):
    batches, run, width = rows.shape
    count = C * G
    return call(
        functools.partial(to_heads_kernel, E, C, G),
        (rows,),
        jax.ShapeDtypeStruct((batches, count, run, width // count), rows.dtype),
        [ANY],
        ANY,
        [DMA((batches, C * G)), DMA((batches, C * G)), DMA((batches,))],
        collective,
        name,
    )


def choose(slots, count):
    cells = lax.broadcasted_iota(jnp.int32, (count, slots.shape[1]), 0).astype(f32)
    return jnp.concatenate(
        [(cells == slots[i : i + 1, :]).astype(bf16) for i in range(slots.shape[0])], axis=0
    )


def dispatch_kernel(
    E, C, A, first, second, slots, gates, out_first, out_second, slots_out, gates_out, landed, packed, ss, sr, gs, gr, zs, zr, xs, xr, ls
):
    e, c, d = position()
    batches, run, width = first.shape
    cap = out_first.shape[3]
    levels, planes = level_peers(C), plane_peers(E)
    everyone = [
        (i, j, lax.rem(e + i, E), lax.rem(c + j, C)) for i in range(E) for j in range(C) if i + j > 0
    ]
    meet([(x, y, d) for _, _, x, y in everyone])
    small = []
    for i, level, device in levels:
        small.append(remote(slots.at[level], slots_out.at[c], ss.at[i], sr.at[i], device))
    for i, j, x, y in everyone:
        small.append(
            remote(gates.at[x, y], gates_out.at[e, c], gs.at[i, j], gr.at[i, j], (x, y, d))
        )
    for copy in small:
        copy.start()
    rows = (first, second)[:A]
    outs = (out_first, out_second)[:A]

    def down(a, b, i, device):
        return remote(rows[a].at[b], landed.at[a, i, b], zs.at[a, i, b], zr.at[a, i, b], device)

    for a in range(A):
        for b in range(batches):
            for i, _, device in levels:
                down(a, b, i, device).start()
    slots_out[c] = slots[c]
    gates_out[e, c] = gates[e, c]

    def across(a, b, i, k, plane, level, device):
        return remote(
            packed.at[a, i, b, plane],
            outs[a].at[e, level, b],
            xs.at[a, i, b, k],
            xr.at[a, i, b, k],
            device,
        )

    def stay(a, b, i, level):
        return pltpu.make_async_copy(packed.at[a, i, b, e], outs[a].at[e, level, b], ls.at[a, i, b])

    def compact(a, b, i, source):
        level = lax.rem(c + C - i, C)
        picks = choose(slots_out[level, b], cap)
        for piece in range(0, width, 512):
            part = jnp.dot(
                picks, source[:, piece : piece + 512], preferred_element_type=f32
            ).astype(bf16)
            packed[a, i, b, :, :, piece : piece + 512] = part.reshape(E, cap, 512)
        for k, plane, device in planes:
            across(a, b, i, k, plane, level, device).start()
        stay(a, b, i, level).start()

    for a in range(A):

        def own(b, carry, a=a):
            compact(a, b, 0, rows[a].at[b])
            return carry

        lax.fori_loop(0, batches, own, 0)
    for copy in small:
        copy.wait_recv()
    for a in range(A):

        def arrived(n, carry, a=a):
            b, i = n // (C - 1), lax.rem(n, C - 1) + 1
            down(a, b, i, (e, c, d)).wait_recv()
            compact(a, b, i, landed.at[a, i, b])
            return carry

        lax.fori_loop(0, batches * (C - 1), arrived, 0)
    for copy in small:
        copy.wait_send()
    for a in range(A):

        def finish(n, carry, a=a):
            b, i = n // C, lax.rem(n, C)
            level = lax.rem(c + C - i, C)
            for k, plane, device in planes:
                across(a, b, i, k, plane, level, device).wait()
            stay(a, b, i, level).wait()

            @pl.when(i > 0)
            def _():
                down(a, b, i, (e, c, d)).wait_send()

            return carry

        lax.fori_loop(0, batches * C, finish, 0)


def dispatch(E, C, first, second, slots, gates, cap, collective, name):
    batches, run, width = first.shape
    A = 2
    rows = jax.ShapeDtypeStruct((E, C, batches, cap, width), bf16)
    return call(
        functools.partial(dispatch_kernel, E, C, A),
        (first, second, slots, gates),
        (
            rows,
            rows,
            jax.ShapeDtypeStruct(slots.shape, f32),
            jax.ShapeDtypeStruct(gates.shape, f32),
        ),
        [VMEM] * 4,
        (ANY, ANY, VMEM, VMEM),
        [
            pltpu.VMEM((A, C, batches, run, width), bf16),
            pltpu.VMEM((A, C, batches, E, cap, width), bf16),
            DMA((C,)),
            DMA((C,)),
            DMA((E, C)),
            DMA((E, C)),
            DMA((A, C, batches)),
            DMA((A, C, batches)),
            DMA((A, C, batches, E)),
            DMA((A, C, batches, E)),
            DMA((A, C, batches)),
        ],
        collective,
        name,
        vmem=56,
    )


def combine_kernel(
    E, C, A, first, second, slots, scalars, out_first, out_second, scalars_out, packed, sums, gs, gr, xs, xr, ls, zs, zr, os
):
    e, c, d = position()
    cap, width = first.shape[3:]
    batches, run = out_first.shape[1:3]
    levels, planes = level_peers(C), plane_peers(E)
    everyone = [
        (i, j, lax.rem(e + i, E), lax.rem(c + j, C)) for i in range(E) for j in range(C) if i + j > 0
    ]
    meet([(x, y, d) for _, _, x, y in everyone])
    small = []
    for i, j, x, y in everyone:
        small.append(
            remote(scalars.at[x, y], scalars_out.at[e, c], gs.at[i, j], gr.at[i, j], (x, y, d))
        )
    for copy in small:
        copy.start()
    scalars_out[e, c] = scalars[e, c]
    rows = (first, second)[:A]
    outs = (out_first, out_second)[:A]

    def across(a, b, i, k, plane, device):
        level = lax.rem(c + i, C)
        return remote(
            rows[a].at[plane, level, b],
            packed.at[a, i, b, e],
            xs.at[a, i, b, k],
            xr.at[a, i, b, k],
            device,
        )

    def stay(a, b, i):
        level = lax.rem(c + i, C)
        return pltpu.make_async_copy(
            rows[a].at[e, level, b], packed.at[a, i, b, e], ls.at[a, i, b]
        )

    def up(a, b, i):
        level = lax.rem(c + i, C)
        return remote(
            sums.at[a, i, b], outs[a].at[c, b], zs.at[a, i, b], zr.at[a, i, b], (e, level, d)
        )

    def keep(a, b):
        return pltpu.make_async_copy(sums.at[a, 0, b], outs[a].at[c, b], os.at[a, b])

    def turn(n):
        return lax.rem(n, batches), lax.rem(n // batches + 1, C)

    for a in range(A):

        def send(n, carry, a=a):
            b, i = turn(n)
            for k, plane, device in planes:
                across(a, b, i, k, plane, device).start()
            stay(a, b, i).start()
            return carry

        lax.fori_loop(0, batches * C, send, 0)
    for a in range(A):

        def add(n, carry, a=a):
            b, i = turn(n)
            for k, plane, device in planes:
                across(a, b, i, k, plane, device).wait_recv()
            stay(a, b, i).wait()
            picks = choose(slots[lax.rem(c + i, C), b], cap)
            for piece in range(0, width, 512):
                part = packed[a, i, b, :, :, piece : piece + 512].reshape(E * cap, 512)
                sums[a, i, b, :, piece : piece + 512] = lax.dot_general(
                    picks, part, (((0,), (0,)), ((), ())), preferred_element_type=f32
                ).astype(bf16)

            @pl.when(i > 0)
            def _():
                up(a, b, i).start()

            @pl.when(i == 0)
            def _():
                keep(a, b).start()

            return carry

        lax.fori_loop(0, batches * C, add, 0)
    for copy in small:
        copy.wait()
    for a in range(A):

        def finish(n, carry, a=a):
            b, i = turn(n)
            for k, plane, device in planes:
                across(a, b, i, k, plane, device).wait_send()

            @pl.when(i > 0)
            def _():
                up(a, b, i).wait()

            @pl.when(i == 0)
            def _():
                keep(a, b).wait()

            return carry

        lax.fori_loop(0, batches * C, finish, 0)


def combine(E, C, first, second, slots, scalars, collective, name):
    batches, cap, width = first.shape[2:]
    run = slots.shape[3]
    A = 2
    rows = jax.ShapeDtypeStruct((C, batches, run, width), bf16)
    return call(
        functools.partial(combine_kernel, E, C, A),
        (first, second, slots, scalars),
        (rows, rows, jax.ShapeDtypeStruct(scalars.shape, f32)),
        [ANY, ANY, VMEM, VMEM],
        (ANY, ANY, VMEM),
        [
            pltpu.VMEM((A, C, batches, E, cap, width), bf16),
            pltpu.VMEM((A, C, batches, run, width), bf16),
            DMA((E, C)),
            DMA((E, C)),
            DMA((A, C, batches, E)),
            DMA((A, C, batches, E)),
            DMA((A, C, batches)),
            DMA((A, C, batches)),
            DMA((A, C, batches)),
            DMA((A, batches)),
        ],
        collective,
        name,
        vmem=56,
    )


def scatter_kernel(E, C, G, rows, out, other, sums, cs, cr, zs, zr, ls):
    e, c, d = position()
    batches = rows.shape[0]
    run, width = rows.shape[3:]
    levels = level_peers(C)
    sibling = (e, c, 1 - d)
    meet([device for _, _, device in levels] + ([sibling] if G > 1 else []))

    def swap(b, level):
        return remote(
            rows.at[b, level, 1 - d], other.at[b, level], cs.at[b, level], cr.at[b, level], sibling
        )

    def send(b, i, level):
        return remote(
            sums.at[b, level], out.at[c, b], zs.at[b, i], zr.at[b, i], (e, level, d)
        )

    def keep(b):
        return pltpu.make_async_copy(sums.at[b, c], out.at[c, b], ls.at[b])

    order = [(i, lax.rem(c + i, C)) for i in range(1, C)] + [(0, c)]
    if G > 1:
        for i, level in order:
            for b in range(batches):
                swap(b, level).start()
    for i, level in order:
        for b in range(batches):
            if G > 1:
                swap(b, level).wait_recv()
                sums[b, level] = (
                    rows[b, level, d].astype(f32) + other[b, level].astype(f32)
                ).astype(bf16)
            else:
                sums[b, level] = rows[b, level, d]
            if i > 0:
                send(b, i, level).start()
            else:
                keep(b).start()
    for i, level in order:
        for b in range(batches):
            if G > 1:
                swap(b, level).wait_send()
            if i > 0:
                send(b, i, level).wait()
            else:
                keep(b).wait()


def column_scatter(E, C, G, rows, collective, name):
    batches, _, _, run, width = rows.shape
    return call(
        functools.partial(scatter_kernel, E, C, G),
        (rows,),
        jax.ShapeDtypeStruct((C, batches, run, width), bf16),
        [VMEM],
        ANY,
        [
            pltpu.VMEM((batches, C, run, width), bf16),
            pltpu.VMEM((batches, C, run, width), bf16),
            DMA((batches, C)),
            DMA((batches, C)),
            DMA((batches, C)),
            DMA((batches, C)),
            DMA((batches,)),
        ],
        collective,
        name,
        vmem=48,
    )


def weights_kernel(
    E, C, G, qkv, proj, out_qkv, out_proj, plane_qkv, sum_qkv, other, pair, plane_proj, sum_proj, as_, ar, bs, br, cs, cr, ds, dr, es, er, ls
):
    e, c, d = position()
    me, peers = column_peers(E, C, G)
    planes, levels = plane_peers(E), level_peers(C)
    sibling = (e, c, 1 - d)
    meet([device for _, _, device in peers] + [device for _, _, device in planes])
    swaps = []
    if G > 1:
        for level in range(C):
            swaps.append(
                remote(proj.at[level, 1 - d], other.at[level], cs.at[level], cr.at[level], sibling)
            )
    for copy in swaps:
        copy.start()
    first = []
    for k, plane, device in planes:
        first.append(remote(qkv.at[plane], plane_qkv.at[k], as_.at[k], ar.at[k], device))
    for copy in first:
        copy.start()
    middle = []
    for level in range(C):
        if G > 1:
            swaps[level].wait_recv()
            pair[level] = (proj[level, d].astype(f32) + other[level].astype(f32)).astype(bf16)
        else:
            pair[level] = proj[level, d]
        for k, plane, device in planes:
            copy = remote(
                pair.at[level, plane], plane_proj.at[level, k], ds.at[level, k], dr.at[level, k], device
            )
            copy.start()
            middle.append(copy)
    for copy in first:
        copy.wait_recv()
    total = qkv[e].astype(f32)
    for k in range(1, E):
        total = total + plane_qkv[k].astype(f32)
    sum_qkv[...] = total.astype(bf16)
    second = []
    for offset, index, device in peers:
        copy = remote(sum_qkv.at[index], out_qkv.at[me], bs.at[offset], br.at[offset], device)
        copy.start()
        second.append(copy)
    out_qkv[me] = sum_qkv[me]
    for copy in middle:
        copy.wait_recv()
    for level in range(C):
        total = pair[level, e].astype(f32)
        for k in range(1, E):
            total = total + plane_proj[level, k].astype(f32)
        sum_proj[level] = total.astype(bf16)
    last = []
    for i, level, device in levels:
        copy = remote(sum_proj.at[level], out_proj.at[c], es.at[i], er.at[i], device)
        copy.start()
        last.append(copy)
    out_proj[c] = sum_proj[c]
    for copy in swaps + first + middle:
        copy.wait_send()
    for copy in second + last:
        copy.wait()


def weight_scatter(E, C, G, qkv, proj, collective, name):
    count, rows, columns = qkv.shape[1:]
    width = proj.shape[4]
    return call(
        functools.partial(weights_kernel, E, C, G),
        (qkv, proj),
        (
            jax.ShapeDtypeStruct((count, rows, columns), bf16),
            jax.ShapeDtypeStruct((C, rows, width), bf16),
        ),
        [VMEM, VMEM],
        (VMEM, VMEM),
        [
            pltpu.VMEM((E, count, rows, columns), bf16),
            pltpu.VMEM((count, rows, columns), bf16),
            pltpu.VMEM((C, E, rows, width), bf16),
            pltpu.VMEM((C, E, rows, width), bf16),
            pltpu.VMEM((C, E, rows, width), bf16),
            pltpu.VMEM((C, rows, width), bf16),
            DMA((E,)),
            DMA((E,)),
            DMA((count,)),
            DMA((count,)),
            DMA((C,)),
            DMA((C,)),
            DMA((C, E)),
            DMA((C, E)),
            DMA((C,)),
            DMA((C,)),
            DMA((1,)),
        ],
        collective,
        name,
        vmem=56,
    )


def contract(left, right, axes):
    return lax.dot_general(left, right, ((axes[:1], axes[1:]), ((), ())), preferred_element_type=f32)


def query_blocks(length):
    size = min(256, length)
    return [(i, size, min(length, i + 2 * size)) for i in range(0, length, size)]


def attend_kernel(scale, queries, keys, values, row_ids, key_ids, mixed, log_total):
    length = queries.shape[1]
    for first, size, seen in query_blocks(length):
        rows = pl.ds(first, size)
        scores = contract(queries[0, rows], keys[0, :seen], (1, 1)) * scale
        scores = jnp.where(key_ids[0, :, :seen] <= row_ids[0, rows], scores, MASKED)
        peak = jnp.max(scores, axis=1, keepdims=True)
        grown = jnp.exp(scores - peak)
        total = jnp.sum(grown, axis=1, keepdims=True)
        probs = (grown * (1.0 / total)).astype(bf16)
        mixed[0, rows] = jnp.dot(probs, values[0, :seen], preferred_element_type=f32).astype(bf16)
        log_total[0, 0, rows] = peak + jnp.log(total)


def attend_back_kernel(
    scale, queries, keys, values, grads, row_ids, key_ids, log_total, query_grad, key_grad, value_grad
):
    length = queries.shape[1]
    key_grad[...] = jnp.zeros_like(key_grad)
    value_grad[...] = jnp.zeros_like(value_grad)
    for first, size, seen in query_blocks(length):
        rows = pl.ds(first, size)
        query, grad = queries[0, rows], grads[0, rows]
        scores = contract(query, keys[0, :seen], (1, 1)) * scale
        scores = jnp.where(key_ids[0, :, :seen] <= row_ids[0, rows], scores, MASKED)
        probs = jnp.exp(scores - log_total[0, 0, rows])
        prod = contract(grad, values[0, :seen], (1, 1))
        delta = jnp.sum(probs * prod, axis=1, keepdims=True)
        score_grad = (probs * (prod - delta)).astype(bf16)
        query_grad[0, rows] = jnp.dot(score_grad, keys[0, :seen], preferred_element_type=f32) * scale
        key_grad[0, :seen] += contract(score_grad, query, (0, 0)) * scale
        value_grad[0, :seen] += contract(probs.astype(bf16), grad, (0, 0))


def attention_specs(length):
    head = pl.BlockSpec((1, length, HEAD), lambda b, h: (b, 0, h))
    row_ids = pl.BlockSpec((1, length, 1), lambda b, h: (b, 0, 0))
    key_ids = pl.BlockSpec((1, 1, length), lambda b, h: (b, 0, 0))
    log_total = pl.BlockSpec((1, 1, length, 1), lambda b, h: (b, h, 0, 0))
    return head, row_ids, key_ids, log_total


def attend(queries, keys, values, ids):
    batches, length, size = queries.shape
    heads = size // HEAD
    head, row_ids, key_ids, log_total = attention_specs(length)
    return pl.pallas_call(
        functools.partial(attend_kernel, HEAD**-0.5),
        grid=(batches, heads),
        out_shape=(
            jax.ShapeDtypeStruct(queries.shape, bf16),
            jax.ShapeDtypeStruct((batches, heads, length, 1), f32),
        ),
        in_specs=[head, head, head, row_ids, key_ids],
        out_specs=(head, log_total),
        compiler_params=pltpu.CompilerParams(vmem_limit_bytes=48 * MIB),
        name="attend",
    )(queries, keys, values, ids[:, :, None], ids[:, None, :])


def attend_back(queries, keys, values, grads, ids, totals):
    batches, length, size = queries.shape
    heads = size // HEAD
    head, row_ids, key_ids, log_total = attention_specs(length)
    grad = jax.ShapeDtypeStruct(queries.shape, f32)
    return pl.pallas_call(
        functools.partial(attend_back_kernel, HEAD**-0.5),
        grid=(batches, heads),
        out_shape=(grad, grad, grad),
        in_specs=[head, head, head, head, row_ids, key_ids, log_total],
        out_specs=(head, head, head),
        compiler_params=pltpu.CompilerParams(vmem_limit_bytes=48 * MIB),
        name="attend_back",
    )(queries, keys, values, grads, ids[:, :, None], ids[:, None, :], totals)


def rms_factor(values):
    return lax.rsqrt(jnp.mean(values * values, axis=-1, keepdims=True) + EPSILON)


def norm_back(grad_hat, hatted, factor):
    return factor * (grad_hat - hatted * jnp.mean(grad_hat * hatted, axis=-1, keepdims=True))


def slot_table(routes, experts):
    batches, run, top = routes.shape
    hits = jnp.swapaxes(routes, 1, 2)[:, :, :, None] == jnp.arange(experts, dtype=jnp.int32)
    ones = hits.astype(bf16)
    tokens, ranks = jnp.arange(run), jnp.arange(top)
    before = (tokens[None, :] < tokens[:, None]).astype(bf16)
    above = (ranks[None, :] < ranks[:, None]).astype(bf16)
    within = jnp.einsum("ts,bksx->bktx", before, ones, preferred_element_type=f32)
    totals = jnp.sum(hits.astype(f32), axis=2)
    earlier = jnp.einsum(
        "kj,bjx->bkx", above, totals.astype(bf16), preferred_element_type=f32
    )
    places = jnp.sum(jnp.where(hits, within + earlier[:, :, None, :], 0.0), axis=1)
    places = jnp.where(jnp.any(hits, axis=1), places, UNUSED_SLOT)
    return jnp.swapaxes(places, 1, 2)


def body(
    tokens,
    block_ids,
    routes,
    norm_gains,
    w_query,
    w_key,
    w_value,
    w_output,
    router,
    expert_gate,
    expert_up,
    expert_down,
    cotangent,
):
    E, C, G = lax.axis_size("expert"), lax.axis_size("context"), lax.axis_size("dp")
    batches, run, width = tokens.shape
    top = routes.shape[2]
    experts = E * C * expert_gate.shape[0]
    capacity = max(2, run * top // experts)
    count = C * G
    size = width // count
    length = count * run
    every = batches * length
    own = batches * run
    me = lax.axis_index("context") * G + lax.axis_index("dp")

    rows = w_query.shape[0]
    small_width = -(-(norm_gains.shape[1] + experts) // 128) * 128
    small = jnp.concatenate([norm_gains, router], axis=1)
    small = jnp.pad(small, ((0, 0), (0, small_width - small.shape[1])))
    pieces = [w.reshape(rows, count, size) for w in (w_query, w_key, w_value)]
    pieces.append(jnp.broadcast_to(small[:, None, :], (rows, count, small_width)))
    weights = jnp.swapaxes(jnp.concatenate(pieces, axis=2), 0, 1)
    full_output = lax.all_gather(w_output, ALL_AXES, axis=0, tiled=True)
    ids = lax.all_gather(block_ids, ("context", "dp"), axis=1, tiled=True)
    column, gathered = start(E, C, G, tokens, weights)
    w_qkv = gathered[:, : 3 * size]
    gains = gathered[:, 3 * size : 3 * size + 4].astype(f32)
    full_router = gathered[:, 3 * size + 4 : 3 * size + 4 + experts]
    head_gains = lax.dynamic_slice(gains, (me * size, 0), (size, 4))

    column = column.reshape(every, width).astype(f32)
    normed = (column * rms_factor(column) * gains[:, 0]).astype(bf16)
    qkv = jnp.dot(normed, w_qkv, preferred_element_type=f32)
    query_raw, key_raw = qkv[:, :size], qkv[:, size : 2 * size]
    value_low = qkv[:, 2 * size :].astype(bf16)
    squares = jnp.stack([jnp.sum(query_raw * query_raw, axis=1), jnp.sum(key_raw * key_raw, axis=1)])
    factors = lax.rsqrt(column_sum(E, C, G, squares, 2, "squares") / width + EPSILON)
    query_factor, key_factor = factors[0][:, None], factors[1][:, None]
    query_hat, key_hat = query_raw * query_factor, key_raw * key_factor
    by_sequence = (batches, length, size)
    query_low = (query_hat * head_gains[:, 1]).astype(bf16).reshape(by_sequence)
    key_low = (key_hat * head_gains[:, 2]).astype(bf16).reshape(by_sequence)
    value_low = value_low.reshape(by_sequence)
    mixed_heads, log_total = attend(query_low, key_low, value_low, ids)
    mixed_low = to_tokens(
        E, C, G, mixed_heads.reshape(batches, count, run, size), 3, "mixed_rows"
    ).reshape(own, width)

    inputs = tokens.reshape(own, width).astype(f32)
    resid = inputs + jnp.dot(mixed_low, full_output, preferred_element_type=f32)
    second_factor = rms_factor(resid)
    second_hat = resid * second_factor
    second_low = (second_hat * gains[:, 3]).astype(bf16)
    logits = jnp.dot(second_low, full_router, preferred_element_type=f32)
    router_probs = jax.nn.softmax(logits, axis=-1)
    places = slot_table(routes, experts).reshape(batches, E, C, run)
    by_level = jnp.transpose(places, (2, 0, 1, 3))
    by_expert = jnp.transpose(places, (1, 2, 0, 3))
    gate_table = jnp.transpose(router_probs.reshape(batches, run, E, C), (2, 3, 0, 1))
    table = jnp.concatenate([by_expert, gate_table], axis=2)

    expert_in, expert_up_in, slots, table = dispatch(
        E,
        C,
        second_low.reshape(batches, run, width),
        cotangent,
        by_level,
        table,
        capacity,
        4,
        "dispatch",
    )
    slot_count = E * C * batches * capacity
    x = expert_in.reshape(slot_count, width)
    upstream_rows = expert_up_in.reshape(slot_count, width)
    cells = jnp.arange(capacity, dtype=jnp.int32).astype(f32)
    holds = table[:, :, :batches, None, :] == cells[:, None]
    gate = jnp.sum(jnp.where(holds, table[:, :, batches:, None, :], 0.0), axis=-1)
    gate = gate.reshape(slot_count, 1)
    w_gate, w_up, w_down = expert_gate[0], expert_up[0], expert_down[0]
    gate_pre = jnp.dot(x, w_gate, preferred_element_type=f32)
    up_pre = jnp.dot(x, w_up, preferred_element_type=f32)
    sigmoid_gate = jax.nn.sigmoid(gate_pre)
    silu_gate = gate_pre * sigmoid_gate
    act = (silu_gate * up_pre).astype(bf16)
    expert_out = jnp.dot(act, w_down, preferred_element_type=f32).astype(bf16).astype(f32)
    upstream_wide = upstream_rows.astype(f32)
    gate_grad = jnp.sum(expert_out * upstream_wide, axis=1)
    out_rows = (gate * expert_out).astype(bf16)
    pair_grad = (gate * upstream_wide).astype(bf16)
    act_grad = contract(pair_grad, w_down, (1, 1))
    gate_pre_grad = (
        act_grad * up_pre * sigmoid_gate * (1.0 + gate_pre * (1.0 - sigmoid_gate))
    ).astype(bf16)
    up_pre_grad = (act_grad * silu_gate).astype(bf16)
    input_back = contract(gate_pre_grad, w_gate, (1, 1)) + contract(up_pre_grad, w_up, (1, 1))
    gate_grad = gate_grad.reshape(E, C, batches, capacity, 1)
    gate_grad = jnp.sum(jnp.where(holds, gate_grad, 0.0), axis=3)
    by_slot = (E, C, batches, capacity, width)
    mixture, second_grad, gate_grad = combine(
        E,
        C,
        out_rows.reshape(by_slot),
        input_back.astype(bf16).reshape(by_slot),
        slots,
        gate_grad,
        5,
        "combine",
    )
    share = functools.partial(lax.psum_scatter, axis_name="dp", tiled=True)
    grad_gate = share(contract(x, gate_pre_grad, (0, 0)).astype(bf16), scatter_dimension=1)
    grad_up = share(contract(x, up_pre_grad, (0, 0)).astype(bf16), scatter_dimension=1)
    grad_down = share(contract(act, pair_grad, (0, 0)).astype(bf16), scatter_dimension=0)

    upstream = cotangent.reshape(own, width).astype(f32)
    mixture = jnp.sum(mixture.astype(f32), axis=0).reshape(own, width)
    activations = (resid + mixture).astype(bf16).reshape(tokens.shape)
    prob_grad = jnp.transpose(gate_grad, (2, 3, 0, 1)).reshape(own, experts)
    logit_grad = router_probs * (
        prob_grad - jnp.sum(router_probs * prob_grad, axis=-1, keepdims=True)
    )
    logit_grad = logit_grad.astype(bf16)
    second_grad = jnp.sum(second_grad.astype(f32), axis=0).reshape(own, width)
    second_grad = second_grad + contract(logit_grad, full_router, (1, 1))
    gain_second = jnp.sum(second_grad * second_hat, axis=0)
    resid_grad = upstream + norm_back(second_grad * gains[:, 3], second_hat, second_factor)
    attn_grad = resid_grad.astype(bf16)
    mixed_grad = contract(attn_grad, full_output, (1, 1)).astype(bf16)

    mixed_grad = to_heads(E, C, G, mixed_grad.reshape(batches, run, width), 6, "mixed_grad_heads")
    query_grad, key_grad, value_grad = (
        grad.reshape(every, size)
        for grad in attend_back(
            query_low, key_low, value_low, mixed_grad.reshape(by_sequence), ids, log_total
        )
    )
    query_back, key_back = query_grad * head_gains[:, 1], key_grad * head_gains[:, 2]
    means = jnp.stack([jnp.sum(query_back * query_hat, axis=1), jnp.sum(key_back * key_hat, axis=1)])
    means = column_sum(E, C, G, means, 7, "norm_means") / width
    raw_grads = jnp.concatenate(
        [
            (query_factor * (query_back - query_hat * means[0][:, None])).astype(bf16),
            (key_factor * (key_back - key_hat * means[1][:, None])).astype(bf16),
            value_grad.astype(bf16),
        ],
        axis=1,
    )
    first_part = contract(raw_grads, w_qkv, (1, 1)).astype(bf16)
    first_grad = column_scatter(
        E, C, G, first_part.reshape(batches, C, G, run, width), 8, "first_grad"
    )
    first_grad = jnp.sum(first_grad.astype(f32), axis=0).reshape(own, width)
    first_factor = rms_factor(inputs)
    first_hat = inputs * first_factor
    gain_first = jnp.sum(first_grad * first_hat, axis=0)
    input_grad = resid_grad + norm_back(first_grad * gains[:, 0], first_hat, first_factor)

    grad_qkv = contract(normed, raw_grads, (0, 0)).astype(bf16)
    grad_proj = contract(mixed_low, attn_grad, (0, 0)).astype(bf16)
    grad_proj = jnp.transpose(grad_proj.reshape(E, C, G, rows, width), (1, 2, 0, 3, 4))
    grad_qkv, grad_proj = weight_scatter(
        E, C, G, grad_qkv.reshape(E, count, rows, 3 * size), grad_proj, 9, "weight_grads"
    )
    grad_qkv = jnp.swapaxes(grad_qkv.astype(f32), 0, 1)
    grad_query, grad_key, grad_value = (
        grad_qkv[:, :, i * size : (i + 1) * size].reshape(rows, width) for i in range(3)
    )
    grad_proj = jnp.sum(grad_proj.astype(f32), axis=0)
    gain_heads = jnp.stack(
        [jnp.sum(query_grad * query_hat, axis=0), jnp.sum(key_grad * key_hat, axis=0)], axis=1
    )
    gain_heads = lax.dynamic_update_slice(
        jnp.zeros((width, 2), f32), gain_heads, (me * size, 0)
    )
    sums = jnp.concatenate(
        [
            gain_first[:, None],
            gain_heads,
            gain_second[:, None],
            contract(second_low, logit_grad, (0, 0)),
        ],
        axis=1,
    )
    sums = lax.psum_scatter(sums, ALL_AXES, scatter_dimension=0, tiled=True)
    return (
        activations,
        input_grad.reshape(tokens.shape),
        sums[:, :4],
        grad_query,
        grad_key,
        grad_value,
        grad_proj,
        sums[:, 4:],
        grad_gate.astype(f32)[None],
        grad_up.astype(f32)[None],
        grad_down.astype(f32)[None],
    )


def solution(mesh):
    by_token = ("context", "dp")
    by_expert = P(("expert", "context"), None, None)
    by_row = P(ALL_AXES, None)
    rows = P("expert", by_token, None)
    return jax.shard_map(
        body,
        mesh=mesh,
        in_specs=(
            rows,
            P("expert", by_token),
            rows,
            by_row,
            by_row,
            by_row,
            by_row,
            by_row,
            by_row,
            by_expert,
            by_expert,
            by_expert,
            rows,
        ),
        out_specs=(
            rows,
            rows,
            by_row,
            by_row,
            by_row,
            by_row,
            by_row,
            by_row,
            P(("expert", "context"), None, "dp"),
            P(("expert", "context"), None, "dp"),
            P(("expert", "context"), "dp", None),
        ),
        check_vma=False,
    )
```

time: 3090 us -> 1190 us (0.39)
  waiting for transfers between devices: 1800 us -> 0.75 us
  Pallas kernels: 0 us -> 861 us
  blocking collectives: 581 us -> 11.4 us
  local copies, waits for them, and re-layouts: 193 us -> 30.7 us
  matrix products: 317 us -> 188 us
  other arithmetic: 143 us -> 75.5 us
    reduce_scatter x9 -> x3, waiting for transfers between devices: 965 us -> 0.01 us  [the longest x1 0.01 us: body(): share(contract(act, pair_grad, (0, 0)).astype(bf16), scatter_dimension=0)]
    pallas_call x0 -> x11, Pallas kernels: none -> 861 us  [the longest x9 830 us: call(): pl.pallas_call(kernel, out_shape=out_shapes, in_specs=in_specs, out_specs...]
    all_to_all x5 -> x0, waiting for transfers between devices: 349 us -> none  [the longest x1 151 us: send_grads(): lax.all_to_all(buffer, ('expert', 'context'), split_axis=0, concat_axis=0...]
    all_to_all x3 -> x0, blocking collectives: 322 us -> none  [the longest x2 225 us: send_inputs(): lax.all_to_all(buffer, ('expert', 'context'), split_axis=0, concat_axis=0...]
    all_gather x8 -> x1, waiting for transfers between devices: 295 us -> 0.01 us  [body(): full_output = lax.all_gather(w_output, ALL_AXES, axis=0, tiled=True)]
    all_gather x4 -> x1, blocking collectives: 259 us -> 11.4 us  [body(): ids = lax.all_gather(block_ids, ('context', 'dp'), axis=1, tiled=True)]
    unnamed x21 -> x6, waiting for transfers between devices: 192 us -> 0.75 us
    dot_general x54 -> x20, matrix products: 316 us -> 188 us  [the longest x12 127 us: contract(): lax.dot_general(left, right, ((axes[:1], axes[1:]), ((), ())), preferred_...]
  transfers between devices with their start and end apart: 24 -> 5, of which waited for: 20 -> 0; matrix products, arithmetic and copies ran while one was open for 12% -> 10% of each run, Pallas kernels for 0% -> 26%
where the time goes in v1:
time: 1190 us; the launch traced here: 1180 us
  Pallas kernels  861 us (72%)
  matrix products  188 us (16%)
  other arithmetic  75.5 us (6%)
  local copies, waits for them, and re-layouts  30.7 us (3%)
  between operations  15.1 us (1%)
    pallas_call x9, Pallas kernels, call(): pl.pallas_call(kernel, out_shape=out_shapes, in_specs=in_specs, out_specs...  830 us
    dot_general x12, matrix products, contract(): lax.dot_general(left, right, ((axes[:1], axes[1:]), ((), ())), preferred_...  127 us
  transfers between devices with their start and end apart: 5, of which 0 were waited for; matrix products, arithmetic and copies ran while one was open for 10% of the time, Pallas kernels for 26%

profile of v1, /device:TPU:1, one launch (start us, length us, event | category | flops | bytes accessed | tf_op | source)
XLA Modules:
  0.0 1182.4 jit_solution(14951283638354879786)
XLA Ops:
  11.0 130.6 %start.1 = (bf16[2,8,128,2048]{3,2,1,0:T(8,128)(2,1)S(1)}, bf16[2048,896]{1,0:T(8,128)(2,1)S(1)}) custom-call(bf16[2,128,2048]{2,1,0:T(8,128)(2,1)S(1)} %copy-done.1, bf16[8,64,896]{2,1,0:T(8,128)(2,1)S(1)} %maximum_bitcast_fusion.weights), custom_call_target="tpu_custom_call" | custom-call | tf_op jit(solution)/shard_map/start/pallas_call | solution.py:25
  145.2 9.3 fusion.5
  154.5 9.1 fusion.18
  172.1 11.4 all_gather.6
  188.0 11.7 attend.1
  200.8 23.9 %mixed_rows.1 = bf16[2,128,2048]{2,1,0:T(8,128)(2,1)S(1)} custom-call(bf16[2,8,128,256]{3,2,1,0:T(8,128)(2,1)S(1)} %bitcast.221), custom_call_target="tpu_custom_call" | custom-call | tf_op jit(solution)/shard_map/mixed_rows/pallas_call | solution.py:25
  238.3 215.7 %dispatch.1 = (bf16[4,4,2,64,2048]{4,3,2,1,0:T(8,128)(2,1)}, bf16[4,4,2,64,2048]{4,3,2,1,0:T(8,128)(2,1)}, f32[4,2,4,128]{3,2,1,0:T(4,128)}, f32[4,4,4,128]{3,2,1,0:T(4,128)}) custom-call(bf16[2,128,2048]{2,1,0:T(8,128)(2,1)} %bitcast.230, bf16[2,128,2048]{2,1,0:T(8,128)(2,1)} %second.1, f32[4,2,4,128]{3,2,1,0:T(4,128)} %copy.57.slots, ...), custom_call_target="tpu_custom_call" | custom-call | tf_op jit(solution)/shard_map/dispatch/pallas_call | solution.py:25
  454.0 14.6 %fusion.15 = f32[2048,1024]{1,0:T(8,128)} fusion(bf16[2048,2048]{1,0:T(8,128)(2,1)} %bitcast.275, bf16[1,2048,1024]{2,1,0:T(8,128)(2,1)} %param.22), kind=kOutput, calls=%fused_computation.33 | convolution fusion | flops 8589934592 | bytes 20971520 | tf_op jit(solution)/shard_map/dot_general | solution.py:956
  468.6 15.2 %multiply_convert_fusion.2 = (bf16[2048,1024]{1,0:T(8,128)(2,1)}, f32[2048,1024]{1,0:T(8,128)}) fusion(f32[2048,1024]{1,0:T(8,128)} %fusion.15, bf16[2048,2048]{1,0:T(8,128)(2,1)S(1)} %bitcast.278, bf16[1,2048,1024]{2,1,0:T(8,128)(2,1)} %param.23), kind=kOutput, calls=%fused_computation.19 | convolution fusion | flops 8602517504 | bytes 33554432 | tf_op jit(solution)/shard_map/dot_general | solution.py:957
  483.8 14.0 %fusion.1 = (f32[2048]{0:T(1024)S(1)}, bf16[2048,2048]{1,0:T(8,128)(2,1)}) fusion(bf16[4,4,2,64,2048]{4,3,2,1,0:T(8,128)(2,1)S(1)} %bitcast.227, bf16[2048,1024]{1,0:T(8,128)(2,1)} %get-tuple-element.86, bf16[1,1024,2048]{2,1,0:T(8,128)(2,1)} %param.24), kind=kOutput, calls=%fused_computation.3 | convolution fusion | flops 8610904064 | bytes 25174016 | tf_op jit(solution)/shard_map/dot_general | solution.py:961
  507.1 22.2 %multiply_convert_fusion = (bf16[2048,1024]{1,0:T(8,128)(2,1)}, bf16[2048,1024]{1,0:T(8,128)(2,1)}) fusion(f32[2048,1024]{1,0:T(8,128)} %fusion.15, f32[2048,1024]{1,0:T(8,128)} %get-tuple-element.87, bf16[2048,2048]{1,0:T(8,128)(2,1)} %bitcast.232, bf16[1,1024,2048]{2,1,0:T(8,128)(2,1)} %param.24), kind=kOutput, calls=%fused_computation.17 | convolution fusion | flops 8617197568 | bytes 37748736 | tf_op jit(solution)/shard_map/dot_general | solution.py:755
  529.3 13.9 %fusion.13 = f32[2048,2048]{1,0:T(8,128)} fusion(bf16[2048,1024]{1,0:T(8,128)(2,1)} %get-tuple-element.62, bf16[1,2048,1024]{2,1,0:T(8,128)(2,1)S(1)} %copy-done.46), kind=kOutput, calls=%fused_computation.31 | convolution fusion | flops 8589934592 | bytes 25165824 | tf_op jit(solution)/shard_map/dot_general | solution.py:755
  543.2 16.6 %add_convert_fusion = bf16[2048,2048]{1,0:T(8,128)(2,1)} fusion(f32[2048,2048]{1,0:T(8,128)} %fusion.13, bf16[2048,1024]{1,0:T(8,128)(2,1)} %get-tuple-element.61, bf16[1,2048,1024]{2,1,0:T(8,128)(2,1)} %param.23), kind=kOutput, calls=%fused_computation.11 | convolution fusion | flops 8598323200 | bytes 33554432 | tf_op jit(solution)/shard_map/dot_general | solution.py:755
  559.8 14.0 %fusion.3 = (bf16[2048,2048]{1,0:T(8,128)(2,1)}, bf16[2048,2048]{1,0:T(8,128)(2,1)}) fusion(bf16[4,4,2,64,2048]{4,3,2,1,0:T(8,128)(2,1)} %get-tuple-element.32, f32[2048]{0:T(1024)S(1)} %mul.310, bf16[2048,2048]{1,0:T(8,128)(2,1)} %get-tuple-element.89), kind=kLoop, calls=%fused_computation.7 | loop fusion | flops 25165824 | bytes 33562624 | tf_op jit(solution)/shard_map/convert_element_type | solution.py:965
  573.8 213.1 %combine.1 = (bf16[4,2,128,2048]{3,2,1,0:T(8,128)(2,1)}, bf16[4,2,128,2048]{3,2,1,0:T(8,128)(2,1)}, f32[4,4,2,128]{3,2,1,0:T(2,128)}) custom-call(bf16[4,4,2,64,2048]{4,3,2,1,0:T(8,128)(2,1)} %bitcast.228, bf16[4,4,2,64,2048]{4,3,2,1,0:T(8,128)(2,1)} %bitcast.234, f32[4,2,4,128]{3,2,1,0:T(4,128)} %get-tuple-element.33.slots, ...), custom_call_target="tpu_custom_call" | custom-call | tf_op jit(solution)/shard_map/combine/pallas_call | solution.py:25
  799.8 24.6 %mixed_grad_heads.1 = bf16[2,8,128,256]{3,2,1,0:T(8,128)(2,1)S(1)} custom-call(bf16[2,128,2048]{2,1,0:T(8,128)(2,1)S(1)} %bitcast.222), custom_call_target="tpu_custom_call" | custom-call | tf_op jit(solution)/shard_map/mixed_grad_heads/pallas_call | solution.py:25
  824.5 18.5 %attend_back.1 = (f32[2,1024,256]{2,1,0:T(8,128)}, f32[2,1024,256]{2,1,0:T(8,128)}, f32[2,1024,256]{2,1,0:T(8,128)}) custom-call(bf16[2,1024,256]{2,1,0:T(8,128)(2,1)S(1)} %bitcast.217, bf16[2,1024,256]{2,1,0:T(8,128)(2,1)S(1)} %bitcast.215, bf16[2,1024,256]{2,1,0:T(8,128)(2,1)S(1)} %bitcast.213, bf16[2,1024,256]{2,1,0:T(8,128)(2,1)S(1)} %bitcast.220, ...), custom_call_target="tpu_custom_call" | custom-call | tf_op jit(solution)/shard_map/attend_back/pallas_call | solution.py:828
  861.1 9.0 convolution_convert_fusion.1
  870.1 77.8 %first_grad.1 = bf16[4,2,128,2048]{3,2,1,0:T(8,128)(2,1)S(1)} custom-call(bf16[2,4,2,128,2048]{4,3,2,1,0:T(8,128)(2,1)} %bitcast.233), custom_call_target="tpu_custom_call" | custom-call | tf_op jit(solution)/shard_map/first_grad/pallas_call | solution.py:25
  952.2 14.1 %convolution_convert_fusion.3 = bf16[1024,2048]{1,0:T(8,128)(2,1)} fusion(bf16[2048,1024]{1,0:T(8,128)(2,1)} %get-tuple-element.86, bf16[2048,2048]{1,0:T(8,128)(2,1)} %get-tuple-element.78), kind=kOutput, calls=%fused_computation.35 | convolution fusion | flops 8592031744 | bytes 16777216 | tf_op jit(solution)/shard_map/dot_general | solution.py:755
  966.4 13.9 %convolution_convert_fusion.4 = bf16[2048,1024]{1,0:T(8,128)(2,1)} fusion(bf16[2048,2048]{1,0:T(8,128)(2,1)} %bitcast.276, bf16[2048,1024]{1,0:T(8,128)(2,1)} %get-tuple-element.61), kind=kOutput, calls=%fused_computation.36 | convolution fusion | flops 8592031744 | bytes 16777216 | tf_op jit(solution)/shard_map/dot_general | solution.py:755
  980.4 14.2 %convolution_convert_fusion.5 = bf16[2048,1024]{1,0:T(8,128)(2,1)} fusion(bf16[2048,2048]{1,0:T(8,128)(2,1)} %bitcast.277, bf16[2048,1024]{1,0:T(8,128)(2,1)} %get-tuple-element.62), kind=kOutput, calls=%fused_computation.37 | convolution fusion | flops 8592031744 | bytes 16777216 | tf_op jit(solution)/shard_map/dot_general | solution.py:755
  1011.5 10.7 convolution_convert_fusion.6
  1022.2 130.8 %weight_grads.1 = (bf16[8,64,768]{2,1,0:T(8,128)(2,1)}, bf16[4,64,2048]{2,1,0:T(8,128)(2,1)}) custom-call(bf16[4,8,64,768]{3,2,1,0:T(8,128)(2,1)} %bitcast.235, bf16[4,2,4,64,2048]{4,3,2,1,0:T(8,128)(2,1)} %bitcast.229), custom_call_target="tpu_custom_call" | custom-call | tf_op jit(solution)/shard_map/weight_grads/pallas_call | solution.py:25
  (208 shorter events, 118.3 us)
Async XLA Ops:
  7.2 220.5 %all-gather.2.cloned.1.call-start = ((), (), s32[]{:S(2)}) async-start(), calls=%async_computation.4 | async-start | bytes 8650752 | tf_op jit(solution)/shard_map/all_gather | solution.py:898
  7.9 1152.1 %reduce-scatter.13.cloned.1.call-start = ((), (), s32[]{:S(2)}) async-start(), calls=%async_computation.8 | async-start | bytes 1081344
  185.1 14.7 %copy-start.38 = (f32[256]{0:T(256)}, f32[256]{0:T(256)S(1)}, u32[]{:S(2)}) copy-start(f32[256]{0:T(256)S(1)} %get-tuple-element.57) | copy-start | bytes 3076
  185.1 14.7 %copy-start.40 = (f32[256]{0:T(256)}, f32[256]{0:T(256)S(1)}, u32[]{:S(2)}) copy-start(f32[256]{0:T(256)S(1)} %get-tuple-element.58) | copy-start | bytes 3076
  185.2 14.6 %copy-start.32 = (f32[1,2048]{1,0:T(1,128)}, f32[1,2048]{1,0:T(1,128)S(1)}, u32[]{:S(2)}) copy-start(f32[1,2048]{1,0:T(1,128)S(1)} %get-tuple-element.76) | copy-start | bytes 24580
  185.2 14.6 %copy-start.34 = (f32[1,2048]{1,0:T(1,128)}, f32[1,2048]{1,0:T(1,128)S(1)}, u32[]{:S(2)}) copy-start(f32[1,2048]{1,0:T(1,128)S(1)} %get-tuple-element.77) | copy-start | bytes 24580
  188.0 37.7 %copy-start.36 = (s32[2,128,8]{1,2,0:T(8,128)S(1)}, s32[2,128,8]{1,2,0:T(8,128)}, u32[]{:S(2)}) copy-start(s32[2,128,8]{1,2,0:T(8,128)} %param.15) | copy-start | bytes 24580
  454.0 14.6 %copy-start.45 = (bf16[4,4,2,64,2048]{4,3,2,1,0:T(8,128)(2,1)S(1)}, bf16[4,4,2,64,2048]{4,3,2,1,0:T(8,128)(2,1)}, u32[]{:S(2)}) copy-start(bf16[4,4,2,64,2048]{4,3,2,1,0:T(8,128)(2,1)} %get-tuple-element.31) | copy-start | bytes 25165828
  454.0 29.8 %slice-start.2 = ((s8[8388608]{0:T(1024)(128)(4,1)}), s8[4194304]{0:T(1024)(128)(4,1)S(1)}, s32[]{:S(2)}) async-start(s8[8388608]{0:T(1024)(128)(4,1)} %bitcast.226), calls=%async_computation.11 | async-start | bytes 8388608
  468.6 15.2 %slice-start.3 = ((s8[8388608]{0:T(1024)(128)(4,1)}), s8[4194304]{0:T(1024)(128)(4,1)S(1)}, s32[]{:S(2)}) async-start(s8[8388608]{0:T(1024)(128)(4,1)} %bitcast.226), calls=%async_computation.12 | async-start | bytes 8388608
  483.8 14.1 %copy-start.37 = (f32[4,4,4,128]{3,2,1,0:T(4,128)S(1)}, f32[4,4,4,128]{3,2,1,0:T(4,128)}, u32[]{:S(2)}) copy-start(f32[4,4,4,128]{3,2,1,0:T(4,128)} %get-tuple-element.30) | copy-start | bytes 98308
  507.1 22.2 %copy-start.46 = (bf16[1,2048,1024]{2,1,0:T(8,128)(2,1)S(1)}, bf16[1,2048,1024]{2,1,0:T(8,128)(2,1)}, u32[]{:S(2)}) copy-start(bf16[1,2048,1024]{2,1,0:T(8,128)(2,1)} %param.22) | copy-start | bytes 12582916
  795.7 47.4 %slice-start = ((s8[6291456]{0:T(1024)(128)(4,1)}), s8[4194304]{0:T(1024)(128)(4,1)S(1)}, s32[]{:S(2)}) async-start(s8[6291456]{0:T(1024)(128)(4,1)} %bitcast.223), calls=%async_computation.9 | async-start | bytes 8388608
  797.4 27.1 %copy-start.4 = (bf16[2048,256]{1,0:T(8,128)(2,1)S(1)}, bf16[2048,256]{1,0:T(8,128)(2,1)}, u32[]{:S(2)}) copy-start(bf16[2048,256]{1,0:T(8,128)(2,1)} %copy-done.3) | copy-start | bytes 3145732
  797.4 27.1 %copy-start.6 = (bf16[2048,256]{1,0:T(8,128)(2,1)S(1)}, bf16[2048,256]{1,0:T(8,128)(2,1)}, u32[]{:S(2)}) copy-start(bf16[2048,256]{1,0:T(8,128)(2,1)} %copy-done.5) | copy-start | bytes 3145732
  797.4 45.6 %slice-start.1 = ((s8[6291456]{0:T(1024)(128)(4,1)}), s8[2097152]{0:T(1024)(128)(4,1)S(1)}, s32[]{:S(2)}) async-start(s8[6291456]{0:T(1024)(128)(4,1)} %bitcast.223), calls=%async_computation.10 | async-start | bytes 4194304
  824.4 18.6 %copy-start.33 = (f32[1,2048]{1,0:T(1,128)S(1)}, f32[1,2048]{1,0:T(1,128)}, u32[]{:S(2)}) copy-start(f32[1,2048]{1,0:T(1,128)} %copy-done.32) | copy-start | bytes 24580
  824.5 18.6 %copy-start.35 = (f32[1,2048]{1,0:T(1,128)S(1)}, f32[1,2048]{1,0:T(1,128)}, u32[]{:S(2)}) copy-start(f32[1,2048]{1,0:T(1,128)} %copy-done.34) | copy-start | bytes 24580
  824.5 18.6 %copy-start.39 = (f32[256]{0:T(256)S(1)}, f32[256]{0:T(256)}, u32[]{:S(2)}) copy-start(f32[256]{0:T(256)} %copy-done.38) | copy-start | bytes 3076
  824.5 18.6 %copy-start.41 = (f32[256]{0:T(256)S(1)}, f32[256]{0:T(256)}, u32[]{:S(2)}) copy-start(f32[256]{0:T(256)} %copy-done.40) | copy-start | bytes 3076
  843.1 13.6 %copy-start.21 = (f32[2,1024,256]{2,1,0:T(8,128)S(1)}, f32[2,1024,256]{2,1,0:T(8,128)}, u32[]{:S(2)}) copy-start(f32[2,1024,256]{2,1,0:T(8,128)} %get-tuple-element.38) | copy-start | bytes 6291460
  952.2 210.8 %reduce-scatter.11.cloned.1.call-start = ((), (), s32[]{:S(2)}) async-start(), calls=%async_computation.7 | async-start | bytes 6291456 | tf_op jit(solution)/shard_map/reduce_scatter | solution.py:988
  966.3 200.8 %reduce-scatter.9.cloned.1.call-start = ((), (), s32[]{:S(2)}) async-start(), calls=%async_computation.6 | async-start | bytes 6291456 | tf_op jit(solution)/shard_map/reduce_scatter | solution.py:987
  980.3 190.9 %reduce-scatter.7.cloned.1.call-start = ((), (), s32[]{:S(2)}) async-start(), calls=%async_computation.5 | async-start | bytes 6291456 | tf_op jit(solution)/shard_map/reduce_scatter | solution.py:986
  (34 other events, 145.6 us)
Sparse Core Ops, SparseCore 0:
  11.0 109.4 all-gather.1
  952.3 153.1 reduce-scatter.12
  1107.9 13.9 reduce-scatter.10
  1124.1 13.2 reduce-scatter.8
  1139.6 13.3 reduce-scatter.6

commit v2 on v1

--- a/solution.py
+++ b/solution.py
@@ -77,7 +77,9 @@
     return [(i, lax.rem(c + i, C), (e, lax.rem(c + i, C), d)) for i in range(1, C)]
 
 
-def start_kernel(E, C, G, tokens, weights, column, gathered, ws, wr, bs, br, hs, hr, ts, tr, ls):
+def start_kernel(
+    E, C, G, tokens, weights, ids, slots, column, gathered, ids_out, slots_out, ws, wr, bs, br, hs, hr, ts, tr, ls, ms, mr, ps, pr
+):
     e, c, d = position()
     me, peers = column_peers(E, C, G)
     planes = plane_peers(E)
@@ -91,6 +93,15 @@
         copy = remote(weights.at[index], mine, ws.at[offset], wr.at[offset], device)
         copy.start()
         weight_copies.append(copy)
+    small = []
+    for offset, _, device in peers:
+        small.append(remote(ids, ids_out.at[me], ms.at[offset], mr.at[offset], device))
+    for i, level, device in level_peers(C):
+        small.append(remote(slots.at[level], slots_out.at[i], ps.at[i], pr.at[i], device))
+    for copy in small:
+        copy.start()
+    ids_out[me] = ids[...]
+    slots_out[0] = slots[c]
     local = [pltpu.make_async_copy(weights.at[me], mine, ls.at[batches])]
     for b in range(batches):
         local.append(pltpu.make_async_copy(tokens.at[b], column.at[b, me], ls.at[b]))
@@ -172,24 +183,26 @@
 
     for copy in weight_copies:
         copy.wait_send()
-    for copy in block_copies:
+    for copy in block_copies + small:
         copy.wait()
     for copy in local[1:]:
         copy.wait()
 
 
-def start(E, C, G, tokens, weights):
+def start(E, C, G, tokens, weights, ids, slots):
     batches, run, width = tokens.shape
     rows, columns = weights.shape[1:]
     return call(
         functools.partial(start_kernel, E, C, G),
-        (tokens, weights),
+        (tokens, weights, ids, slots),
         (
             jax.ShapeDtypeStruct((batches, C * G, run, width), tokens.dtype),
             jax.ShapeDtypeStruct((E * C * G * rows, columns), weights.dtype),
+            jax.ShapeDtypeStruct((C * G,) + ids.shape, ids.dtype),
+            jax.ShapeDtypeStruct(slots.shape, slots.dtype),
         ),
-        [ANY, ANY],
-        (ANY, ANY),
+        [ANY, ANY, VMEM, VMEM],
+        (ANY, ANY, VMEM, VMEM),
         [
             DMA((C * G,)),
             DMA((C * G,)),
@@ -200,6 +213,10 @@
             DMA((batches, 2 * C)),
             DMA((batches, 2 * C)),
             DMA((batches + 1,)),
+            DMA((C * G,)),
+            DMA((C * G,)),
+            DMA((C,)),
+            DMA((C,)),
         ],
         1,
         "start",
@@ -312,268 +329,429 @@
     )
 
 
-def dispatch_kernel(
-    E, C, A, first, second, slots, gates, out_first, out_second, slots_out, gates_out, landed, packed, ss, sr, gs, gr, zs, zr, xs, xr, ls
+def experts_kernel(
+    E,
+    C,
+    rows_x,
+    rows_u,
+    slots,
+    gates,
+    w_gate,
+    w_up,
+    w_down,
+    out_y,
+    out_b,
+    x_out,
+    u_out,
+    pair_out,
+    act_out,
+    gate_back_out,
+    up_back_out,
+    scalars_out,
+    table,
+    scalars,
+    landed,
+    packed,
+    returned,
+    x,
+    u,
+    pair,
+    act,
+    gate_back,
+    up_back,
+    sent,
+    gs,
+    gr,
+    ss,
+    sr,
+    os,
+    zs,
+    zr,
+    xs,
+    xr,
+    ls,
+    ys,
+    yr,
+    bs,
+    us,
+    ur,
+    ks,
+    loads,
+    stores,
 ):
     e, c, d = position()
-    batches, run, width = first.shape
-    cap = out_first.shape[3]
-    levels, planes = level_peers(C), plane_peers(E)
-    everyone = [
-        (i, j, lax.rem(e + i, E), lax.rem(c + j, C)) for i in range(E) for j in range(C) if i + j > 0
+    batches, run, width = rows_x.shape
+    cap = x_out.shape[3]
+    units = w_gate.shape[1]
+    chunks = batches * C
+    total = E * cap
+    slots_kept, kept = packed.shape[1], sent.shape[1]
+    lead, lag = 1, 2
+    everyone = [(k, i) for k in range(E) for i in range(C) if k + i > 0]
+    ahead = [(k, i, (lax.rem(e + k, E), lax.rem(c + i, C), d)) for k, i in everyone]
+    behind = [(k, i, (lax.rem(e + E - k, E), lax.rem(c + C - i, C), d)) for k, i in everyone]
+    meet([device for _, _, device in ahead])
+    sources, arrivals, outs = (rows_x, rows_u), (x_out, u_out), (out_y, out_b)
+
+    high = 2 * c // C
+
+    def far_of(n):
+        return lax.rem((n + batches - 1) // batches, C), lax.rem(n + batches - 1, batches)
+
+    def chunk_of(n):
+        m, b = far_of(n)
+        return b, high * m + (1 - high) * lax.rem(C - m, C)
+
+    def hop(a, b, i, way):
+        there = i + 1 if way == 0 else lax.rem(i + C - 1, C)
+        level = lax.rem(c + 1, C) if way == 0 else lax.rem(c + C - 1, C)
+        return remote(
+            landed.at[a, i, b],
+            landed.at[a, there, b],
+            zs.at[way, a, i, b],
+            zr.at[a, there, b],
+            (e, level, d),
+        )
+
+    def arrival(a, b, i):
+        return remote(
+            landed.at[a, i, b], landed.at[a, i, b], zs.at[0, a, i, b], zr.at[a, i, b], (e, c, 1 - d)
+        )
+
+    def onward(i, way):
+        if way == 0:
+            return jnp.logical_and(i <= c, c < C - 1)
+        return jnp.logical_and(lax.rem(C - i, C) + c < C, c > 0)
+
+    def own(a, b):
+        return pltpu.make_async_copy(sources[a].at[b], landed.at[a, 0, b], os.at[a, b])
+
+    def across(a, n, k):
+        plane = lax.rem(e + k, E)
+        b, i = chunk_of(n)
+        return remote(
+            packed.at[a, lax.rem(n, slots_kept), plane],
+            arrivals[a].at[i, b, k],
+            xs.at[a, i, b, k],
+            xr.at[a, i, b, k],
+            (plane, c, d),
+        )
+
+    def stay(a, n):
+        b, i = chunk_of(n)
+        return pltpu.make_async_copy(
+            packed.at[a, lax.rem(n, slots_kept), e], arrivals[a].at[i, b, 0], ls.at[a, i, b]
+        )
+
+    def back(a, n, b, i, k):
+        return remote(
+            sent.at[a, lax.rem(n, kept), k],
+            returned.at[a, i, b, e],
+            ys.at[a, i, b, k],
+            yr.at[a, i, b, k],
+            (lax.rem(e + E - k, E), c, d),
+        )
+
+    def back_own(a, n, b, i):
+        return pltpu.make_async_copy(
+            sent.at[a, lax.rem(n, kept), 0], returned.at[a, i, b, e], bs.at[a, i, b]
+        )
+
+    def up(a, b, i):
+        return remote(
+            landed.at[a, i, b],
+            outs[a].at[c, b],
+            us.at[a, i, b],
+            ur.at[a, i, b],
+            (e, lax.rem(c + C - i, C), d),
+        )
+
+    def keep(a, b):
+        return pltpu.make_async_copy(landed.at[a, 0, b], outs[a].at[c, b], ks.at[a, b])
+
+    def load(a, b, i):
+        target = (x, u)[a]
+        return pltpu.make_async_copy(arrivals[a].at[i, b], target, loads.at[a])
+
+    def store(j, b, i):
+        source = (pair, act, gate_back, up_back)[j]
+        target = (pair_out, act_out, gate_back_out, up_back_out)[j]
+        return pltpu.make_async_copy(source, target.at[i, b], stores.at[j])
+
+    for b in range(batches):
+        for a in range(2):
+            own(a, b).start()
+    for b in range(batches):
+        for a in range(2):
+            own(a, b).wait()
+            for way in range(2):
+
+                @pl.when(onward(0, way))
+                def _():
+                    hop(a, b, 0, way).start()
+
+    small = [
+        remote(gates.at[device[0], device[1]], table.at[k, i], gs.at[k, i], gr.at[k, i], device)
+        for k, i, device in ahead
     ]
-    meet([(x, y, d) for _, _, x, y in everyone])
-    small = []
-    for i, level, device in levels:
-        small.append(remote(slots.at[level], slots_out.at[c], ss.at[i], sr.at[i], device))
-    for i, j, x, y in everyone:
-        small.append(
-            remote(gates.at[x, y], gates_out.at[e, c], gs.at[i, j], gr.at[i, j], (x, y, d))
-        )
     for copy in small:
         copy.start()
-    rows = (first, second)[:A]
-    outs = (out_first, out_second)[:A]
-
-    def down(a, b, i, device):
-        return remote(rows[a].at[b], landed.at[a, i, b], zs.at[a, i, b], zr.at[a, i, b], device)
-
-    for a in range(A):
-        for b in range(batches):
-            for i, _, device in levels:
-                down(a, b, i, device).start()
-    slots_out[c] = slots[c]
-    gates_out[e, c] = gates[e, c]
-
-    def across(a, b, i, k, plane, level, device):
-        return remote(
-            packed.at[a, i, b, plane],
-            outs[a].at[e, level, b],
-            xs.at[a, i, b, k],
-            xr.at[a, i, b, k],
-            device,
-        )
-
-    def stay(a, b, i, level):
-        return pltpu.make_async_copy(packed.at[a, i, b, e], outs[a].at[e, level, b], ls.at[a, i, b])
-
-    def compact(a, b, i, source):
-        level = lax.rem(c + C - i, C)
-        picks = choose(slots_out[level, b], cap)
-        for piece in range(0, width, 512):
-            part = jnp.dot(
-                picks, source[:, piece : piece + 512], preferred_element_type=f32
+    table[0, 0] = gates[e, c]
+
+    def relay(n):
+        far, b = far_of(n)
+        for a in range(2):
+            for way in range(2):
+                i = far if way == 0 else C - far
+
+                @pl.when((far <= c) if way == 0 else (far + c < C))
+                def _():
+                    arrival(a, b, i).wait_recv()
+
+                    @pl.when(onward(i, way))
+                    def _():
+                        hop(a, b, i, way).start()
+
+    def compact(n):
+        b, i = chunk_of(n)
+        picks = choose(slots[i, b], cap)
+        place = lax.rem(n, slots_kept)
+
+        @pl.when(n >= slots_kept)
+        def _():
+            for a in range(2):
+                for k in range(1, E):
+                    across(a, n - slots_kept, k).wait_send()
+
+        for a in range(2):
+            for at in range(0, width, 512):
+                part = jnp.dot(
+                    picks, landed[a, i, b, :, at : at + 512], preferred_element_type=f32
+                ).astype(bf16)
+                packed[a, place, :, :, at : at + 512] = part.reshape(E, cap, 512)
+            for k in range(1, E):
+                across(a, n, k).start()
+            stay(a, n).start()
+
+    def expert(n):
+        b, i = chunk_of(n)
+        for a in range(2):
+            for k in range(1, E):
+                across(a, n, k).wait_recv()
+            stay(a, n).wait()
+            load(a, b, i).start()
+
+        @pl.when(n > 0)
+        def _():
+            before = chunk_of(n - 1)
+            for j in range(4):
+                store(j, *before).wait()
+
+        @pl.when(n >= kept)
+        def _():
+            before = chunk_of(n - kept)
+            for a in range(2):
+                for k in range(1, E):
+                    back(a, n - kept, *before, k).wait_send()
+
+        holds, gate = [], []
+        cells = lax.broadcasted_iota(jnp.int32, (cap, run), 0).astype(f32)
+        for k in range(E):
+            hold = cells == table[k, i, b]
+            holds.append(hold)
+            gate.append(
+                jnp.sum(jnp.where(hold, table[k, i, batches + b], 0.0), axis=1, keepdims=True)
+            )
+        gate = jnp.concatenate(gate, axis=0)
+        for a in range(2):
+            load(a, b, i).wait()
+        for at in range(0, width, 512):
+            part = u[:, :, at : at + 512].reshape(total, 512).astype(f32)
+            pair[:, :, at : at + 512] = (gate * part).astype(bf16).reshape(E, cap, 512)
+        store(0, b, i).start()
+        inputs = x[...].reshape(total, width)
+        grads = pair[...].reshape(total, width)
+        for at in range(0, units, 256):
+            gate_pre = jnp.dot(inputs, w_gate[:, at : at + 256], preferred_element_type=f32)
+            up_pre = jnp.dot(inputs, w_up[:, at : at + 256], preferred_element_type=f32)
+            act_grad = contract(grads, w_down[at : at + 256, :], (1, 1))
+            sigmoid = jax.nn.sigmoid(gate_pre)
+            silu = gate_pre * sigmoid
+            act[:, at : at + 256] = (silu * up_pre).astype(bf16)
+            gate_back[:, at : at + 256] = (
+                act_grad * up_pre * sigmoid * (1.0 + gate_pre * (1.0 - sigmoid))
             ).astype(bf16)
-            packed[a, i, b, :, :, piece : piece + 512] = part.reshape(E, cap, 512)
-        for k, plane, device in planes:
-            across(a, b, i, k, plane, level, device).start()
-        stay(a, b, i, level).start()
-
-    for a in range(A):
-
-        def own(b, carry, a=a):
-            compact(a, b, 0, rows[a].at[b])
-            return carry
-
-        lax.fori_loop(0, batches, own, 0)
+            up_back[:, at : at + 256] = (act_grad * silu).astype(bf16)
+        for j in range(1, 4):
+            store(j, b, i).start()
+        place = lax.rem(n, kept)
+        gate_grad = jnp.zeros((total, 1), f32)
+        for at in range(0, width, 512):
+            out = jnp.dot(act[...], w_down[:, at : at + 512], preferred_element_type=f32)
+            out = out.astype(bf16).astype(f32)
+            gate_grad += jnp.sum(
+                out * u[:, :, at : at + 512].reshape(total, 512).astype(f32), axis=1, keepdims=True
+            )
+            sent[0, place, :, :, at : at + 512] = (gate * out).astype(bf16).reshape(E, cap, 512)
+            back_rows = contract(gate_back[...], w_gate[at : at + 512, :], (1, 1))
+            back_rows += contract(up_back[...], w_up[at : at + 512, :], (1, 1))
+            sent[1, place, :, :, at : at + 512] = back_rows.astype(bf16).reshape(E, cap, 512)
+        for a in (1, 0):
+            for k in range(1, E):
+                back(a, n, b, i, k).start()
+            back_own(a, n, b, i).start()
+        for k in range(E):
+            scalars[k, i, b] = jnp.sum(
+                jnp.where(holds[k], gate_grad[k * cap : (k + 1) * cap], 0.0), axis=0, keepdims=True
+            )
+
+    def combine(n):
+        b, i = chunk_of(n)
+        picks = choose(slots[i, b], cap)
+        for a in (1, 0):
+            for k in range(1, E):
+                back(a, n, b, i, k).wait_recv()
+            back_own(a, n, b, i).wait()
+            for way in range(2):
+
+                @pl.when(onward(i, way))
+                def _():
+                    hop(a, b, i, way).wait_send()
+
+            for at in range(0, width, 512):
+                part = returned[a, i, b, :, :, at : at + 512].reshape(total, 512)
+                landed[a, i, b, :, at : at + 512] = contract(picks, part, (0, 0)).astype(bf16)
+
+            @pl.when(i > 0)
+            def _():
+                up(a, b, i).start()
+
+            @pl.when(i == 0)
+            def _():
+                keep(a, b).start()
+
+    def step(s, carry):
+        @pl.when(jnp.logical_and(s > 0, s <= batches * (C - 1)))
+        def _():
+            relay(s)
+
+        @pl.when(s < chunks)
+        def _():
+            compact(s)
+
+        @pl.when(jnp.logical_and(s >= lead, s < chunks + lead))
+        def _():
+            expert(s - lead)
+
+        @pl.when(s >= lag)
+        def _():
+            combine(s - lag)
+
+        return carry
+
     for copy in small:
         copy.wait_recv()
-    for a in range(A):
-
-        def arrived(n, carry, a=a):
-            b, i = n // (C - 1), lax.rem(n, C - 1) + 1
-            down(a, b, i, (e, c, d)).wait_recv()
-            compact(a, b, i, landed.at[a, i, b])
-            return carry
-
-        lax.fori_loop(0, batches * (C - 1), arrived, 0)
+    lax.fori_loop(0, chunks + lag, step, 0)
+    scalars_out[e, c] = scalars[0, 0]
+    last = [
+        remote(scalars.at[k, i], scalars_out.at[e, c], ss.at[k, i], sr.at[k, i], device)
+        for k, i, device in behind
+    ]
+    for copy in last:
+        copy.start()
     for copy in small:
         copy.wait_send()
-    for a in range(A):
-
-        def finish(n, carry, a=a):
-            b, i = n // C, lax.rem(n, C)
-            level = lax.rem(c + C - i, C)
-            for k, plane, device in planes:
-                across(a, b, i, k, plane, level, device).wait()
-            stay(a, b, i, level).wait()
+    for j in range(4):
+        store(j, *chunk_of(chunks - 1)).wait()
+
+    def finish(n, carry):
+        b, i = chunk_of(n)
+        for a in range(2):
+
+            @pl.when(n >= chunks - slots_kept)
+            def _():
+                for k in range(1, E):
+                    across(a, n, k).wait_send()
+
+            @pl.when(n >= chunks - kept)
+            def _():
+                for k in range(1, E):
+                    back(a, n, b, i, k).wait_send()
 
             @pl.when(i > 0)
             def _():
-                down(a, b, i, (e, c, d)).wait_send()
-
-            return carry
-
-        lax.fori_loop(0, batches * C, finish, 0)
-
-
-def dispatch(E, C, first, second, slots, gates, cap, collective, name):
-    batches, run, width = first.shape
-    A = 2
-    rows = jax.ShapeDtypeStruct((E, C, batches, cap, width), bf16)
+                up(a, b, i).wait()
+
+            @pl.when(i == 0)
+            def _():
+                keep(a, b).wait()
+
+        return carry
+
+    lax.fori_loop(0, chunks, finish, 0)
+    for copy in last:
+        copy.wait()
+
+
+def run_experts(E, C, rows_x, rows_u, slots, gates, w_gate, w_up, w_down, cap, collective, name):
+    batches, run, width = rows_x.shape
+    units = w_gate.shape[1]
+    total = E * cap
+    kept = 3
+    by_slot = jax.ShapeDtypeStruct((C, batches, E, cap, width), bf16)
+    by_token = jax.ShapeDtypeStruct((C, batches, run, width), bf16)
+    hidden = jax.ShapeDtypeStruct((C, batches, total, units), bf16)
     return call(
-        functools.partial(dispatch_kernel, E, C, A),
-        (first, second, slots, gates),
+        functools.partial(experts_kernel, E, C),
+        (rows_x, rows_u, slots, gates, w_gate, w_up, w_down),
         (
-            rows,
-            rows,
-            jax.ShapeDtypeStruct(slots.shape, f32),
-            jax.ShapeDtypeStruct(gates.shape, f32),
+            by_token,
+            by_token,
+            by_slot,
+            by_slot,
+            by_slot,
+            hidden,
+            hidden,
+            hidden,
+            jax.ShapeDtypeStruct((E, C, batches, 1, run), f32),
         ),
-        [VMEM] * 4,
-        (ANY, ANY, VMEM, VMEM),
+        [ANY, ANY, VMEM, VMEM, VMEM, VMEM, VMEM],
+        (ANY,) * 8 + (VMEM,),
         [
-            pltpu.VMEM((A, C, batches, run, width), bf16),
-            pltpu.VMEM((A, C, batches, E, cap, width), bf16),
-            DMA((C,)),
-            DMA((C,)),
+            pltpu.VMEM(gates.shape, f32),
+            pltpu.VMEM((E, C, batches, 1, run), f32),
+            pltpu.VMEM((2, C, batches, run, width), bf16),
+            pltpu.VMEM((2, kept, E, cap, width), bf16),
+            pltpu.VMEM((2, C, batches, E, cap, width), bf16),
+            pltpu.VMEM((E, cap, width), bf16),
+            pltpu.VMEM((E, cap, width), bf16),
+            pltpu.VMEM((E, cap, width), bf16),
+            pltpu.VMEM((total, units), bf16),
+            pltpu.VMEM((total, units), bf16),
+            pltpu.VMEM((total, units), bf16),
+            pltpu.VMEM((2, kept, E, cap, width), bf16),
             DMA((E, C)),
             DMA((E, C)),
-            DMA((A, C, batches)),
-            DMA((A, C, batches)),
-            DMA((A, C, batches, E)),
-            DMA((A, C, batches, E)),
-            DMA((A, C, batches)),
+            DMA((E, C)),
+            DMA((E, C)),
+            DMA((2, batches)),
+            DMA((2, 2, C, batches)),
+            DMA((2, C, batches)),
+            DMA((2, C, batches, E)),
+            DMA((2, C, batches, E)),
+            DMA((2, C, batches)),
+            DMA((2, C, batches, E)),
+            DMA((2, C, batches, E)),
+            DMA((2, C, batches)),
+            DMA((2, C, batches)),
+            DMA((2, C, batches)),
+            DMA((2, batches)),
+            DMA((2,)),
+            DMA((4,)),
         ],
         collective,
         name,
-        vmem=56,
-    )
-
-
-def combine_kernel(
-    E, C, A, first, second, slots, scalars, out_first, out_second, scalars_out, packed, sums, gs, gr, xs, xr, ls, zs, zr, os
-):
-    e, c, d = position()
-    cap, width = first.shape[3:]
-    batches, run = out_first.shape[1:3]
-    levels, planes = level_peers(C), plane_peers(E)
-    everyone = [
-        (i, j, lax.rem(e + i, E), lax.rem(c + j, C)) for i in range(E) for j in range(C) if i + j > 0
-    ]
-    meet([(x, y, d) for _, _, x, y in everyone])
-    small = []
-    for i, j, x, y in everyone:
-        small.append(
-            remote(scalars.at[x, y], scalars_out.at[e, c], gs.at[i, j], gr.at[i, j], (x, y, d))
-        )
-    for copy in small:
-        copy.start()
-    scalars_out[e, c] = scalars[e, c]
-    rows = (first, second)[:A]
-    outs = (out_first, out_second)[:A]
-
-    def across(a, b, i, k, plane, device):
-        level = lax.rem(c + i, C)
-        return remote(
-            rows[a].at[plane, level, b],
-            packed.at[a, i, b, e],
-            xs.at[a, i, b, k],
-            xr.at[a, i, b, k],
-            device,
-        )
-
-    def stay(a, b, i):
-        level = lax.rem(c + i, C)
-        return pltpu.make_async_copy(
-            rows[a].at[e, level, b], packed.at[a, i, b, e], ls.at[a, i, b]
-        )
-
-    def up(a, b, i):
-        level = lax.rem(c + i, C)
-        return remote(
-            sums.at[a, i, b], outs[a].at[c, b], zs.at[a, i, b], zr.at[a, i, b], (e, level, d)
-        )
-
-    def keep(a, b):
-        return pltpu.make_async_copy(sums.at[a, 0, b], outs[a].at[c, b], os.at[a, b])
-
-    def turn(n):
-        return lax.rem(n, batches), lax.rem(n // batches + 1, C)
-
-    for a in range(A):
-
-        def send(n, carry, a=a):
-            b, i = turn(n)
-            for k, plane, device in planes:
-                across(a, b, i, k, plane, device).start()
-            stay(a, b, i).start()
-            return carry
-
-        lax.fori_loop(0, batches * C, send, 0)
-    for a in range(A):
-
-        def add(n, carry, a=a):
-            b, i = turn(n)
-            for k, plane, device in planes:
-                across(a, b, i, k, plane, device).wait_recv()
-            stay(a, b, i).wait()
-            picks = choose(slots[lax.rem(c + i, C), b], cap)
-            for piece in range(0, width, 512):
-                part = packed[a, i, b, :, :, piece : piece + 512].reshape(E * cap, 512)
-                sums[a, i, b, :, piece : piece + 512] = lax.dot_general(
-                    picks, part, (((0,), (0,)), ((), ())), preferred_element_type=f32
-                ).astype(bf16)
-
-            @pl.when(i > 0)
-            def _():
-                up(a, b, i).start()
-
-            @pl.when(i == 0)
-            def _():
-                keep(a, b).start()
-
-            return carry
-
-        lax.fori_loop(0, batches * C, add, 0)
-    for copy in small:
-        copy.wait()
-    for a in range(A):
-
-        def finish(n, carry, a=a):
-            b, i = turn(n)
-            for k, plane, device in planes:
-                across(a, b, i, k, plane, device).wait_send()
-
-            @pl.when(i > 0)
-            def _():
-                up(a, b, i).wait()
-
-            @pl.when(i == 0)
-            def _():
-                keep(a, b).wait()
-
-            return carry
-
-        lax.fori_loop(0, batches * C, finish, 0)
-
-
-def combine(E, C, first, second, slots, scalars, collective, name):
-    batches, cap, width = first.shape[2:]
-    run = slots.shape[3]
-    A = 2
-    rows = jax.ShapeDtypeStruct((C, batches, run, width), bf16)
-    return call(
-        functools.partial(combine_kernel, E, C, A),
-        (first, second, slots, scalars),
-        (rows, rows, jax.ShapeDtypeStruct(scalars.shape, f32)),
-        [ANY, ANY, VMEM, VMEM],
-        (ANY, ANY, VMEM),
-        [
-            pltpu.VMEM((A, C, batches, E, cap, width), bf16),
-            pltpu.VMEM((A, C, batches, run, width), bf16),
-            DMA((E, C)),
-            DMA((E, C)),
-            DMA((A, C, batches, E)),
-            DMA((A, C, batches, E)),
-            DMA((A, C, batches)),
-            DMA((A, C, batches)),
-            DMA((A, C, batches)),
-            DMA((A, batches)),
-        ],
-        collective,
-        name,
-        vmem=56,
+        vmem=60,
     )
 
 
@@ -896,8 +1074,11 @@
     pieces.append(jnp.broadcast_to(small[:, None, :], (rows, count, small_width)))
     weights = jnp.swapaxes(jnp.concatenate(pieces, axis=2), 0, 1)
     full_output = lax.all_gather(w_output, ALL_AXES, axis=0, tiled=True)
-    ids = lax.all_gather(block_ids, ("context", "dp"), axis=1, tiled=True)
-    column, gathered = start(E, C, G, tokens, weights)
+    places = slot_table(routes, experts).reshape(batches, E, C, run)
+    by_level = jnp.transpose(places, (2, 0, 1, 3))
+    by_expert = jnp.transpose(places, (1, 2, 0, 3))
+    column, gathered, ids, slots = start(E, C, G, tokens, weights, block_ids, by_level)
+    ids = jnp.swapaxes(ids, 0, 1).reshape(batches, length)
     w_qkv = gathered[:, : 3 * size]
     gains = gathered[:, 3 * size : 3 * size + 4].astype(f32)
     full_router = gathered[:, 3 * size + 4 : 3 * size + 4 + experts]
@@ -928,59 +1109,26 @@
     second_low = (second_hat * gains[:, 3]).astype(bf16)
     logits = jnp.dot(second_low, full_router, preferred_element_type=f32)
     router_probs = jax.nn.softmax(logits, axis=-1)
-    places = slot_table(routes, experts).reshape(batches, E, C, run)
-    by_level = jnp.transpose(places, (2, 0, 1, 3))
-    by_expert = jnp.transpose(places, (1, 2, 0, 3))
     gate_table = jnp.transpose(router_probs.reshape(batches, run, E, C), (2, 3, 0, 1))
-    table = jnp.concatenate([by_expert, gate_table], axis=2)
-
-    expert_in, expert_up_in, slots, table = dispatch(
+    table = jnp.concatenate([by_expert, gate_table], axis=2)[:, :, :, None, :]
+
+    mixture, second_grad, x, _, pair_grad, act, gate_pre_grad, up_pre_grad, gate_grad = run_experts(
         E,
         C,
         second_low.reshape(batches, run, width),
         cotangent,
-        by_level,
+        slots,
         table,
+        expert_gate[0],
+        expert_up[0],
+        expert_down[0],
         capacity,
         4,
-        "dispatch",
+        "experts",
     )
     slot_count = E * C * batches * capacity
-    x = expert_in.reshape(slot_count, width)
-    upstream_rows = expert_up_in.reshape(slot_count, width)
-    cells = jnp.arange(capacity, dtype=jnp.int32).astype(f32)
-    holds = table[:, :, :batches, None, :] == cells[:, None]
-    gate = jnp.sum(jnp.where(holds, table[:, :, batches:, None, :], 0.0), axis=-1)
-    gate = gate.reshape(slot_count, 1)
-    w_gate, w_up, w_down = expert_gate[0], expert_up[0], expert_down[0]
-    gate_pre = jnp.dot(x, w_gate, preferred_element_type=f32)
-    up_pre = jnp.dot(x, w_up, preferred_element_type=f32)
-    sigmoid_gate = jax.nn.sigmoid(gate_pre)
-    silu_gate = gate_pre * sigmoid_gate
-    act = (silu_gate * up_pre).astype(bf16)
-    expert_out = jnp.dot(act, w_down, preferred_element_type=f32).astype(bf16).astype(f32)
-    upstream_wide = upstream_rows.astype(f32)
-    gate_grad = jnp.sum(expert_out * upstream_wide, axis=1)
-    out_rows = (gate * expert_out).astype(bf16)
-    pair_grad = (gate * upstream_wide).astype(bf16)
-    act_grad = contract(pair_grad, w_down, (1, 1))
-    gate_pre_grad = (
-        act_grad * up_pre * sigmoid_gate * (1.0 + gate_pre * (1.0 - sigmoid_gate))
-    ).astype(bf16)
-    up_pre_grad = (act_grad * silu_gate).astype(bf16)
-    input_back = contract(gate_pre_grad, w_gate, (1, 1)) + contract(up_pre_grad, w_up, (1, 1))
-    gate_grad = gate_grad.reshape(E, C, batches, capacity, 1)
-    gate_grad = jnp.sum(jnp.where(holds, gate_grad, 0.0), axis=3)
-    by_slot = (E, C, batches, capacity, width)
-    mixture, second_grad, gate_grad = combine(
-        E,
-        C,
-        out_rows.reshape(by_slot),
-        input_back.astype(bf16).reshape(by_slot),
-        slots,
-        gate_grad,
-        5,
-        "combine",
+    x, pair_grad, act, gate_pre_grad, up_pre_grad = (
+        rows.reshape(slot_count, -1) for rows in (x, pair_grad, act, gate_pre_grad, up_pre_grad)
     )
     share = functools.partial(lax.psum_scatter, axis_name="dp", tiled=True)
     grad_gate = share(contract(x, gate_pre_grad, (0, 0)).astype(bf16), scatter_dimension=1)
@@ -990,7 +1138,7 @@
     upstream = cotangent.reshape(own, width).astype(f32)
     mixture = jnp.sum(mixture.astype(f32), axis=0).reshape(own, width)
     activations = (resid + mixture).astype(bf16).reshape(tokens.shape)
-    prob_grad = jnp.transpose(gate_grad, (2, 3, 0, 1)).reshape(own, experts)
+    prob_grad = jnp.transpose(gate_grad[:, :, :, 0, :], (2, 3, 0, 1)).reshape(own, experts)
     logit_grad = router_probs * (
         prob_grad - jnp.sum(router_probs * prob_grad, axis=-1, keepdims=True)
     )

time: 1190 us -> 1080 us (0.908)
  matrix products: 188 us -> 92.7 us
  other arithmetic: 75.5 us -> 54.1 us
  Pallas kernels: 861 us -> 873 us
    dot_general x12 -> x9, matrix products: 127 us -> 74.2 us  [contract(): lax.dot_general(left, right, ((axes[:1], axes[1:]), ((), ())), preferred_...]
    dot_general x3 -> x0, matrix products: 43.8 us -> none  [the longest x1 15.2 us: body(): up_pre = jnp.dot(x, w_up, preferred_element_type=f32)]
    convert_element_type x3 -> x0, other arithmetic: 22 us -> none  [the longest x2 22 us: body(): pair_grad = (gate * upstream_wide).astype(bf16)]
    pallas_call x9 -> x8, Pallas kernels: 830 us -> 843 us  [call(): pl.pallas_call(kernel, out_shape=out_shapes, in_specs=in_specs, out_specs...]
  transfers between devices with their start and end apart: 5 -> 5, of which waited for: 0 -> 0; matrix products, arithmetic and copies ran while one was open for 10% -> 11% of each run, Pallas kernels for 26% -> 29%
where the time goes in v2:
time: 1080 us; the launch traced here: 1060 us
  Pallas kernels  873 us (81%)
  matrix products  92.7 us (9%)
  other arithmetic  54.1 us (5%)
  local copies, waits for them, and re-layouts  28 us (3%)
  between operations  14.7 us (1%)
    pallas_call x8, Pallas kernels, call(): pl.pallas_call(kernel, out_shape=out_shapes, in_specs=in_specs, out_specs...  843 us
    dot_general x9, matrix products, contract(): lax.dot_general(left, right, ((axes[:1], axes[1:]), ((), ())), preferred_...  74.2 us
  transfers between devices with their start and end apart: 5, of which 0 were waited for; matrix products, arithmetic and copies ran while one was open for 11% of the time, Pallas kernels for 29%

profile of v2, /device:TPU:1, one launch (start us, length us, event | category | flops | bytes accessed | tf_op | source)
XLA Modules:
  0.0 1063.8 jit_solution(7635823060742853295)
XLA Ops:
  13.7 131.2 %start.1 = (bf16[2,8,128,2048]{3,2,1,0:T(8,128)(2,1)S(1)}, bf16[2048,896]{1,0:T(8,128)(2,1)S(1)}, s32[8,2,128]{2,1,0:T(2,128)S(1)}, f32[4,2,4,128]{3,2,1,0:T(4,128)S(1)}) custom-call(bf16[2,128,2048]{2,1,0:T(8,128)(2,1)S(1)} %copy-done.1, bf16[8,64,896]{2,1,0:T(8,128)(2,1)S(1)} %maximum_bitcast_fusion.weights, s32[2,128]{1,0:T(2,128)S(1)} %copy-done.11, ...), custom_call_target="tpu_custom_call" | custom-call | tf_op jit(solution)/shard_map/start/pallas_call | solution.py:25
  149.1 9.3 fusion.1
  158.4 9.1 fusion.3
  170.2 5.7 squares.1
  180.3 11.9 %attend.1 = (bf16[2,1024,256]{2,1,0:T(8,128)(2,1)S(1)}, f32[2,2,1024,1]{3,2,1,0:T(8,128)}) custom-call(bf16[2,1024,256]{2,1,0:T(8,128)(2,1)S(1)} %bitcast.194, bf16[2,1024,256]{2,1,0:T(8,128)(2,1)S(1)} %bitcast.192, bf16[2,1024,256]{2,1,0:T(8,128)(2,1)S(1)} %bitcast.190, s32[2,1024,1]{2,1,0:T(8,128)S(1)} %copy.47.row_ids, s32[2,1,1024]{2,1,0:T(1,128)S(1)} %bitcast.201), custom_call_target="tpu_custom_call" | custom-call | tf_op jit(solution)/shard_map/attend/pallas_call | solution.py:987
  192.2 24.7 %mixed_rows.1 = bf16[2,128,2048]{2,1,0:T(8,128)(2,1)S(1)} custom-call(bf16[2,8,128,256]{3,2,1,0:T(8,128)(2,1)S(1)} %bitcast.199), custom_call_target="tpu_custom_call" | custom-call | tf_op jit(solution)/shard_map/mixed_rows/pallas_call | solution.py:25
  218.2 6.2 multiply_reduce_fusion.8
  227.6 439.7 %experts.1 = (bf16[4,2,128,2048]{3,2,1,0:T(8,128)(2,1)}, bf16[4,2,128,2048]{3,2,1,0:T(8,128)(2,1)}, bf16[4,2,4,64,2048]{4,3,2,1,0:T(8,128)(2,1)}, bf16[4,2,4,64,...) custom-call(bf16[2,128,2048]{2,1,0:T(8,128)(2,1)} %bitcast.209, ...), custom_call_target="tpu_custom_call" | custom-call | tf_op jit(solution)/shard_map/experts/pallas_call | solution.py:25
  680.6 25.7 %mixed_grad_heads.1 = bf16[2,8,128,256]{3,2,1,0:T(8,128)(2,1)S(1)} custom-call(bf16[2,128,2048]{2,1,0:T(8,128)(2,1)S(1)} %bitcast.200), custom_call_target="tpu_custom_call" | custom-call | tf_op jit(solution)/shard_map/mixed_grad_heads/pallas_call | solution.py:25
  706.3 18.4 %attend_back.1 = (f32[2,1024,256]{2,1,0:T(8,128)}, f32[2,1024,256]{2,1,0:T(8,128)}, f32[2,1024,256]{2,1,0:T(8,128)}) custom-call(bf16[2,1024,256]{2,1,0:T(8,128)(2,1)S(1)} %bitcast.195, bf16[2,1024,256]{2,1,0:T(8,128)(2,1)S(1)} %bitcast.193, bf16[2,1024,256]{2,1,0:T(8,128)(2,1)S(1)} %bitcast.191, bf16[2,1024,256]{2,1,0:T(8,128)(2,1)S(1)} %bitcast.198, ...), custom_call_target="tpu_custom_call" | custom-call | tf_op jit(solution)/shard_map/attend_back/pallas_call | solution.py:1006
  728.6 7.7 norm_means.1
  738.1 4.9 multiply_convert_fusion.1
  743.0 9.1 convolution_convert_fusion.1
  752.1 77.6 %first_grad.1 = bf16[4,2,128,2048]{3,2,1,0:T(8,128)(2,1)S(1)} custom-call(bf16[2,4,2,128,2048]{4,3,2,1,0:T(8,128)(2,1)} %bitcast.211), custom_call_target="tpu_custom_call" | custom-call | tf_op jit(solution)/shard_map/first_grad/pallas_call | solution.py:25
  834.0 14.0 %convolution_convert_fusion.2 = bf16[1024,2048]{1,0:T(8,128)(2,1)} fusion(bf16[2048,1024]{1,0:T(8,128)(2,1)} %bitcast.260, bf16[2048,2048]{1,0:T(8,128)(2,1)} %bitcast.257), kind=kOutput, calls=%fused_computation.10 | convolution fusion | flops 8592031744 | bytes 16777216 | tf_op jit(solution)/shard_map/dot_general | solution.py:933
  848.1 14.2 %convolution_convert_fusion.3 = bf16[2048,1024]{1,0:T(8,128)(2,1)} fusion(bf16[2048,2048]{1,0:T(8,128)(2,1)} %bitcast.255, bf16[2048,1024]{1,0:T(8,128)(2,1)} %bitcast.259), kind=kOutput, calls=%fused_computation.11 | convolution fusion | flops 8592031744 | bytes 16777216 | tf_op jit(solution)/shard_map/dot_general | solution.py:933
  862.3 14.0 %convolution_convert_fusion.4 = bf16[2048,1024]{1,0:T(8,128)(2,1)} fusion(bf16[2048,2048]{1,0:T(8,128)(2,1)} %bitcast.256, bf16[2048,1024]{1,0:T(8,128)(2,1)} %bitcast.258), kind=kOutput, calls=%fused_computation.12 | convolution fusion | flops 8592031744 | bytes 16777216 | tf_op jit(solution)/shard_map/dot_general | solution.py:933
  877.5 7.2 convolution_convert_fusion
  884.7 8.4 copy.72
  893.2 10.8 %convolution_convert_fusion.5 = bf16[2048,768]{1,0:T(8,128)(2,1)} fusion(bf16[2048,2048]{1,0:T(8,128)(2,1)} %fusion.1, bf16[2048,256]{1,0:T(8,128)(2,1)S(1)} %bitcast.219, bf16[2048,256]{1,0:T(8,128)(2,1)S(1)} %copy-done.30, bf16[2048,256]{1,0:T(8,128)(2,1)S(1)} %copy-done.28), kind=kOutput, calls=%fused_computation.13 | convolution fusion | flops 6453460992 | bytes 14680064 | tf_op jit(solution)/shard_map/dot_general | solution.py:933
  904.0 130.7 %weight_grads.1 = (bf16[8,64,768]{2,1,0:T(8,128)(2,1)}, bf16[4,64,2048]{2,1,0:T(8,128)(2,1)}) custom-call(bf16[4,8,64,768]{3,2,1,0:T(8,128)(2,1)} %bitcast.215, bf16[4,2,4,64,2048]{4,3,2,1,0:T(8,128)(2,1)} %bitcast.208), custom_call_target="tpu_custom_call" | custom-call | tf_op jit(solution)/shard_map/weight_grads/pallas_call | solution.py:25
  1044.5 4.1 bitcast_convert_fusion
  1048.6 4.2 bitcast_convert_fusion.1
  1052.8 4.2 bitcast_convert_fusion.2
  (158 shorter events, 56.1 us)
Async XLA Ops:
  7.2 6.5 copy-start.1
  7.2 6.5 copy-start.11
  7.2 211.0 %all-gather.2.cloned.1.call-start = ((), (), s32[]{:S(2)}) async-start(), calls=%async_computation.4 | async-start | bytes 8650752 | tf_op jit(solution)/shard_map/all_gather | solution.py:1076
  7.9 1033.6 %reduce-scatter.13.cloned.1.call-start = ((), (), s32[]{:S(2)}) async-start(), calls=%async_computation.8 | async-start | bytes 1081344
  145.6 12.8 %copy-start.8 = (bf16[2048,896]{1,0:T(8,128)(2,1)}, bf16[2048,896]{1,0:T(8,128)(2,1)S(1)}, u32[]{:S(2)}) copy-start(bf16[2048,896]{1,0:T(8,128)(2,1)S(1)} %get-tuple-element.31) | copy-start | bytes 11010052
  180.3 11.9 %copy-start.2 = (bf16[2048,256]{1,0:T(8,128)(2,1)}, bf16[2048,256]{1,0:T(8,128)(2,1)S(1)}, u32[]{:S(2)}) copy-start(bf16[2048,256]{1,0:T(8,128)(2,1)S(1)} %get-tuple-element.67) | copy-start | bytes 3145732
  180.3 11.9 %copy-start.4 = (bf16[2048,256]{1,0:T(8,128)(2,1)}, bf16[2048,256]{1,0:T(8,128)(2,1)S(1)}, u32[]{:S(2)}) copy-start(bf16[2048,256]{1,0:T(8,128)(2,1)S(1)} %get-tuple-element.68) | copy-start | bytes 3145732
  668.7 3.7 copy-start.18
  672.4 5.7 slice-start.2
  676.3 48.5 %slice-start = ((s8[6291456]{0:T(1024)(128)(4,1)}), s8[4194304]{0:T(1024)(128)(4,1)S(1)}, s32[]{:S(2)}) async-start(s8[6291456]{0:T(1024)(128)(4,1)} %bitcast.205), calls=%async_computation.9 | async-start | bytes 8388608
  678.1 46.6 %slice-start.1 = ((s8[6291456]{0:T(1024)(128)(4,1)}), s8[2097152]{0:T(1024)(128)(4,1)S(1)}, s32[]{:S(2)}) async-start(s8[6291456]{0:T(1024)(128)(4,1)} %bitcast.205), calls=%async_computation.10 | async-start | bytes 4194304
  680.6 25.7 %copy-start.3 = (bf16[2048,256]{1,0:T(8,128)(2,1)S(1)}, bf16[2048,256]{1,0:T(8,128)(2,1)}, u32[]{:S(2)}) copy-start(bf16[2048,256]{1,0:T(8,128)(2,1)} %copy-done.2) | copy-start | bytes 3145732
  680.6 25.7 %copy-start.5 = (bf16[2048,256]{1,0:T(8,128)(2,1)S(1)}, bf16[2048,256]{1,0:T(8,128)(2,1)}, u32[]{:S(2)}) copy-start(bf16[2048,256]{1,0:T(8,128)(2,1)} %copy-done.4) | copy-start | bytes 3145732
  728.5 9.6 copy-start.22
  738.1 4.9 copy-start.25
  738.1 4.9 copy-start.9
  743.0 9.1 copy-start.27
  743.0 9.1 copy-start.29
  833.9 210.5 %reduce-scatter.11.cloned.1.call-start = ((), (), s32[]{:S(2)}) async-start(), calls=%async_computation.7 | async-start | bytes 6291456 | tf_op jit(solution)/shard_map/reduce_scatter | solution.py:1136
  848.0 200.6 %reduce-scatter.9.cloned.1.call-start = ((), (), s32[]{:S(2)}) async-start(), calls=%async_computation.6 | async-start | bytes 6291456 | tf_op jit(solution)/shard_map/reduce_scatter | solution.py:1135
  862.3 190.6 %reduce-scatter.7.cloned.1.call-start = ((), (), s32[]{:S(2)}) async-start(), calls=%async_computation.5 | async-start | bytes 6291456 | tf_op jit(solution)/shard_map/reduce_scatter | solution.py:1134
  884.7 8.4 copy-start.26
  884.7 8.4 copy-start.28
  884.7 8.4 copy-start.30
  (17 other events, 40.4 us)
Sparse Core Ops, SparseCore 0:
  11.0 113.6 all-gather.1
  834.1 153.8 reduce-scatter.12
  990.9 13.7 reduce-scatter.10
  1007.4 13.3 reduce-scatter.8
  1023.7 13.3 reduce-scatter.6

commit v3 on v2

--- a/solution.py
+++ b/solution.py
@@ -78,21 +78,114 @@
 
 
 def start_kernel(
-    E, C, G, tokens, weights, ids, slots, column, gathered, ids_out, slots_out, ws, wr, bs, br, hs, hr, ts, tr, ls, ms, mr, ps, pr
+    E,
+    C,
+    G,
+    tokens,
+    weights,
+    small_weights,
+    output,
+    ids,
+    slots,
+    column,
+    gathered,
+    small_gathered,
+    full_output,
+    ids_out,
+    slots_out,
+    ws,
+    wr,
+    bs,
+    br,
+    hs,
+    hr,
+    ts,
+    tr,
+    ls,
+    ms,
+    mr,
+    ps,
+    pr,
+    fs,
+    fr,
+    gs,
+    gr,
 ):
     e, c, d = position()
     me, peers = column_peers(E, C, G)
     planes = plane_peers(E)
     batches = tokens.shape[0]
-    rows = weights.shape[1]
-    per_plane = C * G * rows
+    sibling = (e, c, 1 - d)
     meet([device for _, _, device in peers] + [device for _, _, device in planes])
-    mine = gathered.at[pl.ds(pl.multiple_of(e * per_plane + me * rows, rows), rows)]
+    kinds = ((weights, gathered), (small_weights, small_gathered))
     weight_copies = []
-    for offset, index, device in peers:
-        copy = remote(weights.at[index], mine, ws.at[offset], wr.at[offset], device)
+    for j, (source, target) in enumerate(kinds):
+        for offset, index, device in peers:
+            part = source.at[index] if j == 0 else source
+            weight_copies.append(
+                remote(part, target.at[e, me], ws.at[j, offset], wr.at[j, offset], device)
+            )
+    for copy in weight_copies:
         copy.start()
-        weight_copies.append(copy)
+    local = [
+        pltpu.make_async_copy(weights.at[me], gathered.at[e, me], ls.at[0]),
+        pltpu.make_async_copy(small_weights, small_gathered.at[e, me], ls.at[1]),
+        pltpu.make_async_copy(output, full_output.at[e, c, d], ls.at[2]),
+    ]
+    for b in range(batches):
+        local.append(pltpu.make_async_copy(tokens.at[b], column.at[b, me], ls.at[3 + b]))
+    for copy in local:
+        copy.start()
+
+    def source_of(item):
+        return output if item == 0 else tokens.at[item - 1]
+
+    def place(item, level):
+        return full_output.at[e, level, d] if item == 0 else column.at[item - 1, level * G + d]
+
+    def to_sibling(source, item, level, arrival):
+        return remote(
+            source, place(item, level), ts.at[item, arrival], tr.at[item, arrival], sibling
+        )
+
+    def step(hop, source, item, level, up):
+        to = (e, c + 1, d) if up else (e, c - 1, d)
+        way = 0 if up else 1
+        return remote(
+            source, place(item, level), hs.at[way, item, hop], hr.at[way, item, hop], to
+        )
+
+    def relay(item, hop):
+        for up in (True, False):
+            level = c - hop if up else c + hop
+            here = (c >= hop) if up else (c + hop < C)
+            onward = (c < C - 1) if up else (c > 0)
+
+            @pl.when(here)
+            def _():
+                landed = place(item, level)
+                step(hop - 1, landed, item, level, up).wait_recv()
+                if hop < C - 1:
+
+                    @pl.when(onward)
+                    def _():
+                        step(hop, landed, item, level, up).start()
+
+                if G > 1:
+                    to_sibling(landed, item, level, hop if up else C - 1 + hop).start()
+
+    for item in range(batches + 1):
+
+        @pl.when(c < C - 1)
+        def _():
+            step(0, source_of(item), item, c, True).start()
+
+        @pl.when(c > 0)
+        def _():
+            step(0, source_of(item), item, c, False).start()
+
+        if G > 1:
+            to_sibling(source_of(item), item, c, 0).start()
     small = []
     for offset, _, device in peers:
         small.append(remote(ids, ids_out.at[me], ms.at[offset], mr.at[offset], device))
@@ -102,121 +195,107 @@
         copy.start()
     ids_out[me] = ids[...]
     slots_out[0] = slots[c]
-    local = [pltpu.make_async_copy(weights.at[me], mine, ls.at[batches])]
-    for b in range(batches):
-        local.append(pltpu.make_async_copy(tokens.at[b], column.at[b, me], ls.at[b]))
-    for copy in local:
-        copy.start()
-
-    sibling = (e, c, 1 - d)
-
-    def to_sibling(source, b, index, level):
-        return remote(source, column.at[b, index], ts.at[b, level], tr.at[b, level], sibling)
-
-    def step(hop, source, b, index, up):
-        to = (e, c + 1, d) if up else (e, c - 1, d)
-        way = 0 if up else 1
-        return remote(source, column.at[b, index], hs.at[way, b, hop], hr.at[way, b, hop], to)
-
-    for b in range(batches):
-
-        @pl.when(c < C - 1)
-        def _():
-            step(0, tokens.at[b], b, me, True).start()
-
-        @pl.when(c > 0)
-        def _():
-            step(0, tokens.at[b], b, me, False).start()
-
-        if G > 1:
-            to_sibling(tokens.at[b], b, me, 0).start()
     for copy in weight_copies:
         copy.wait_recv()
-    local[0].wait()
-    block = gathered.at[pl.ds(pl.multiple_of(e * per_plane, per_plane), per_plane)]
-    block_copies = []
-    for i, _, device in planes:
-        copy = remote(block, block, bs.at[i], br.at[i], device)
-        copy.start()
-        block_copies.append(copy)
+    for copy in local[:3]:
+        copy.wait()
+    plane_copies = []
+    for j, (_, target) in enumerate(kinds):
+        for i, _, device in planes:
+            copy = remote(target.at[e], target.at[e], bs.at[j, i], br.at[j, i], device)
+            copy.start()
+            plane_copies.append(copy)
     for hop in range(1, C):
-        for b in range(batches):
-            for up in (True, False):
-                origin = c - hop if up else c + hop
-                index = origin * G + d
-                level = hop if up else C - 1 + hop
-                here = (c >= hop) if up else (c + hop < C)
-                onward = (c < C - 1) if up else (c > 0)
-
-                @pl.when(here)
-                def _():
-                    landed = column.at[b, index]
-                    step(hop - 1, landed, b, index, up).wait_recv()
-                    if hop < C - 1:
-
-                        @pl.when(onward)
-                        def _():
-                            step(hop, landed, b, index, up).start()
-
-                    if G > 1:
-                        to_sibling(landed, b, index, level).start()
-
-    for b in range(batches):
+        relay(0, hop)
+
+    def output_copy(i, plane, device):
+        mine = full_output.at[e, :, d]
+        return remote(mine, mine, fs.at[i], fr.at[i], device)
+
+    def output_sibling(i):
+        part = full_output.at[lax.rem(e + E - i, E), :, d]
+        return remote(part, part, gs.at[i], gr.at[i], sibling)
+
+    for i, plane, device in planes:
+        output_copy(i, plane, device).start()
+    for hop in range(1, C):
+        for item in range(1, batches + 1):
+            relay(item, hop)
+    for i, plane, device in planes:
+        output_copy(i, plane, device).wait_recv()
         if G > 1:
-            to_sibling(tokens.at[b], b, me, 0).wait()
+            output_sibling(i).start()
+
+    for item in range(batches + 1):
+        if G > 1:
+            to_sibling(source_of(item), item, c, 0).wait()
         for hop in range(C - 1):
             for up in (True, False):
-                level = hop + 1 if up else C + hop
+                arrival = hop + 1 if up else C + hop
                 origin = c - hop if up else c + hop
-                sends = jnp.logical_and(origin >= 0, c < C - 1) if up else jnp.logical_and(origin < C, c > 0)
-                arrives = (c >= hop + 1) if up else (c + hop + 1 < C)
+                if up:
+                    sends = jnp.logical_and(origin >= 0, c < C - 1)
+                    arrives = c >= hop + 1
+                else:
+                    sends = jnp.logical_and(origin < C, c > 0)
+                    arrives = c + hop + 1 < C
 
                 @pl.when(sends)
                 def _():
-                    step(hop, tokens.at[b], b, me, up).wait_send()
+                    step(hop, source_of(item), item, c, up).wait_send()
 
                 if G > 1:
 
                     @pl.when(arrives)
                     def _():
-                        to_sibling(tokens.at[b], b, me, level).wait()
-
+                        to_sibling(source_of(item), item, c, arrival).wait()
+
+    for i, plane, device in planes:
+        output_copy(i, plane, device).wait_send()
+        if G > 1:
+            output_sibling(i).wait()
     for copy in weight_copies:
         copy.wait_send()
-    for copy in block_copies + small:
+    for copy in plane_copies + small + local[3:]:
         copy.wait()
-    for copy in local[1:]:
-        copy.wait()
-
-
-def start(E, C, G, tokens, weights, ids, slots):
+
+
+def start(E, C, G, tokens, weights, small_weights, output, ids, slots):
     batches, run, width = tokens.shape
+    count = C * G
     rows, columns = weights.shape[1:]
+    items = batches + 1
     return call(
         functools.partial(start_kernel, E, C, G),
-        (tokens, weights, ids, slots),
+        (tokens, weights, small_weights, output, ids, slots),
         (
-            jax.ShapeDtypeStruct((batches, C * G, run, width), tokens.dtype),
-            jax.ShapeDtypeStruct((E * C * G * rows, columns), weights.dtype),
-            jax.ShapeDtypeStruct((C * G,) + ids.shape, ids.dtype),
+            jax.ShapeDtypeStruct((batches, count, run, width), tokens.dtype),
+            jax.ShapeDtypeStruct((E, count, rows, columns), weights.dtype),
+            jax.ShapeDtypeStruct((E, count) + small_weights.shape, weights.dtype),
+            jax.ShapeDtypeStruct((E, C, G, rows, width), weights.dtype),
+            jax.ShapeDtypeStruct((count,) + ids.shape, ids.dtype),
             jax.ShapeDtypeStruct(slots.shape, slots.dtype),
         ),
-        [ANY, ANY, VMEM, VMEM],
-        (ANY, ANY, VMEM, VMEM),
+        [ANY, ANY, ANY, ANY, VMEM, VMEM],
+        (ANY, ANY, ANY, ANY, VMEM, VMEM),
         [
-            DMA((C * G,)),
-            DMA((C * G,)),
+            DMA((2, count)),
+            DMA((2, count)),
+            DMA((2, E)),
+            DMA((2, E)),
+            DMA((2, items, C)),
+            DMA((2, items, C)),
+            DMA((items, 2 * C)),
+            DMA((items, 2 * C)),
+            DMA((items + 2,)),
+            DMA((count,)),
+            DMA((count,)),
+            DMA((C,)),
+            DMA((C,)),
             DMA((E,)),
             DMA((E,)),
-            DMA((2, batches, C)),
-            DMA((2, batches, C)),
-            DMA((batches, 2 * C)),
-            DMA((batches, 2 * C)),
-            DMA((batches + 1,)),
-            DMA((C * G,)),
-            DMA((C * G,)),
-            DMA((C,)),
-            DMA((C,)),
+            DMA((E,)),
+            DMA((E,)),
         ],
         1,
         "start",
@@ -277,43 +356,6 @@
         functools.partial(to_tokens_kernel, E, C, G),
         (heads,),
         jax.ShapeDtypeStruct((batches, run, count * size), heads.dtype),
-        [ANY],
-        ANY,
-        [DMA((batches, C * G)), DMA((batches, C * G)), DMA((batches,))],
-        collective,
-        name,
-    )
-
-
-def to_heads_kernel(E, C, G, rows, heads, ss, rs, ls):
-    me, peers = column_peers(E, C, G)
-    batches = rows.shape[0]
-    size = heads.shape[3]
-    meet([device for _, _, device in peers])
-
-    def part(b, index):
-        return rows.at[b, :, pl.ds(pl.multiple_of(index * size, size), size)]
-
-    copies = []
-    for b in range(batches):
-        for offset, index, device in peers:
-            copies.append(
-                remote(part(b, index), heads.at[b, me], ss.at[b, offset], rs.at[b, offset], device)
-            )
-        copies.append(pltpu.make_async_copy(part(b, me), heads.at[b, me], ls.at[b]))
-    for copy in copies:
-        copy.start()
-    for copy in copies:
-        copy.wait()
-
-
-def to_heads(E, C, G, rows, collective, name):
-    batches, run, width = rows.shape
-    count = C * G
-    return call(
-        functools.partial(to_heads_kernel, E, C, G),
-        (rows,),
-        jax.ShapeDtypeStruct((batches, count, run, width // count), rows.dtype),
         [ANY],
         ANY,
         [DMA((batches, C * G)), DMA((batches, C * G)), DMA((batches,))],
@@ -755,177 +797,547 @@
     )
 
 
-def scatter_kernel(E, C, G, rows, out, other, sums, cs, cr, zs, zr, ls):
-    e, c, d = position()
-    batches = rows.shape[0]
-    run, width = rows.shape[3:]
-    levels = level_peers(C)
-    sibling = (e, c, 1 - d)
-    meet([device for _, _, device in levels] + ([sibling] if G > 1 else []))
-
-    def swap(b, level):
-        return remote(
-            rows.at[b, level, 1 - d], other.at[b, level], cs.at[b, level], cr.at[b, level], sibling
-        )
-
-    def send(b, i, level):
-        return remote(
-            sums.at[b, level], out.at[c, b], zs.at[b, i], zr.at[b, i], (e, level, d)
-        )
-
-    def keep(b):
-        return pltpu.make_async_copy(sums.at[b, c], out.at[c, b], ls.at[b])
-
-    order = [(i, lax.rem(c + i, C)) for i in range(1, C)] + [(0, c)]
-    if G > 1:
-        for i, level in order:
-            for b in range(batches):
-                swap(b, level).start()
-    for i, level in order:
-        for b in range(batches):
-            if G > 1:
-                swap(b, level).wait_recv()
-                sums[b, level] = (
-                    rows[b, level, d].astype(f32) + other[b, level].astype(f32)
-                ).astype(bf16)
-            else:
-                sums[b, level] = rows[b, level, d]
-            if i > 0:
-                send(b, i, level).start()
-            else:
-                keep(b).start()
-    for i, level in order:
-        for b in range(batches):
-            if G > 1:
-                swap(b, level).wait_send()
-            if i > 0:
-                send(b, i, level).wait()
-            else:
-                keep(b).wait()
-
-
-def column_scatter(E, C, G, rows, collective, name):
-    batches, _, _, run, width = rows.shape
-    return call(
-        functools.partial(scatter_kernel, E, C, G),
-        (rows,),
-        jax.ShapeDtypeStruct((C, batches, run, width), bf16),
-        [VMEM],
-        ANY,
-        [
-            pltpu.VMEM((batches, C, run, width), bf16),
-            pltpu.VMEM((batches, C, run, width), bf16),
-            DMA((batches, C)),
-            DMA((batches, C)),
-            DMA((batches, C)),
-            DMA((batches, C)),
-            DMA((batches,)),
-        ],
-        collective,
-        name,
-        vmem=48,
-    )
-
-
-def weights_kernel(
-    E, C, G, qkv, proj, out_qkv, out_proj, plane_qkv, sum_qkv, other, pair, plane_proj, sum_proj, as_, ar, bs, br, cs, cr, ds, dr, es, er, ls
+def middle_kernel(
+    E,
+    C,
+    G,
+    rows,
+    mixed,
+    grads,
+    x,
+    pair,
+    gate_back,
+    up_back,
+    act,
+    heads,
+    proj,
+    own_gate,
+    own_up,
+    own_down,
+    other_gate,
+    other_up,
+    other_down,
+    hidden,
+    wide,
+    kept,
+    sent,
+    swap,
+    swapped,
+    chip,
+    plane_parts,
+    level_part,
+    hs,
+    hr,
+    hl,
+    cs,
+    cr,
+    ps,
+    pr,
+    zs,
+    zr,
+    rs,
+    wide_sem,
+    ks,
+    xs,
+    xr,
 ):
     e, c, d = position()
     me, peers = column_peers(E, C, G)
     planes, levels = plane_peers(E), level_peers(C)
+    batches = rows.shape[0]
+    size = heads.shape[3]
+    block, width = swap.shape[1:]
+    step = wide.shape[2]
+    half = own_gate.shape[1]
     sibling = (e, c, 1 - d)
     meet([device for _, _, device in peers] + [device for _, _, device in planes])
-    swaps = []
-    if G > 1:
-        for level in range(C):
-            swaps.append(
-                remote(proj.at[level, 1 - d], other.at[level], cs.at[level], cr.at[level], sibling)
+
+    def head_part(b, index):
+        return rows.at[b, :, pl.ds(pl.multiple_of(index * size, size), size)]
+
+    head_copies = []
+    for b in range(batches):
+        for offset, index, device in peers:
+            head_copies.append(
+                remote(head_part(b, index), heads.at[b, me], hs.at[b, offset], hr.at[b, offset], device)
             )
-    for copy in swaps:
+        head_copies.append(pltpu.make_async_copy(head_part(b, me), heads.at[b, me], hl.at[b]))
+    for copy in head_copies:
         copy.start()
-    first = []
-    for k, plane, device in planes:
-        first.append(remote(qkv.at[plane], plane_qkv.at[k], as_.at[k], ar.at[k], device))
-    for copy in first:
+
+    hidden_copies = [
+        pltpu.make_async_copy(source, hidden.at[j], rs.at[j])
+        for j, source in enumerate((gate_back, up_back, act))
+    ]
+    for copy in hidden_copies:
         copy.start()
-    middle = []
-    for level in range(C):
-        if G > 1:
-            swaps[level].wait_recv()
-            pair[level] = (proj[level, d].astype(f32) + other[level].astype(f32)).astype(bf16)
-        else:
-            pair[level] = proj[level, d]
-        for k, plane, device in planes:
-            copy = remote(
-                pair.at[level, plane], plane_proj.at[level, k], ds.at[level, k], dr.at[level, k], device
-            )
+    count = width // step
+    sources = [x] * count + [pair] * count
+
+    def wide_copy(item):
+        at = (item % count) * step
+        return pltpu.make_async_copy(
+            sources[item].at[:, pl.ds(at, step)], wide.at[item % 2], wide_sem.at[item % 2]
+        )
+
+    wide_copy(0).start()
+    wide_copy(1).start()
+
+    def chip_copy(level):
+        return remote(swap.at[level], swapped.at[level], cs.at[level], cr.at[level], sibling)
+
+    def proj_part(core, level):
+        part = mixed[:, level, core].reshape(block, mixed.shape[4])
+        return jnp.dot(part, grads[...], preferred_element_type=f32)
+
+    def plane_copy(level, k, device):
+        return remote(
+            chip.at[level, lax.rem(e + k, E)],
+            plane_parts.at[level, k],
+            ps.at[level, k],
+            pr.at[level, k],
+            device,
+        )
+
+    def give(level, carry):
+        swap[level] = proj_part(1 - d, level).astype(bf16)
+        chip_copy(level).start()
+        return carry
+
+    def take(level, carry):
+        part = proj_part(d, level)
+        chip_copy(level).wait_recv()
+        part = (part + swapped[level].astype(f32)).astype(bf16)
+        chip[level] = part.reshape(chip.shape[1:])
+        for k, _, device in planes:
+            plane_copy(level, k, device).start()
+        return carry
+
+    lax.fori_loop(0, C, give, 0)
+    lax.fori_loop(0, C, take, 0)
+
+    def plane_sum(level, carry):
+        total = chip[level, e].astype(f32)
+        for k, _, device in planes:
+            plane_copy(level, k, device).wait_recv()
+            total = total + plane_parts[level, k].astype(f32)
+        level_part[level] = total.astype(bf16)
+        return carry
+
+    def keep_copy(j, at, place):
+        target = (own_gate, own_up, own_down)[j]
+        where = target.at[:, pl.ds(at, step)] if j == 2 else target.at[pl.ds(at, step)]
+        return pltpu.make_async_copy(kept.at[place], where, ks.at[place])
+
+    def send_copy(j, at, place):
+        target = (other_gate, other_up, other_down)[j]
+        where = target.at[:, pl.ds(at, step)] if j == 2 else target.at[pl.ds(at, step)]
+        return remote(sent.at[place], where, xs.at[place], xr.at[place], sibling)
+
+    kept_copies, sent_copies = [], []
+    for copy in hidden_copies:
+        copy.wait()
+    for item in range(2 * count):
+        wide_copy(item).wait()
+        at = (item % count) * step
+        left = wide[item % 2]
+        for j in (0, 1) if item < count else (2,):
+            place = len(sent_copies)
+
+            def product(core):
+                part = hidden[j, :, pl.ds(pl.multiple_of(core * half, half), half)]
+                return contract(part, left, (0, 0)) if j == 2 else contract(left, part, (0, 0))
+
+            sent[place] = product(1 - d).astype(bf16)
+            copy = send_copy(j, at, place)
             copy.start()
-            middle.append(copy)
-    for copy in first:
-        copy.wait_recv()
-    total = qkv[e].astype(f32)
-    for k in range(1, E):
-        total = total + plane_qkv[k].astype(f32)
-    sum_qkv[...] = total.astype(bf16)
-    second = []
-    for offset, index, device in peers:
-        copy = remote(sum_qkv.at[index], out_qkv.at[me], bs.at[offset], br.at[offset], device)
-        copy.start()
-        second.append(copy)
-    out_qkv[me] = sum_qkv[me]
-    for copy in middle:
-        copy.wait_recv()
-    for level in range(C):
-        total = pair[level, e].astype(f32)
-        for k in range(1, E):
-            total = total + plane_proj[level, k].astype(f32)
-        sum_proj[level] = total.astype(bf16)
-    last = []
-    for i, level, device in levels:
-        copy = remote(sum_proj.at[level], out_proj.at[c], es.at[i], er.at[i], device)
-        copy.start()
-        last.append(copy)
-    out_proj[c] = sum_proj[c]
-    for copy in swaps + first + middle:
-        copy.wait_send()
-    for copy in second + last:
+            sent_copies.append(copy)
+            if place >= 2:
+                kept_copies[place - 2].wait()
+            kept[place % 2] = product(d)
+            copy = keep_copy(j, at, place % 2)
+            copy.start()
+            kept_copies.append(copy)
+        if item + 2 < 2 * count:
+            wide_copy(item + 2).start()
+        if item == count - 1:
+            lax.fori_loop(0, C, plane_sum, 0)
+            level_copies = []
+            for i, level, device in levels:
+                copy = remote(level_part.at[level], proj.at[c], zs.at[i], zr.at[i], device)
+                copy.start()
+                level_copies.append(copy)
+            proj[c] = level_part[c]
+
+    for copy in kept_copies[-2:]:
         copy.wait()
-
-
-def weight_scatter(E, C, G, qkv, proj, collective, name):
-    count, rows, columns = qkv.shape[1:]
-    width = proj.shape[4]
+    for copy in sent_copies + level_copies + head_copies:
+        copy.wait()
+
+    def done(level, carry):
+        chip_copy(level).wait_send()
+        for k, _, device in planes:
+            plane_copy(level, k, device).wait_send()
+        return carry
+
+    lax.fori_loop(0, C, done, 0)
+
+
+def middle(E, C, G, rows, mixed, grads, x, pair, gate_back, up_back, act, collective, name):
+    batches, run, width = rows.shape
+    count = C * G
+    part = mixed.shape[3]
+    block = E * part
+    total, units = act.shape
+    half = units // G
+    step = min(512, width)
+    items = 3 * (width // step)
+    tall = (width, half)
+    flat = (half, width)
     return call(
-        functools.partial(weights_kernel, E, C, G),
-        (qkv, proj),
+        functools.partial(middle_kernel, E, C, G),
+        (rows, mixed, grads, x, pair, gate_back, up_back, act),
         (
-            jax.ShapeDtypeStruct((count, rows, columns), bf16),
-            jax.ShapeDtypeStruct((C, rows, width), bf16),
+            jax.ShapeDtypeStruct((batches, count, run, width // count), bf16),
+            jax.ShapeDtypeStruct((C, part, width), bf16),
+            jax.ShapeDtypeStruct(tall, f32),
+            jax.ShapeDtypeStruct(tall, f32),
+            jax.ShapeDtypeStruct(flat, f32),
+            jax.ShapeDtypeStruct(tall, bf16),
+            jax.ShapeDtypeStruct(tall, bf16),
+            jax.ShapeDtypeStruct(flat, bf16),
         ),
-        [VMEM, VMEM],
-        (VMEM, VMEM),
+        [ANY, VMEM, VMEM] + [ANY] * 5,
+        (ANY, VMEM) + (ANY,) * 6,
         [
-            pltpu.VMEM((E, count, rows, columns), bf16),
-            pltpu.VMEM((count, rows, columns), bf16),
-            pltpu.VMEM((C, E, rows, width), bf16),
-            pltpu.VMEM((C, E, rows, width), bf16),
-            pltpu.VMEM((C, E, rows, width), bf16),
-            pltpu.VMEM((C, rows, width), bf16),
-            DMA((E,)),
-            DMA((E,)),
-            DMA((count,)),
-            DMA((count,)),
+            pltpu.VMEM((3, total, units), bf16),
+            pltpu.VMEM((2, total, step), bf16),
+            pltpu.VMEM((2, step, half), f32),
+            pltpu.VMEM((items, step, half), bf16),
+            pltpu.VMEM((C, block, width), bf16),
+            pltpu.VMEM((C, block, width), bf16),
+            pltpu.VMEM((C, E, part, width), bf16),
+            pltpu.VMEM((C, E, part, width), bf16),
+            pltpu.VMEM((C, part, width), bf16),
+            DMA((batches, count)),
+            DMA((batches, count)),
+            DMA((batches,)),
             DMA((C,)),
             DMA((C,)),
             DMA((C, E)),
             DMA((C, E)),
             DMA((C,)),
             DMA((C,)),
-            DMA((1,)),
+            DMA((3,)),
+            DMA((2,)),
+            DMA((2,)),
+            DMA((items,)),
+            DMA((items,)),
         ],
         collective,
         name,
-        vmem=56,
+        vmem=60,
+    )
+
+
+def finish_kernel(
+    E,
+    C,
+    G,
+    raw,
+    w_qkv,
+    normed,
+    small,
+    first,
+    out_qkv,
+    out_small,
+    small_parts,
+    small_sum,
+    swap,
+    swapped,
+    own,
+    passed,
+    tokens,
+    parts,
+    plane_parts,
+    sum_qkv,
+    cs,
+    cr,
+    zs,
+    zr,
+    ts,
+    qs,
+    qr,
+    os,
+    orr,
+    ss,
+    sr,
+    fs,
+    fr,
+):
+    e, c, d = position()
+    me, peers = column_peers(E, C, G)
+    planes = plane_peers(E)
+    batches, _, run, columns = raw.shape
+    width = w_qkv.shape[0]
+    rows = batches * run
+    sibling = (e, c, 1 - d)
+    meet([device for _, _, device in peers] + [device for _, _, device in planes])
+    block = tokens.shape[2]
+
+    def token_copy(item):
+        plane = lax.rem(e + 1 + item, E)
+        return pltpu.make_async_copy(
+            normed.at[:, pl.ds(pl.multiple_of(plane * block, block), block)],
+            tokens.at[item % 2],
+            ts.at[item % 2],
+        )
+
+    token_copy(0).start()
+    token_copy(1).start()
+    small_copies = [
+        remote(small.at[plane], small_parts.at[i], ss.at[i], sr.at[i], device)
+        for i, plane, device in planes
+    ]
+    for copy in small_copies:
+        copy.start()
+
+    def product(level, core, at, size):
+        left = jnp.concatenate([raw[b, level * G + core] for b in range(batches)], axis=0)
+        return contract(left, w_qkv[at : at + size, :], (1, 1))
+
+    def chip_copy(level):
+        return remote(swap.at[level], swapped.at[level], cs.at[level], cr.at[level], sibling)
+
+    def give(level):
+        for at in range(0, width, 512):
+            swap[level, :, at : at + 512] = product(level, 1 - d, at, 512).astype(bf16)
+        chip_copy(level).start()
+
+    def take(level):
+        chip_copy(level).wait_recv()
+        for at in range(0, width, 512):
+            part = product(level, d, at, 512) + swapped[level, :, at : at + 512].astype(f32)
+            own[level, :, at : at + 512] = part.astype(bf16)
+
+    def hop(way, level, b):
+        there = c + 1 if way == 0 else c - 1
+        to = level if way == 0 else level + (C - level) * ((C - 1 - (there - level)) // (C - 1))
+        return remote(
+            own.at[level, pl.ds(b * run, run)],
+            passed.at[to, pl.ds(b * run, run)],
+            zs.at[way, level, b],
+            zr.at[to, b],
+            (e, there, d),
+        )
+
+    def arrival(entry, b):
+        part = passed.at[entry, pl.ds(b * run, run)]
+        return remote(part, part, zs.at[0, 0, b], zr.at[entry, b], sibling)
+
+    def send(way, level, last):
+        for b in range(batches):
+
+            @pl.when(last)
+            def _():
+                arrival(level, b).wait_recv()
+                piece = pl.ds(b * run, run)
+                own[level, piece] = (
+                    own[level, piece].astype(f32) + passed[level, piece].astype(f32)
+                ).astype(bf16)
+
+            hop(way, level, b).start()
+
+    order = [C - 1, 0] + list(range(C - 2, 0, -1))
+    for level in order:
+        give(level)
+
+    def plane_copy(item):
+        plane = lax.rem(e + 1 + item, E)
+        return remote(
+            parts.at[item],
+            plane_parts.at[item],
+            qs.at[item],
+            qr.at[item],
+            (plane, c, d),
+        )
+
+    raw_flat = raw[...].reshape(-1, columns)
+
+    def weights(item):
+        token_copy(item).wait()
+        for at in range(0, columns, 256):
+            size = min(256, columns - at)
+            parts[item, :, at : at + size] = contract(
+                tokens[item % 2], raw_flat[:, at : at + size], (0, 0)
+            ).astype(bf16)
+        if item + 2 < E:
+            token_copy(item + 2).start()
+        if item < E - 1:
+            plane_copy(item).start()
+
+    mirror = C - 1 - c
+    items = list(range(E))
+    for level in order:
+        take(level)
+        if level == 0:
+            @pl.when(c == 0)
+            def _():
+                send(0, C - 1, False)
+
+            @pl.when(c == C - 1)
+            def _():
+                send(1, 0, False)
+
+            weights(items.pop(0))
+    weights(items.pop(0))
+    for turn in range(1, C - 1):
+
+        @pl.when(c <= turn)
+        def _():
+            send(0, C - 1 - (turn - c), c > 0)
+
+        @pl.when(mirror <= turn)
+        def _():
+            send(1, turn - mirror, mirror > 0)
+
+        if items:
+            weights(items.pop(0))
+    while items:
+        weights(items.pop(0))
+    for item in range(E - 1):
+        plane_copy(item).wait_recv()
+    for at in range(0, block, 128):
+        piece = pl.ds(at, min(128, block - at))
+        total = parts[E - 1, piece].astype(f32)
+        for item in range(E - 1):
+            total = total + plane_parts[item, piece].astype(f32)
+        sum_qkv[piece] = total.astype(bf16)
+    share = block // (C * G)
+
+    def row_copy(offset, index, device):
+        return remote(
+            sum_qkv.at[pl.ds(pl.multiple_of(index * share, share), share)],
+            out_qkv.at[me],
+            os.at[offset],
+            orr.at[offset],
+            device,
+        )
+
+    def small_copy(offset, index, device):
+        return remote(
+            small_sum.at[pl.ds(pl.multiple_of(index * share, share), share)],
+            out_small.at[me],
+            fs.at[offset],
+            fr.at[offset],
+            device,
+        )
+
+    for copy in small_copies:
+        copy.wait_recv()
+    total = small[e]
+    for i in range(1, E):
+        total = total + small_parts[i]
+    small_sum[...] = total
+    for offset, index, device in peers:
+        small_copy(offset, index, device).start()
+        row_copy(offset, index, device).start()
+    out_small[me] = small_sum[pl.ds(pl.multiple_of(me * share, share), share)]
+    out_qkv[me] = sum_qkv[pl.ds(pl.multiple_of(me * share, share), share)]
+
+    def arrived(entry):
+        for b in range(batches):
+            arrival(entry, b).wait_recv()
+
+    @pl.when(c > 0)
+    def _():
+        arrived(c)
+
+    @pl.when(c < C - 1)
+    def _():
+        arrived(C)
+
+    for at in range(0, width, 512):
+        first[:, at : at + 512] = own[c, :, at : at + 512].astype(f32)
+
+    @pl.when(c > 0)
+    def _():
+        for at in range(0, width, 512):
+            first[:, at : at + 512] += passed[c, :, at : at + 512].astype(f32)
+
+    @pl.when(c < C - 1)
+    def _():
+        for at in range(0, width, 512):
+            first[:, at : at + 512] += passed[C, :, at : at + 512].astype(f32)
+
+    for level in range(C):
+        chip_copy(level).wait_send()
+        for b in range(batches):
+
+            @pl.when(level > c)
+            def _():
+                hop(0, level, b).wait_send()
+
+            @pl.when(level < c)
+            def _():
+                hop(1, level, b).wait_send()
+
+    for item in range(E - 1):
+        plane_copy(item).wait_send()
+    for copy in small_copies:
+        copy.wait_send()
+    for offset, index, device in peers:
+        row_copy(offset, index, device).wait()
+        small_copy(offset, index, device).wait()
+
+
+def finish(E, C, G, raw, w_qkv, normed, small, collective, name):
+    batches, count, run, columns = raw.shape
+    width = w_qkv.shape[0]
+    every = normed.shape[0]
+    rows = batches * run
+    block = width // E
+    share = block // count
+    lanes = small.shape[2]
+    by_level = pltpu.VMEM((C, rows, width), bf16)
+    return call(
+        functools.partial(finish_kernel, E, C, G),
+        (raw, w_qkv, normed, small),
+        (
+            jax.ShapeDtypeStruct((rows, width), f32),
+            jax.ShapeDtypeStruct((count, share, columns), bf16),
+            jax.ShapeDtypeStruct((count, share, lanes), f32),
+        ),
+        [VMEM, VMEM, ANY, VMEM],
+        (VMEM, VMEM, VMEM),
+        [
+            pltpu.VMEM((E, block, lanes), f32),
+            pltpu.VMEM((block, lanes), f32),
+            by_level,
+            by_level,
+            by_level,
+            pltpu.VMEM((C + 1, rows, width), bf16),
+            pltpu.VMEM((2, every, block), bf16),
+            pltpu.VMEM((E, block, columns), bf16),
+            pltpu.VMEM((E, block, columns), bf16),
+            pltpu.VMEM((block, columns), bf16),
+            DMA((C,)),
+            DMA((C,)),
+            DMA((2, C, batches)),
+            DMA((C + 1, batches)),
+            DMA((2,)),
+            DMA((E,)),
+            DMA((E,)),
+            DMA((count,)),
+            DMA((count,)),
+            DMA((E,)),
+            DMA((E,)),
+            DMA((count,)),
+            DMA((count,)),
+        ],
+        collective,
+        name,
+        vmem=60,
     )
 
 
@@ -1071,17 +1483,19 @@
     small = jnp.concatenate([norm_gains, router], axis=1)
     small = jnp.pad(small, ((0, 0), (0, small_width - small.shape[1])))
     pieces = [w.reshape(rows, count, size) for w in (w_query, w_key, w_value)]
-    pieces.append(jnp.broadcast_to(small[:, None, :], (rows, count, small_width)))
     weights = jnp.swapaxes(jnp.concatenate(pieces, axis=2), 0, 1)
-    full_output = lax.all_gather(w_output, ALL_AXES, axis=0, tiled=True)
     places = slot_table(routes, experts).reshape(batches, E, C, run)
     by_level = jnp.transpose(places, (2, 0, 1, 3))
     by_expert = jnp.transpose(places, (1, 2, 0, 3))
-    column, gathered, ids, slots = start(E, C, G, tokens, weights, block_ids, by_level)
+    column, w_qkv, small, full_output, ids, slots = start(
+        E, C, G, tokens, weights, small, w_output, block_ids, by_level
+    )
     ids = jnp.swapaxes(ids, 0, 1).reshape(batches, length)
-    w_qkv = gathered[:, : 3 * size]
-    gains = gathered[:, 3 * size : 3 * size + 4].astype(f32)
-    full_router = gathered[:, 3 * size + 4 : 3 * size + 4 + experts]
+    w_qkv = w_qkv.reshape(width, 3 * size)
+    small = small.reshape(width, small_width)
+    full_output = full_output.reshape(width, width)
+    gains = small[:, :4].astype(f32)
+    full_router = small[:, 4 : 4 + experts]
     head_gains = lax.dynamic_slice(gains, (me * size, 0), (size, 4))
 
     column = column.reshape(every, width).astype(f32)
@@ -1130,11 +1544,6 @@
     x, pair_grad, act, gate_pre_grad, up_pre_grad = (
         rows.reshape(slot_count, -1) for rows in (x, pair_grad, act, gate_pre_grad, up_pre_grad)
     )
-    share = functools.partial(lax.psum_scatter, axis_name="dp", tiled=True)
-    grad_gate = share(contract(x, gate_pre_grad, (0, 0)).astype(bf16), scatter_dimension=1)
-    grad_up = share(contract(x, up_pre_grad, (0, 0)).astype(bf16), scatter_dimension=1)
-    grad_down = share(contract(act, pair_grad, (0, 0)).astype(bf16), scatter_dimension=0)
-
     upstream = cotangent.reshape(own, width).astype(f32)
     mixture = jnp.sum(mixture.astype(f32), axis=0).reshape(own, width)
     activations = (resid + mixture).astype(bf16).reshape(tokens.shape)
@@ -1150,7 +1559,25 @@
     attn_grad = resid_grad.astype(bf16)
     mixed_grad = contract(attn_grad, full_output, (1, 1)).astype(bf16)
 
-    mixed_grad = to_heads(E, C, G, mixed_grad.reshape(batches, run, width), 6, "mixed_grad_heads")
+    mixed_grad, grad_proj, *expert_grads = middle(
+        E,
+        C,
+        G,
+        mixed_grad.reshape(batches, run, width),
+        jnp.swapaxes(mixed_low, 0, 1).reshape(E, C, G, rows, own),
+        attn_grad,
+        x,
+        pair_grad,
+        gate_pre_grad,
+        up_pre_grad,
+        act,
+        6,
+        "middle",
+    )
+    grad_gate, grad_up, grad_down = (
+        (mine + other.astype(f32))[None] for mine, other in zip(expert_grads[:3], expert_grads[3:])
+    )
+    grad_proj = jnp.sum(grad_proj.astype(f32), axis=0)
     query_grad, key_grad, value_grad = (
         grad.reshape(every, size)
         for grad in attend_back(
@@ -1168,55 +1595,54 @@
         ],
         axis=1,
     )
-    first_part = contract(raw_grads, w_qkv, (1, 1)).astype(bf16)
-    first_grad = column_scatter(
-        E, C, G, first_part.reshape(batches, C, G, run, width), 8, "first_grad"
-    )
-    first_grad = jnp.sum(first_grad.astype(f32), axis=0).reshape(own, width)
+    gain_heads = jnp.stack(
+        [jnp.sum(query_grad * query_hat, axis=0), jnp.sum(key_grad * key_hat, axis=0)], axis=1
+    )
+    gain_heads = lax.dynamic_update_slice(
+        jnp.zeros((width, 2), f32), gain_heads, (me * size, 0)
+    )
+    sums = jnp.concatenate(
+        [gain_heads, gain_second[:, None], contract(second_low, logit_grad, (0, 0))], axis=1
+    )
+    sums = jnp.pad(sums, ((0, 0), (0, small_width - sums.shape[1])))
+    first_grad, grad_qkv, sums = finish(
+        E,
+        C,
+        G,
+        raw_grads.reshape(batches, count, run, 3 * size),
+        w_qkv,
+        normed,
+        sums.reshape(E, width // E, small_width),
+        8,
+        "finish",
+    )
+    sums = jnp.sum(sums, axis=0)
     first_factor = rms_factor(inputs)
     first_hat = inputs * first_factor
-    gain_first = jnp.sum(first_grad * first_hat, axis=0)
     input_grad = resid_grad + norm_back(first_grad * gains[:, 0], first_hat, first_factor)
 
-    grad_qkv = contract(normed, raw_grads, (0, 0)).astype(bf16)
-    grad_proj = contract(mixed_low, attn_grad, (0, 0)).astype(bf16)
-    grad_proj = jnp.transpose(grad_proj.reshape(E, C, G, rows, width), (1, 2, 0, 3, 4))
-    grad_qkv, grad_proj = weight_scatter(
-        E, C, G, grad_qkv.reshape(E, count, rows, 3 * size), grad_proj, 9, "weight_grads"
-    )
     grad_qkv = jnp.swapaxes(grad_qkv.astype(f32), 0, 1)
     grad_query, grad_key, grad_value = (
         grad_qkv[:, :, i * size : (i + 1) * size].reshape(rows, width) for i in range(3)
     )
-    grad_proj = jnp.sum(grad_proj.astype(f32), axis=0)
-    gain_heads = jnp.stack(
-        [jnp.sum(query_grad * query_hat, axis=0), jnp.sum(key_grad * key_hat, axis=0)], axis=1
-    )
-    gain_heads = lax.dynamic_update_slice(
-        jnp.zeros((width, 2), f32), gain_heads, (me * size, 0)
-    )
-    sums = jnp.concatenate(
-        [
-            gain_first[:, None],
-            gain_heads,
-            gain_second[:, None],
-            contract(second_low, logit_grad, (0, 0)),
-        ],
-        axis=1,
-    )
-    sums = lax.psum_scatter(sums, ALL_AXES, scatter_dimension=0, tiled=True)
+    gain_first = sum(
+        jnp.sum(w.astype(f32) * grad, axis=1)
+        for w, grad in ((w_query, grad_query), (w_key, grad_key), (w_value, grad_value))
+    )
+    gain_first = gain_first / norm_gains[:, 0].astype(f32)
+    grad_gains = jnp.concatenate([gain_first[:, None], sums[:, :3]], axis=1)
     return (
         activations,
         input_grad.reshape(tokens.shape),
-        sums[:, :4],
+        grad_gains,
         grad_query,
         grad_key,
         grad_value,
         grad_proj,
-        sums[:, 4:],
-        grad_gate.astype(f32)[None],
-        grad_up.astype(f32)[None],
-        grad_down.astype(f32)[None],
+        sums[:, 3 : 3 + experts],
+        grad_gate,
+        grad_up,
+        grad_down,
     )
 
 

time: 1080 us -> 947 us (0.88)
  matrix products: 92.7 us -> 22.6 us
  Pallas kernels: 873 us -> 812 us
  other arithmetic: 54.1 us -> 68.8 us
  between operations: 14.7 us -> 1.92 us
    dot_general x9 -> x3, matrix products: 74.2 us -> 4.7 us  [contract(): lax.dot_general(left, right, ((axes[:1], axes[1:]), ((), ())), preferred_...]
    pallas_call x8 -> x7, Pallas kernels: 843 us -> 782 us  [call(): pl.pallas_call(kernel, out_shape=out_shapes, in_specs=in_specs, out_specs...]
    unnamed x77 -> x128, local copies, waits for them, and re-layouts: 11.5 us -> 24.3 us
  transfers between devices with their start and end apart: 5 -> 0, of which waited for: 0 -> 0; matrix products, arithmetic and copies ran while one was open for 11% -> 0% of each run, Pallas kernels for 29% -> 0%
where the time goes in v3:
time: 947 us; the launch traced here: 937 us
  Pallas kernels  812 us (86%)
  other arithmetic  68.8 us (7%)
  local copies, waits for them, and re-layouts  31.3 us (3%)
  matrix products  22.6 us (2%)
    pallas_call x7, Pallas kernels, call(): pl.pallas_call(kernel, out_shape=out_shapes, in_specs=in_specs, out_specs...  782 us
    unnamed x128, local copies, waits for them, and re-layouts  24.3 us

profile of v3, /device:TPU:1, one launch (start us, length us, event | category | flops | bytes accessed | tf_op | source)
XLA Modules:
  0.0 936.8 jit_solution(2505370744416978003)
XLA Ops:
  7.5 119.8 %start.1 = (bf16[2,8,128,2048]{3,2,1,0:T(8,128)(2,1)S(1)}, bf16[4,8,64,768]{3,2,1,0:T(8,128)(2,1)S(1)}, bf16[4,8,64,128]{3,2,1,0:T(8,128)(2,1)S(1)}, bf16[4,4,2,...) custom-call(bf16[2,128,2048]{2,1,0:T(8,128)(2,1)S(1)} %copy-done.1, ...), custom_call_target="tpu_custom_call" | custom-call | tf_op jit(solution)/shard_map/start/pallas_call | solution.py:25
  129.6 3.2 copy-done.15
  136.7 8.6 fusion.1.normed
  145.3 8.5 multiply_convert_fusion
  153.8 10.0 %fusion.30 = f32[2048,768]{1,0:T(8,128)S(1)} fusion(bf16[2048,2048]{1,0:T(8,128)(2,1)} %bitcast.209, bf16[2048,768]{1,0:T(8,128)(2,1)} %bitcast.194), kind=kOutput, calls=%fused_computation.102 | convolution fusion | flops 6442450944 | bytes 17825792 | tf_op jit(solution)/shard_map/dot_general | solution.py:1503
  166.6 6.3 squares.1
  174.8 2.6 multiply_convert_fusion.4
  177.4 12.0 %attend.1 = (bf16[2,1024,256]{2,1,0:T(8,128)(2,1)S(1)}, f32[2,2,1024,1]{3,2,1,0:T(8,128)}) custom-call(bf16[2,1024,256]{2,1,0:T(8,128)(2,1)S(1)} %bitcast.187, bf16[2,1024,256]{2,1,0:T(8,128)(2,1)S(1)} %bitcast.185, bf16[2,1024,256]{2,1,0:T(8,128)(2,1)S(1)} %bitcast.183, s32[2,1024,1]{2,1,0:T(8,128)S(1)} %copy.73.row_ids, s32[2,1,1024]{2,1,0:T(1,128)S(1)} %bitcast.198), custom_call_target="tpu_custom_call" | custom-call | tf_op jit(solution)/shard_map/attend/pallas_call | solution.py:1399
  189.4 24.5 %mixed_rows.1 = bf16[2,128,2048]{2,1,0:T(8,128)(2,1)S(1)} custom-call(bf16[2,8,128,256]{3,2,1,0:T(8,128)(2,1)S(1)} %bitcast.196), custom_call_target="tpu_custom_call" | custom-call | tf_op jit(solution)/shard_map/mixed_rows/pallas_call | solution.py:25
  217.1 6.2 multiply_reduce_fusion.7
  226.1 440.8 %experts.1 = (bf16[4,2,128,2048]{3,2,1,0:T(8,128)(2,1)}, bf16[4,2,128,2048]{3,2,1,0:T(8,128)(2,1)}, bf16[4,2,4,64,2048]{4,3,2,1,0:T(8,128)(2,1)}, bf16[4,2,4,64,...) custom-call(bf16[2,128,2048]{2,1,0:T(8,128)(2,1)} %bitcast.206, ...), custom_call_target="tpu_custom_call" | custom-call | tf_op jit(solution)/shard_map/experts/pallas_call | solution.py:25
  666.9 4.7 convert_reduce_fusion.1
  677.1 3.4 convolution_convert_fusion
  680.5 75.5 %middle.1 = (bf16[2,8,128,256]{3,2,1,0:T(8,128)(2,1)}, bf16[4,64,2048]{2,1,0:T(8,128)(2,1)}, f32[2048,512]{1,0:T(8,128)}, f32[2048,512]{1,0:T(8,128)}, f32[512,2...) custom-call(bf16[2,128,2048]{2,1,0:T(8,128)(2,1)} %bitcast.229, ...), custom_call_target="tpu_custom_call" | custom-call | tf_op jit(solution)/shard_map/middle/pallas_call | solution.py:25
  759.6 18.6 %attend_back.1 = (f32[2,1024,256]{2,1,0:T(8,128)}, f32[2,1024,256]{2,1,0:T(8,128)}, f32[2,1024,256]{2,1,0:T(8,128)}) custom-call(bf16[2,1024,256]{2,1,0:T(8,128)(2,1)S(1)} %bitcast.188, bf16[2,1024,256]{2,1,0:T(8,128)(2,1)S(1)} %bitcast.186, bf16[2,1024,256]{2,1,0:T(8,128)(2,1)S(1)} %bitcast.184, bf16[2,1024,256]{2,1,0:T(8,128)(2,1)S(1)} %bitcast.197, ...), custom_call_target="tpu_custom_call" | custom-call | tf_op jit(solution)/shard_map/attend_back/pallas_call | solution.py:1418
  778.3 2.8 convert_element_type.136
  781.1 3.7 fusion.3
  785.7 11.9 %norm_means.1 = f32[8,2,2048]{2,1,0:T(2,128)S(1)} custom-call(f32[2,2048]{1,0:T(2,128)S(1)} %pad_maximum_fusion.4.part), custom_call_target="tpu_custom_call" | custom-call | tf_op jit(solution)/shard_map/norm_means/pallas_call | solution.py:25
  799.0 4.7 multiply_convert_fusion.2
  807.9 102.9 %finish.1 = (f32[256,2048]{1,0:T(8,128)}, bf16[8,64,768]{2,1,0:T(8,128)(2,1)}, f32[8,64,128]{2,1,0:T(8,128)}) custom-call(bf16[2,8,128,768]{3,2,1,0:T(8,128)(2,1)} %bitcast.207, bf16[2048,768]{1,0:T(8,128)(2,1)} %bitcast.195, bf16[2048,2048]{1,0:T(8,128)(2,1)} %fusion.1.normed, f32[4,512,128]{2,1,0:T(8,128)} %bitcast.220), custom_call_target="tpu_custom_call" | custom-call | tf_op jit(solution)/shard_map/finish/pallas_call | solution.py:25
  913.3 5.1 multiply_add_fusion
  925.0 2.9 add_bitcast_fusion.2
  929.4 2.9 add_bitcast_fusion.1
  933.8 2.7 add_bitcast_fusion
  (194 shorter events, 50.9 us)
Async XLA Ops:
  0.6 6.7 copy-start.42
  0.7 6.7 copy-start.41
  0.7 6.8 copy-start.1
  0.7 6.8 copy-start.12
  0.7 6.8 copy-start.14
  132.8 12.5 %copy-start.6 = (bf16[4,8,64,128]{3,2,1,0:T(8,128)(2,1)}, bf16[4,8,64,128]{3,2,1,0:T(8,128)(2,1)S(1)}, u32[]{:S(2)}) copy-start(bf16[4,8,64,128]{3,2,1,0:T(8,128)(2,1)S(1)} %get-tuple-element.42) | copy-start | bytes 1572868
  136.3 38.4 %copy-start.52 = (f32[256,1]{0,1:T(1,128)}, f32[256,1]{0,1:T(1,128)S(1)}, u32[]{:S(2)}) copy-start(f32[256,1]{0,1:T(1,128)S(1)} %get-tuple-element.118) | copy-start | bytes 3076
  136.3 38.4 %copy-start.54 = (f32[256,1]{0,1:T(1,128)}, f32[256,1]{0,1:T(1,128)S(1)}, u32[]{:S(2)}) copy-start(f32[256,1]{0,1:T(1,128)S(1)} %get-tuple-element.119) | copy-start | bytes 3076
  173.1 4.3 copy-start.45
  173.1 4.3 copy-start.47
  177.4 12.0 %copy-start.2 = (bf16[2048,256]{1,0:T(8,128)(2,1)}, bf16[2048,256]{1,0:T(8,128)(2,1)S(1)}, u32[]{:S(2)}) copy-start(bf16[2048,256]{1,0:T(8,128)(2,1)S(1)} %get-tuple-element.105) | copy-start | bytes 3145732
  177.4 12.0 %copy-start.4 = (bf16[2048,256]{1,0:T(8,128)(2,1)}, bf16[2048,256]{1,0:T(8,128)(2,1)S(1)}, u32[]{:S(2)}) copy-start(bf16[2048,256]{1,0:T(8,128)(2,1)S(1)} %get-tuple-element.106) | copy-start | bytes 3145732
  223.3 451.1 %copy-start.50 = (f32[256]{0:T(256)}, f32[256]{0:T(256)S(1)}, u32[]{:S(2)}) copy-start(f32[256]{0:T(256)S(1)} %add_rsqrt_fusion.2) | copy-start | bytes 3076
  666.9 4.7 copy-start.49
  666.9 4.7 copy-start.23
  666.9 5.0 copy-start.27
  671.9 4.6 slice-start
  799.0 4.7 copy-start.31
  807.9 102.9 %copy-start.56 = (f32[256]{0:T(256)S(1)}, f32[256]{0:T(256)}, u32[]{:S(2)}) copy-start(f32[256]{0:T(256)} %rsqrt_bitcast_fusion) | copy-start | bytes 3076
  807.9 105.2 %copy-start.21 = (f32[256,2048]{1,0:T(8,128)S(1)}, f32[256,2048]{1,0:T(8,128)}, u32[]{:S(2)}) copy-start(f32[256,2048]{1,0:T(8,128)} %copy-done.20) | copy-start | bytes 6291460
  921.9 5.9 copy-start.37
  923.1 4.8 copy-start.38
  925.0 4.4 copy-start.34
  929.4 4.4 copy-start.33
  (38 other events, 83.1 us)

commit v4 on v3

--- a/solution.py
+++ b/solution.py
@@ -329,41 +329,6 @@
     return jnp.sum(parts, axis=0)
 
 
-def to_tokens_kernel(E, C, G, heads, rows, ss, rs, ls):
-    me, peers = column_peers(E, C, G)
-    batches = rows.shape[0]
-    size = heads.shape[3]
-    meet([device for _, _, device in peers])
-    mine = pl.ds(pl.multiple_of(me * size, size), size)
-    copies = []
-    for b in range(batches):
-        for offset, index, device in peers:
-            copies.append(
-                remote(
-                    heads.at[b, index], rows.at[b, :, mine], ss.at[b, offset], rs.at[b, offset], device
-                )
-            )
-        copies.append(pltpu.make_async_copy(heads.at[b, me], rows.at[b, :, mine], ls.at[b]))
-    for copy in copies:
-        copy.start()
-    for copy in copies:
-        copy.wait()
-
-
-def to_tokens(E, C, G, heads, collective, name):
-    batches, count, run, size = heads.shape
-    return call(
-        functools.partial(to_tokens_kernel, E, C, G),
-        (heads,),
-        jax.ShapeDtypeStruct((batches, run, count * size), heads.dtype),
-        [ANY],
-        ANY,
-        [DMA((batches, C * G)), DMA((batches, C * G)), DMA((batches,))],
-        collective,
-        name,
-    )
-
-
 def choose(slots, count):
     cells = lax.broadcasted_iota(jnp.int32, (count, slots.shape[1]), 0).astype(f32)
     return jnp.concatenate(
@@ -371,11 +336,404 @@
     )
 
 
+class Flow:
+    def __init__(self, E, C, rows, slots, landed, packed, target, own, zs, zr, xs, xr, stay):
+        self.E, self.C, self.rows, self.slots = E, C, rows, slots
+        self.landed, self.packed, self.target = landed, packed, target
+        self.sems = own, zs, zr, xs, xr, stay
+        self.e, self.c, self.d = position()
+        self.batches = rows.shape[0]
+        self.cap, self.width = target.shape[3:]
+        self.kept = packed.shape[0]
+        self.chunks = self.batches * C
+
+    def level_entry(self, far):
+        high = 2 * self.c // self.C
+        return high * far + (1 - high) * lax.rem(self.C - far, self.C)
+
+    def own(self, b):
+        return pltpu.make_async_copy(self.rows.at[b], self.landed.at[0, b], self.sems[0].at[b])
+
+    def hop(self, b, i, way):
+        there = i + 1 if way == 0 else lax.rem(i + self.C - 1, self.C)
+        level = lax.rem(self.c + (1 if way == 0 else self.C - 1), self.C)
+        return remote(
+            self.landed.at[i, b],
+            self.landed.at[there, b],
+            self.sems[1].at[way, i, b],
+            self.sems[2].at[there, b],
+            (self.e, level, self.d),
+        )
+
+    def arrival(self, b, i):
+        entry = self.landed.at[i, b]
+        return remote(
+            entry,
+            entry,
+            self.sems[1].at[0, i, b],
+            self.sems[2].at[i, b],
+            (self.e, self.c, 1 - self.d),
+        )
+
+    def onward(self, i, way):
+        if way == 0:
+            return jnp.logical_and(i <= self.c, self.c < self.C - 1)
+        return jnp.logical_and(lax.rem(self.C - i, self.C) + self.c < self.C, self.c > 0)
+
+    def begin(self):
+        for b in range(self.batches):
+            self.own(b).start()
+        for b in range(self.batches):
+            self.own(b).wait()
+            for way in range(2):
+
+                @pl.when(self.onward(0, way))
+                def _():
+                    self.hop(b, 0, way).start()
+
+    def relay(self, far, b):
+        for way in range(2):
+            i = far if way == 0 else self.C - far
+
+            @pl.when((far <= self.c) if way == 0 else (far + self.c < self.C))
+            def _():
+                self.arrival(b, i).wait_recv()
+
+                @pl.when(self.onward(i, way))
+                def _():
+                    self.hop(b, i, way).start()
+
+    def hops_sent(self, b, i):
+        for way in range(2):
+
+            @pl.when(self.onward(i, way))
+            def _():
+                self.hop(b, i, way).wait_send()
+
+    def across(self, n, b, i, k):
+        plane = lax.rem(self.e + k, self.E)
+        return remote(
+            self.packed.at[lax.rem(n, self.kept), plane],
+            self.target.at[i, b, k],
+            self.sems[3].at[i, b, k],
+            self.sems[4].at[i, b, k],
+            (plane, self.c, self.d),
+        )
+
+    def stay(self, n, b, i):
+        return pltpu.make_async_copy(
+            self.packed.at[lax.rem(n, self.kept), self.e],
+            self.target.at[i, b, 0],
+            self.sems[5].at[i, b],
+        )
+
+    def compact(self, n, b, i):
+        place = lax.rem(n, self.kept)
+        picks = choose(self.slots[i, b], self.cap)
+        for at in range(0, self.width, 512):
+            part = jnp.dot(
+                picks, self.landed[i, b, :, at : at + 512], preferred_element_type=f32
+            ).astype(bf16)
+            self.packed[place, :, :, at : at + 512] = part.reshape(self.E, self.cap, 512)
+        for k in range(1, self.E):
+            self.across(n, b, i, k).start()
+        self.stay(n, b, i).start()
+
+    def crossed(self, n, b, i):
+        for k in range(1, self.E):
+            self.across(n, b, i, k).wait_send()
+
+    def arrived(self, n, b, i):
+        for k in range(1, self.E):
+            self.across(n, b, i, k).wait_recv()
+
+    @staticmethod
+    def scratch(E, C, batches, run, width, cap, kept):
+        return [
+            pltpu.VMEM((C, batches, run, width), bf16),
+            pltpu.VMEM((kept, E, cap, width), bf16),
+            DMA((batches,)),
+            DMA((2, C, batches)),
+            DMA((C, batches)),
+            DMA((C, batches, E)),
+            DMA((C, batches, E)),
+            DMA((C, batches)),
+        ]
+
+
+def forward_kernel(
+    E,
+    C,
+    G,
+    column,
+    gain,
+    head_gains,
+    w_qkv,
+    row_ids,
+    key_ids,
+    slots,
+    upstream,
+    normed,
+    queries,
+    keys,
+    values,
+    query_hat,
+    key_hat,
+    log_total,
+    factors,
+    mixed,
+    u_out,
+    raw,
+    low,
+    squares,
+    parts,
+    heads,
+    landed,
+    packed,
+    own,
+    zs,
+    zr,
+    xs,
+    xr,
+    stay,
+    raw_sem,
+    low_sem,
+    ss,
+    sr,
+    ms,
+    mr,
+    ml,
+):
+    me, peers = column_peers(E, C, G)
+    planes = plane_peers(E)
+    every, width = column.shape
+    batches, length, size = heads.shape
+    run = length // (C * G)
+    block = raw.shape[1]
+    blocks = every // block
+    scale = HEAD**-0.5
+    meet([device for _, _, device in peers] + [device for _, _, device in planes])
+    flow = Flow(E, C, upstream, slots, landed, packed, u_out, own, zs, zr, xs, xr, stay)
+
+    def load(j):
+        at = pl.multiple_of(j * block, block)
+        place = lax.rem(j, 2)
+        return pltpu.make_async_copy(column.at[pl.ds(at, block)], raw.at[place], raw_sem.at[place])
+
+    def store(j):
+        at = pl.multiple_of(j * block, block)
+        place = lax.rem(j, 2)
+        return pltpu.make_async_copy(low.at[place], normed.at[pl.ds(at, block)], low_sem.at[place])
+
+    def chunk_of(n):
+        return n % batches, flow.level_entry(n // batches)
+
+    chunk = iter(range(flow.chunks))
+
+    def carry_on(count):
+        for _ in range(count):
+            n = next(chunk, None)
+            if n is None:
+                return
+            if n >= flow.kept:
+                before = n - flow.kept, *chunk_of(n - flow.kept)
+                flow.crossed(*before)
+                flow.stay(*before).wait()
+            if n >= batches:
+                flow.relay(n // batches, n % batches)
+            flow.compact(n, *chunk_of(n))
+
+    load(0).start()
+    load(1).start()
+    flow.begin()
+    carry_on(batches)
+    ones = jnp.ones((8, size), f32)
+
+    def project(j, carry):
+        place = lax.rem(j, 2)
+        rows = pl.ds(pl.multiple_of(j * block, block), block)
+        load(j).wait()
+
+        @pl.when(j >= 2)
+        def _():
+            store(j - 2).wait()
+
+        total = jnp.zeros((block, 1), f32)
+        for at in range(0, width, 512):
+            part = raw[place, :, at : at + 512].astype(f32)
+            total += jnp.sum(part * part, axis=1, keepdims=True)
+        factor = lax.rsqrt(total / width + EPSILON)
+        for at in range(0, width, 512):
+            part = raw[place, :, at : at + 512].astype(f32) * factor
+            low[place, :, at : at + 512] = (part * gain[:, at : at + 512]).astype(bf16)
+        store(j).start()
+
+        @pl.when(j + 2 < blocks)
+        def _():
+            load(j + 2).start()
+
+        for kind in range(3):
+            part = jnp.dot(
+                low[place],
+                w_qkv[:, kind * size : (kind + 1) * size],
+                preferred_element_type=f32,
+            )
+            if kind == 2:
+                values[rows] = part.astype(bf16)
+            else:
+                (query_hat, key_hat)[kind][rows] = part
+                sums = lax.dot_general(
+                    ones,
+                    part * part,
+                    (((1,), (1,)), ((), ())),
+                    precision=lax.Precision.HIGHEST,
+                    preferred_element_type=f32,
+                )
+                squares[kind, :, rows] = sums[:1]
+        return carry
+
+    half = blocks // 2
+    lax.fori_loop(0, half, project, 0)
+    carry_on(1)
+    lax.fori_loop(half, blocks, project, 0)
+    shares = [
+        remote(squares, parts.at[me], ss.at[offset], sr.at[offset], device)
+        for offset, _, device in peers
+    ]
+    for copy in shares:
+        copy.start()
+    parts[me] = squares[...]
+    carry_on(1)
+    for copy in shares:
+        copy.wait_recv()
+    total = parts[0]
+    for index in range(1, C * G):
+        total = total + parts[index]
+    factors[...] = lax.rsqrt(total / width + EPSILON)
+    rows_at = lax.broadcasted_iota(jnp.int32, (block, block), 0)
+    same = rows_at == lax.broadcasted_iota(jnp.int32, (block, block), 1)
+
+    def scaled(j, carry):
+        rows = pl.ds(pl.multiple_of(j * block, block), block)
+        for kind, (hat, out) in enumerate(((query_hat, queries), (key_hat, keys))):
+            factor = jnp.sum(jnp.where(same, factors[kind, :, rows], 0.0), axis=1, keepdims=True)
+            part = hat[rows] * factor
+            hat[rows] = part
+            out[rows] = (part * head_gains[kind : kind + 1]).astype(bf16)
+        return carry
+
+    lax.fori_loop(0, blocks, scaled, 0)
+    carry_on(1)
+
+    def mixed_copy(b, offset, index, device):
+        where = pl.ds(pl.multiple_of(me * size, size), size)
+        part = heads.at[b, pl.ds(pl.multiple_of(index * run, run), run)]
+        return remote(part, mixed.at[b, :, where], ms.at[b, offset], mr.at[b, offset], device)
+
+    def mixed_own(b):
+        where = pl.ds(pl.multiple_of(me * size, size), size)
+        part = heads.at[b, pl.ds(pl.multiple_of(me * run, run), run)]
+        return pltpu.make_async_copy(part, mixed.at[b, :, where], ml.at[b])
+
+    for b in range(batches):
+
+        def head(h, carry, b=b):
+            lanes = pl.ds(pl.multiple_of(h * HEAD, HEAD), HEAD)
+            for first, count, seen in query_blocks(length):
+                rows = pl.ds(b * length + first, count)
+                seen_rows = pl.ds(b * length, seen)
+                scores = contract(queries[rows, lanes], keys[seen_rows, lanes], (1, 1)) * scale
+                allowed = key_ids[b, :, :seen] <= row_ids[b, first : first + count]
+                scores = jnp.where(allowed, scores, MASKED)
+                peak = jnp.max(scores, axis=1, keepdims=True)
+                grown = jnp.exp(scores - peak)
+                total = jnp.sum(grown, axis=1, keepdims=True)
+                probs = (grown * (1.0 / total)).astype(bf16)
+                heads[b, first : first + count, lanes] = jnp.dot(
+                    probs, values[seen_rows, lanes], preferred_element_type=f32
+                ).astype(bf16)
+                log_total[b, h, first : first + count] = peak + jnp.log(total)
+            return carry
+
+        lax.fori_loop(0, size // HEAD, head, 0)
+        for offset, index, device in peers:
+            mixed_copy(b, offset, index, device).start()
+        mixed_own(b).start()
+        carry_on(1)
+    carry_on(flow.chunks)
+
+    for copy in shares:
+        copy.wait_send()
+    for j in (blocks - 2, blocks - 1):
+        store(j).wait()
+    for b in range(batches):
+        for offset, index, device in peers:
+            mixed_copy(b, offset, index, device).wait()
+        mixed_own(b).wait()
+
+    for n in range(flow.chunks):
+        b, i = chunk_of(n)
+        flow.hops_sent(b, i)
+        flow.arrived(n, b, i)
+        if n >= flow.chunks - flow.kept:
+            flow.crossed(n, b, i)
+            flow.stay(n, b, i).wait()
+
+
+def run_forward(E, C, G, column, gain, head_gains, w_qkv, ids, slots, upstream, cap, collective, name):
+    every, width = column.shape
+    batches, run = upstream.shape[:2]
+    count = C * G
+    length = count * run
+    size = width // count
+    block = min(256, every)
+    low = jax.ShapeDtypeStruct((every, size), bf16)
+    wide = jax.ShapeDtypeStruct((every, size), f32)
+    return call(
+        functools.partial(forward_kernel, E, C, G),
+        (column, gain, head_gains, w_qkv, ids[:, :, None], ids[:, None, :], slots, upstream),
+        (
+            jax.ShapeDtypeStruct((every, width), bf16),
+            low,
+            low,
+            low,
+            wide,
+            wide,
+            jax.ShapeDtypeStruct((batches, size // HEAD, length, 1), f32),
+            jax.ShapeDtypeStruct((2, 1, every), f32),
+            jax.ShapeDtypeStruct(upstream.shape, bf16),
+            jax.ShapeDtypeStruct((C, batches, E, cap, width), bf16),
+        ),
+        [ANY] + [VMEM] * 6 + [ANY],
+        (ANY,) + (VMEM,) * 7 + (ANY, ANY),
+        [
+            pltpu.VMEM((2, block, width), bf16),
+            pltpu.VMEM((2, block, width), bf16),
+            pltpu.VMEM((2, 1, every), f32),
+            pltpu.VMEM((count, 2, 1, every), f32),
+            pltpu.VMEM((batches, length, size), bf16),
+        ]
+        + Flow.scratch(E, C, batches, run, width, cap, 3)
+        + [
+            DMA((2,)),
+            DMA((2,)),
+            DMA((count,)),
+            DMA((count,)),
+            DMA((batches, count)),
+            DMA((batches, count)),
+            DMA((batches,)),
+        ],
+        collective,
+        name,
+        vmem=56,
+    )
+
+
 def experts_kernel(
     E,
     C,
     rows_x,
-    rows_u,
+    u_in,
     slots,
     gates,
     w_gate,
@@ -384,7 +742,6 @@
     out_y,
     out_b,
     x_out,
-    u_out,
     pair_out,
     act_out,
     gate_back_out,
@@ -394,6 +751,13 @@
     scalars,
     landed,
     packed,
+    own,
+    zs,
+    zr,
+    xs,
+    xr,
+    stay,
+    sums,
     returned,
     x,
     u,
@@ -406,12 +770,6 @@
     gr,
     ss,
     sr,
-    os,
-    zs,
-    zr,
-    xs,
-    xr,
-    ls,
     ys,
     yr,
     bs,
@@ -427,63 +785,21 @@
     units = w_gate.shape[1]
     chunks = batches * C
     total = E * cap
-    slots_kept, kept = packed.shape[1], sent.shape[1]
+    kept = sent.shape[1]
     lead, lag = 1, 2
     everyone = [(k, i) for k in range(E) for i in range(C) if k + i > 0]
     ahead = [(k, i, (lax.rem(e + k, E), lax.rem(c + i, C), d)) for k, i in everyone]
     behind = [(k, i, (lax.rem(e + E - k, E), lax.rem(c + C - i, C), d)) for k, i in everyone]
     meet([device for _, _, device in ahead])
-    sources, arrivals, outs = (rows_x, rows_u), (x_out, u_out), (out_y, out_b)
-
-    high = 2 * c // C
+    outs = out_y, out_b
+    flow = Flow(E, C, rows_x, slots, landed, packed, x_out, own, zs, zr, xs, xr, stay)
 
     def far_of(n):
         return lax.rem((n + batches - 1) // batches, C), lax.rem(n + batches - 1, batches)
 
     def chunk_of(n):
-        m, b = far_of(n)
-        return b, high * m + (1 - high) * lax.rem(C - m, C)
-
-    def hop(a, b, i, way):
-        there = i + 1 if way == 0 else lax.rem(i + C - 1, C)
-        level = lax.rem(c + 1, C) if way == 0 else lax.rem(c + C - 1, C)
-        return remote(
-            landed.at[a, i, b],
-            landed.at[a, there, b],
-            zs.at[way, a, i, b],
-            zr.at[a, there, b],
-            (e, level, d),
-        )
-
-    def arrival(a, b, i):
-        return remote(
-            landed.at[a, i, b], landed.at[a, i, b], zs.at[0, a, i, b], zr.at[a, i, b], (e, c, 1 - d)
-        )
-
-    def onward(i, way):
-        if way == 0:
-            return jnp.logical_and(i <= c, c < C - 1)
-        return jnp.logical_and(lax.rem(C - i, C) + c < C, c > 0)
-
-    def own(a, b):
-        return pltpu.make_async_copy(sources[a].at[b], landed.at[a, 0, b], os.at[a, b])
-
-    def across(a, n, k):
-        plane = lax.rem(e + k, E)
-        b, i = chunk_of(n)
-        return remote(
-            packed.at[a, lax.rem(n, slots_kept), plane],
-            arrivals[a].at[i, b, k],
-            xs.at[a, i, b, k],
-            xr.at[a, i, b, k],
-            (plane, c, d),
-        )
-
-    def stay(a, n):
-        b, i = chunk_of(n)
-        return pltpu.make_async_copy(
-            packed.at[a, lax.rem(n, slots_kept), e], arrivals[a].at[i, b, 0], ls.at[a, i, b]
-        )
+        far, b = far_of(n)
+        return b, flow.level_entry(far)
 
     def back(a, n, b, i, k):
         return remote(
@@ -501,7 +817,7 @@
 
     def up(a, b, i):
         return remote(
-            landed.at[a, i, b],
+            sums.at[a, i, b],
             outs[a].at[c, b],
             us.at[a, i, b],
             ur.at[a, i, b],
@@ -509,29 +825,18 @@
         )
 
     def keep(a, b):
-        return pltpu.make_async_copy(landed.at[a, 0, b], outs[a].at[c, b], ks.at[a, b])
+        return pltpu.make_async_copy(sums.at[a, 0, b], outs[a].at[c, b], ks.at[a, b])
 
     def load(a, b, i):
-        target = (x, u)[a]
-        return pltpu.make_async_copy(arrivals[a].at[i, b], target, loads.at[a])
+        source, target = ((x_out, x), (u_in, u))[a]
+        return pltpu.make_async_copy(source.at[i, b], target, loads.at[a])
 
     def store(j, b, i):
         source = (pair, act, gate_back, up_back)[j]
         target = (pair_out, act_out, gate_back_out, up_back_out)[j]
         return pltpu.make_async_copy(source, target.at[i, b], stores.at[j])
 
-    for b in range(batches):
-        for a in range(2):
-            own(a, b).start()
-    for b in range(batches):
-        for a in range(2):
-            own(a, b).wait()
-            for way in range(2):
-
-                @pl.when(onward(0, way))
-                def _():
-                    hop(a, b, 0, way).start()
-
+    flow.begin()
     small = [
         remote(gates.at[device[0], device[1]], table.at[k, i], gs.at[k, i], gr.at[k, i], device)
         for k, i, device in ahead
@@ -540,48 +845,19 @@
         copy.start()
     table[0, 0] = gates[e, c]
 
-    def relay(n):
-        far, b = far_of(n)
-        for a in range(2):
-            for way in range(2):
-                i = far if way == 0 else C - far
-
-                @pl.when((far <= c) if way == 0 else (far + c < C))
-                def _():
-                    arrival(a, b, i).wait_recv()
-
-                    @pl.when(onward(i, way))
-                    def _():
-                        hop(a, b, i, way).start()
-
     def compact(n):
-        b, i = chunk_of(n)
-        picks = choose(slots[i, b], cap)
-        place = lax.rem(n, slots_kept)
-
-        @pl.when(n >= slots_kept)
+        @pl.when(n >= flow.kept)
         def _():
-            for a in range(2):
-                for k in range(1, E):
-                    across(a, n - slots_kept, k).wait_send()
-
-        for a in range(2):
-            for at in range(0, width, 512):
-                part = jnp.dot(
-                    picks, landed[a, i, b, :, at : at + 512], preferred_element_type=f32
-                ).astype(bf16)
-                packed[a, place, :, :, at : at + 512] = part.reshape(E, cap, 512)
-            for k in range(1, E):
-                across(a, n, k).start()
-            stay(a, n).start()
+            flow.crossed(n - flow.kept, *chunk_of(n - flow.kept))
+
+        flow.compact(n, *chunk_of(n))
 
     def expert(n):
         b, i = chunk_of(n)
-        for a in range(2):
-            for k in range(1, E):
-                across(a, n, k).wait_recv()
-            stay(a, n).wait()
-            load(a, b, i).start()
+        load(1, b, i).start()
+        flow.arrived(n, b, i)
+        flow.stay(n, b, i).wait()
+        load(0, b, i).start()
 
         @pl.when(n > 0)
         def _():
@@ -654,15 +930,9 @@
             for k in range(1, E):
                 back(a, n, b, i, k).wait_recv()
             back_own(a, n, b, i).wait()
-            for way in range(2):
-
-                @pl.when(onward(i, way))
-                def _():
-                    hop(a, b, i, way).wait_send()
-
             for at in range(0, width, 512):
                 part = returned[a, i, b, :, :, at : at + 512].reshape(total, 512)
-                landed[a, i, b, :, at : at + 512] = contract(picks, part, (0, 0)).astype(bf16)
+                sums[a, i, b, :, at : at + 512] = contract(picks, part, (0, 0)).astype(bf16)
 
             @pl.when(i > 0)
             def _():
@@ -675,7 +945,7 @@
     def step(s, carry):
         @pl.when(jnp.logical_and(s > 0, s <= batches * (C - 1)))
         def _():
-            relay(s)
+            flow.relay(*far_of(s))
 
         @pl.when(s < chunks)
         def _():
@@ -708,12 +978,13 @@
 
     def finish(n, carry):
         b, i = chunk_of(n)
+        flow.hops_sent(b, i)
+
+        @pl.when(n >= chunks - flow.kept)
+        def _():
+            flow.crossed(n, b, i)
+
         for a in range(2):
-
-            @pl.when(n >= chunks - slots_kept)
-            def _():
-                for k in range(1, E):
-                    across(a, n, k).wait_send()
 
             @pl.when(n >= chunks - kept)
             def _():
@@ -735,7 +1006,7 @@
         copy.wait()
 
 
-def run_experts(E, C, rows_x, rows_u, slots, gates, w_gate, w_up, w_down, cap, collective, name):
+def run_experts(E, C, rows_x, u_in, slots, gates, w_gate, w_up, w_down, cap, collective, name):
     batches, run, width = rows_x.shape
     units = w_gate.shape[1]
     total = E * cap
@@ -745,11 +1016,10 @@
     hidden = jax.ShapeDtypeStruct((C, batches, total, units), bf16)
     return call(
         functools.partial(experts_kernel, E, C),
-        (rows_x, rows_u, slots, gates, w_gate, w_up, w_down),
+        (rows_x, u_in, slots, gates, w_gate, w_up, w_down),
         (
             by_token,
             by_token,
-            by_slot,
             by_slot,
             by_slot,
             hidden,
@@ -758,12 +1028,14 @@
             jax.ShapeDtypeStruct((E, C, batches, 1, run), f32),
         ),
         [ANY, ANY, VMEM, VMEM, VMEM, VMEM, VMEM],
-        (ANY,) * 8 + (VMEM,),
+        (ANY,) * 7 + (VMEM,),
         [
             pltpu.VMEM(gates.shape, f32),
             pltpu.VMEM((E, C, batches, 1, run), f32),
+        ]
+        + Flow.scratch(E, C, batches, run, width, cap, kept)
+        + [
             pltpu.VMEM((2, C, batches, run, width), bf16),
-            pltpu.VMEM((2, kept, E, cap, width), bf16),
             pltpu.VMEM((2, C, batches, E, cap, width), bf16),
             pltpu.VMEM((E, cap, width), bf16),
             pltpu.VMEM((E, cap, width), bf16),
@@ -776,12 +1048,6 @@
             DMA((E, C)),
             DMA((E, C)),
             DMA((E, C)),
-            DMA((2, batches)),
-            DMA((2, 2, C, batches)),
-            DMA((2, C, batches)),
-            DMA((2, C, batches, E)),
-            DMA((2, C, batches, E)),
-            DMA((2, C, batches)),
             DMA((2, C, batches, E)),
             DMA((2, C, batches, E)),
             DMA((2, C, batches)),
@@ -1350,20 +1616,6 @@
     return [(i, size, min(length, i + 2 * size)) for i in range(0, length, size)]
 
 
-def attend_kernel(scale, queries, keys, values, row_ids, key_ids, mixed, log_total):
-    length = queries.shape[1]
-    for first, size, seen in query_blocks(length):
-        rows = pl.ds(first, size)
-        scores = contract(queries[0, rows], keys[0, :seen], (1, 1)) * scale
-        scores = jnp.where(key_ids[0, :, :seen] <= row_ids[0, rows], scores, MASKED)
-        peak = jnp.max(scores, axis=1, keepdims=True)
-        grown = jnp.exp(scores - peak)
-        total = jnp.sum(grown, axis=1, keepdims=True)
-        probs = (grown * (1.0 / total)).astype(bf16)
-        mixed[0, rows] = jnp.dot(probs, values[0, :seen], preferred_element_type=f32).astype(bf16)
-        log_total[0, 0, rows] = peak + jnp.log(total)
-
-
 def attend_back_kernel(
     scale, queries, keys, values, grads, row_ids, key_ids, log_total, query_grad, key_grad, value_grad
 ):
@@ -1390,24 +1642,6 @@
     key_ids = pl.BlockSpec((1, 1, length), lambda b, h: (b, 0, 0))
     log_total = pl.BlockSpec((1, 1, length, 1), lambda b, h: (b, h, 0, 0))
     return head, row_ids, key_ids, log_total
-
-
-def attend(queries, keys, values, ids):
-    batches, length, size = queries.shape
-    heads = size // HEAD
-    head, row_ids, key_ids, log_total = attention_specs(length)
-    return pl.pallas_call(
-        functools.partial(attend_kernel, HEAD**-0.5),
-        grid=(batches, heads),
-        out_shape=(
-            jax.ShapeDtypeStruct(queries.shape, bf16),
-            jax.ShapeDtypeStruct((batches, heads, length, 1), f32),
-        ),
-        in_specs=[head, head, head, row_ids, key_ids],
-        out_specs=(head, log_total),
-        compiler_params=pltpu.CompilerParams(vmem_limit_bytes=48 * MIB),
-        name="attend",
-    )(queries, keys, values, ids[:, :, None], ids[:, None, :])
 
 
 def attend_back(queries, keys, values, grads, ids, totals):
@@ -1498,23 +1732,38 @@
     full_router = small[:, 4 : 4 + experts]
     head_gains = lax.dynamic_slice(gains, (me * size, 0), (size, 4))
 
-    column = column.reshape(every, width).astype(f32)
-    normed = (column * rms_factor(column) * gains[:, 0]).astype(bf16)
-    qkv = jnp.dot(normed, w_qkv, preferred_element_type=f32)
-    query_raw, key_raw = qkv[:, :size], qkv[:, size : 2 * size]
-    value_low = qkv[:, 2 * size :].astype(bf16)
-    squares = jnp.stack([jnp.sum(query_raw * query_raw, axis=1), jnp.sum(key_raw * key_raw, axis=1)])
-    factors = lax.rsqrt(column_sum(E, C, G, squares, 2, "squares") / width + EPSILON)
-    query_factor, key_factor = factors[0][:, None], factors[1][:, None]
-    query_hat, key_hat = query_raw * query_factor, key_raw * key_factor
+    (
+        normed,
+        query_low,
+        key_low,
+        value_low,
+        query_hat,
+        key_hat,
+        log_total,
+        factors,
+        mixed_low,
+        upstream_rows,
+    ) = run_forward(
+        E,
+        C,
+        G,
+        column.reshape(every, width),
+        jnp.swapaxes(gains[:, :1], 0, 1),
+        jnp.swapaxes(head_gains[:, 1:3], 0, 1),
+        w_qkv,
+        ids,
+        slots,
+        cotangent,
+        capacity,
+        2,
+        "forward",
+    )
+    mixed_low = mixed_low.reshape(own, width)
+    query_factor, key_factor = factors[0, 0][:, None], factors[1, 0][:, None]
     by_sequence = (batches, length, size)
-    query_low = (query_hat * head_gains[:, 1]).astype(bf16).reshape(by_sequence)
-    key_low = (key_hat * head_gains[:, 2]).astype(bf16).reshape(by_sequence)
-    value_low = value_low.reshape(by_sequence)
-    mixed_heads, log_total = attend(query_low, key_low, value_low, ids)
-    mixed_low = to_tokens(
-        E, C, G, mixed_heads.reshape(batches, count, run, size), 3, "mixed_rows"
-    ).reshape(own, width)
+    query_low, key_low, value_low = (
+        low.reshape(by_sequence) for low in (query_low, key_low, value_low)
+    )
 
     inputs = tokens.reshape(own, width).astype(f32)
     resid = inputs + jnp.dot(mixed_low, full_output, preferred_element_type=f32)
@@ -1526,11 +1775,11 @@
     gate_table = jnp.transpose(router_probs.reshape(batches, run, E, C), (2, 3, 0, 1))
     table = jnp.concatenate([by_expert, gate_table], axis=2)[:, :, :, None, :]
 
-    mixture, second_grad, x, _, pair_grad, act, gate_pre_grad, up_pre_grad, gate_grad = run_experts(
+    mixture, second_grad, x, pair_grad, act, gate_pre_grad, up_pre_grad, gate_grad = run_experts(
         E,
         C,
         second_low.reshape(batches, run, width),
-        cotangent,
+        upstream_rows,
         slots,
         table,
         expert_gate[0],

time: 947 us -> 895 us (0.945)
  other arithmetic: 68.8 us -> 43.8 us
  Pallas kernels: 812 us -> 794 us
  matrix products: 22.6 us -> 12.7 us
    convert_element_type x3 -> x2, other arithmetic: 19.7 us -> 0.87 us  [the longest x1 0.86 us: body(): (key_factor * (key_back - key_hat * means[1][:, None])).astype(bf16)]
    pallas_call x1 -> x0, Pallas kernels: 12 us -> none  [attend(): pl.pallas_call(functools.partial(attend_kernel, HEAD ** (-0.5)), grid=(ba...]
    dot_general x1 -> x0, matrix products: 10 us -> none  [body(): qkv = jnp.dot(normed, w_qkv, preferred_element_type=f32)]
    pallas_call x7 -> x6, Pallas kernels: 782 us -> 775 us  [call(): pl.pallas_call(kernel, out_shape=out_shapes, in_specs=in_specs, out_specs...]
    unnamed x128 -> x124, local copies, waits for them, and re-layouts: 24.3 us -> 23.3 us
where the time goes in v4:
time: 895 us; the launch traced here: 885 us
  Pallas kernels  794 us (89%)
  other arithmetic  43.8 us (5%)
  local copies, waits for them, and re-layouts  33.3 us (4%)
  matrix products  12.7 us (1%)
    pallas_call x6, Pallas kernels, call(): pl.pallas_call(kernel, out_shape=out_shapes, in_specs=in_specs, out_specs...  775 us
    unnamed x124, local copies, waits for them, and re-layouts  23.3 us
    pallas_call x1, Pallas kernels, attend_back(): pl.pallas_call(functools.partial(attend_back_kernel, HEAD ** (-0.5)), gri...  18.6 us

profile of v4, /device:TPU:1, one launch (start us, length us, event | category | flops | bytes accessed | tf_op | source)
XLA Modules:
  0.0 885.0 jit_solution(7283590710154309179)
XLA Ops:
  0.7 1.6 multiply_reduce_fusion.4
  7.5 119.8 %start.1 = (bf16[2,8,128,2048]{3,2,1,0:T(8,128)(2,1)S(1)}, bf16[4,8,64,768]{3,2,1,0:T(8,128)(2,1)S(1)}, bf16[4,8,64,128]{3,2,1,0:T(8,128)(2,1)S(1)}, bf16[4,4,2,...) custom-call(bf16[2,128,2048]{2,1,0:T(8,128)(2,1)S(1)} %copy-done, ...), custom_call_target="tpu_custom_call" | custom-call | tf_op jit(solution)/shard_map/start/pallas_call | solution.py:25
  127.3 1.7 copy-done.1
  128.9 3.2 copy-done.3
  132.8 3.2 copy-done.12
  140.1 108.5 %forward.1 = (bf16[2048,2048]{1,0:T(8,128)(2,1)}, bf16[2048,256]{1,0:T(8,128)(2,1)}, bf16[2048,256]{1,0:T(8,128)(2,1)}, bf16[2048,256]{1,0:T(8,128)(2,1)}, f32[2...) custom-call(bf16[2048,2048]{1,0:T(8,128)(2,1)} %bitcast.176, ...), custom_call_target="tpu_custom_call" | custom-call | tf_op jit(solution)/shard_map/forward/pallas_call | solution.py:25
  250.0 2.3 copy.75
  252.3 5.8 multiply_reduce_fusion.6
  260.5 355.4 %experts.1 = (bf16[4,2,128,2048]{3,2,1,0:T(8,128)(2,1)}, bf16[4,2,128,2048]{3,2,1,0:T(8,128)(2,1)}, bf16[4,2,4,64,2048]{4,3,2,1,0:T(8,128)(2,1)}, bf16[4,2,4,64,...) custom-call(bf16[2,128,2048]{2,1,0:T(8,128)(2,1)} %bitcast.192, ...), custom_call_target="tpu_custom_call" | custom-call | tf_op jit(solution)/shard_map/experts/pallas_call | solution.py:25
  615.9 4.7 convert_reduce_fusion.1
  626.2 3.3 convolution_convert_fusion
  629.5 76.0 %middle.1 = (bf16[2,8,128,256]{3,2,1,0:T(8,128)(2,1)}, bf16[4,64,2048]{2,1,0:T(8,128)(2,1)}, f32[2048,512]{1,0:T(8,128)}, f32[2048,512]{1,0:T(8,128)}, f32[512,2...) custom-call(bf16[2,128,2048]{2,1,0:T(8,128)(2,1)} %bitcast.214, ...), custom_call_target="tpu_custom_call" | custom-call | tf_op jit(solution)/shard_map/middle/pallas_call | solution.py:25
  709.2 18.6 %attend_back.1 = (f32[2,1024,256]{2,1,0:T(8,128)}, f32[2,1024,256]{2,1,0:T(8,128)}, f32[2,1024,256]{2,1,0:T(8,128)}) custom-call(bf16[2,1024,256]{2,1,0:T(8,128)(2,1)S(1)} %bitcast.180, bf16[2,1024,256]{2,1,0:T(8,128)(2,1)S(1)} %bitcast.181, bf16[2,1024,256]{2,1,0:T(8,128)(2,1)S(1)} %bitcast.182, bf16[2,1024,256]{2,1,0:T(8,128)(2,1)S(1)} %bitcast.183, ...), custom_call_target="tpu_custom_call" | custom-call | tf_op jit(solution)/shard_map/attend_back/pallas_call | solution.py:1652
  727.8 2.8 convert_element_type.107
  730.7 2.2 fusion.1
  734.9 12.3 %norm_means.1 = f32[8,2,2048]{2,1,0:T(2,128)S(1)} custom-call(f32[2,2048]{1,0:T(2,128)S(1)} %pad_maximum_fusion.3.part), custom_call_target="tpu_custom_call" | custom-call | tf_op jit(solution)/shard_map/norm_means/pallas_call | solution.py:25
  748.7 2.8 multiply_convert_fusion.1
  752.7 1.8 pad_maximum_fusion
  756.9 103.0 %finish.1 = (f32[256,2048]{1,0:T(8,128)}, bf16[8,64,768]{2,1,0:T(8,128)(2,1)}, f32[8,64,128]{2,1,0:T(8,128)}) custom-call(bf16[2,8,128,768]{3,2,1,0:T(8,128)(2,1)} %bitcast.193, bf16[2048,768]{1,0:T(8,128)(2,1)} %bitcast.175, bf16[2048,2048]{1,0:T(8,128)(2,1)} %get-tuple-element.76.normed, f32[4,512,128]{2,1,0:T(8,128)} %bitcast.205), custom_call_target="tpu_custom_call" | custom-call | tf_op jit(solution)/shard_map/finish/pallas_call | solution.py:25
  860.0 2.2 multiply_reduce_fusion
  862.4 5.1 multiply_add_fusion
  873.2 2.9 add_bitcast_fusion.2
  877.6 2.9 add_bitcast_fusion.1
  882.0 2.7 add_bitcast_fusion
  (182 shorter events, 38.6 us)
Async XLA Ops:
  0.6 6.7 copy-start.42
  0.7 6.7 copy-start.41
  0.7 6.8 copy-start
  0.7 6.8 copy-start.8
  0.7 6.8 copy-start.11
  248.6 3.7 copy-start.39
  258.2 365.9 %copy-start.49 = (f32[256]{0:T(256)}, f32[256]{0:T(256)S(1)}, u32[]{:S(2)}) copy-start(f32[256]{0:T(256)S(1)} %add_rsqrt_fusion) | copy-start | bytes 3076
  615.9 4.7 copy-start.46
  615.9 4.8 copy-start.19
  615.9 5.0 copy-start.26
  620.9 5.3 slice-start
  622.5 3.7 slice-start.1
  629.5 76.0 %copy-start.2 = (s32[2,1024,1]{2,1,0:T(8,128)S(1)}, s32[2,1024,1]{2,1,0:T(8,128)}, u32[]{:S(2)}) copy-start(s32[2,1024,1]{2,1,0:T(8,128)} %copy.74.row_ids) | copy-start | bytes 24580
  629.5 76.0 %copy-start.4 = (bf16[2048,256]{1,0:T(8,128)(2,1)S(1)}, bf16[2048,256]{1,0:T(8,128)(2,1)}, u32[]{:S(2)}) copy-start(bf16[2048,256]{1,0:T(8,128)(2,1)} %get-tuple-element.61) | copy-start | bytes 3145732
  629.5 76.0 %copy-start.9 = (s32[2,8,128]{2,1,0:T(8,128)S(1)}, s32[2,8,128]{2,1,0:T(8,128)}, u32[]{:S(2)}) copy-start(s32[2,8,128]{2,1,0:T(8,128)} %copy.73) | copy-start | bytes 24580
  756.9 103.1 %copy-start.51 = (f32[256]{0:T(256)S(1)}, f32[256]{0:T(256)}, u32[]{:S(2)}) copy-start(f32[256]{0:T(256)} %rsqrt_bitcast_fusion) | copy-start | bytes 3076
  756.9 105.3 %copy-start.17 = (f32[256,2048]{1,0:T(8,128)S(1)}, f32[256,2048]{1,0:T(8,128)}, u32[]{:S(2)}) copy-start(f32[256,2048]{1,0:T(8,128)} %copy-done.16) | copy-start | bytes 6291460
  862.4 5.1 copy-start.45
  870.1 6.0 copy-start.36
  871.3 4.8 copy-start.37
  873.2 3.5 copy-start.28
  873.2 4.4 copy-start.33
  877.6 3.5 copy-start.27
  877.6 4.4 copy-start.32
  (36 other events, 76.2 us)

commit v5 on v4

--- a/solution.py
+++ b/solution.py
@@ -302,33 +302,6 @@
     )
 
 
-def share_kernel(E, C, G, part, parts, ss, rs):
-    me, peers = column_peers(E, C, G)
-    meet([device for _, _, device in peers])
-    copies = []
-    for offset, _, device in peers:
-        copy = remote(part, parts.at[me], ss.at[offset], rs.at[offset], device)
-        copy.start()
-        copies.append(copy)
-    parts[me] = part[...]
-    for copy in copies:
-        copy.wait()
-
-
-def column_sum(E, C, G, part, collective, name):
-    parts = call(
-        functools.partial(share_kernel, E, C, G),
-        (part,),
-        jax.ShapeDtypeStruct((C * G,) + part.shape, part.dtype),
-        [VMEM],
-        VMEM,
-        [DMA((C * G,)), DMA((C * G,))],
-        collective,
-        name,
-    )
-    return jnp.sum(parts, axis=0)
-
-
 def choose(slots, count):
     cells = lax.broadcasted_iota(jnp.int32, (count, slots.shape[1]), 0).astype(f32)
     return jnp.concatenate(
@@ -458,6 +431,77 @@
             DMA((C, batches, E)),
             DMA((C, batches, E)),
             DMA((C, batches)),
+        ]
+
+
+class Return:
+    def __init__(self, E, C, runs, rows, slots, out, returned, sums, ys, yr, bs, us, ur, ks):
+        self.E, self.C, self.runs = E, C, runs
+        self.rows, self.slots, self.out = rows, slots, out
+        self.returned, self.sums = returned, sums
+        self.sems = ys, yr, bs, us, ur, ks
+        self.e, self.c, self.d = position()
+
+    def back(self, n, k):
+        b, i = self.runs[n]
+        return remote(
+            self.rows.at[i, b, k],
+            self.returned.at[n, self.e],
+            self.sems[0].at[n, k],
+            self.sems[1].at[n, k],
+            (lax.rem(self.e + self.E - k, self.E), self.c, self.d),
+        )
+
+    def own(self, n):
+        b, i = self.runs[n]
+        return pltpu.make_async_copy(
+            self.rows.at[i, b, 0], self.returned.at[n, self.e], self.sems[2].at[n]
+        )
+
+    def along(self, n):
+        i = self.runs[n][1]
+        if i == 0:
+            return pltpu.make_async_copy(self.sums.at[n], self.out.at[n], self.sems[5].at[n])
+        to = (self.e, lax.rem(self.c + self.C - i, self.C), self.d)
+        return remote(
+            self.sums.at[n], self.out.at[n], self.sems[3].at[n], self.sems[4].at[n], to
+        )
+
+    def begin(self):
+        for n in range(len(self.runs)):
+            for k in range(1, self.E):
+                self.back(n, k).start()
+            self.own(n).start()
+
+    def combine(self, n):
+        b, i = self.runs[n]
+        for k in range(1, self.E):
+            self.back(n, k).wait_recv()
+        self.own(n).wait()
+        cap, width = self.rows.shape[3:]
+        picks = choose(self.slots[i, b], cap)
+        for at in range(0, width, 512):
+            part = self.returned[n, :, :, at : at + 512].reshape(self.E * cap, 512)
+            self.sums[n, :, at : at + 512] = contract(picks, part, (0, 0)).astype(bf16)
+        self.along(n).start()
+
+    def end(self):
+        for n in range(len(self.runs)):
+            for k in range(1, self.E):
+                self.back(n, k).wait_send()
+            self.along(n).wait()
+
+    @staticmethod
+    def scratch(E, C, count, run, width, cap):
+        return [
+            pltpu.VMEM((count, E, cap, width), bf16),
+            pltpu.VMEM((count, run, width), bf16),
+            DMA((count, E)),
+            DMA((count, E)),
+            DMA((count,)),
+            DMA((count,)),
+            DMA((count,)),
+            DMA((count,)),
         ]
 
 
@@ -739,9 +783,9 @@
     w_gate,
     w_up,
     w_down,
-    out_y,
-    out_b,
+    out,
     x_out,
+    y_out,
     pair_out,
     act_out,
     gate_back_out,
@@ -765,6 +809,7 @@
     act,
     gate_back,
     up_back,
+    gated,
     sent,
     gs,
     gr,
@@ -785,13 +830,12 @@
     units = w_gate.shape[1]
     chunks = batches * C
     total = E * cap
-    kept = sent.shape[1]
+    kept = sent.shape[0]
     lead, lag = 1, 2
     everyone = [(k, i) for k in range(E) for i in range(C) if k + i > 0]
     ahead = [(k, i, (lax.rem(e + k, E), lax.rem(c + i, C), d)) for k, i in everyone]
     behind = [(k, i, (lax.rem(e + E - k, E), lax.rem(c + C - i, C), d)) for k, i in everyone]
     meet([device for _, _, device in ahead])
-    outs = out_y, out_b
     flow = Flow(E, C, rows_x, slots, landed, packed, x_out, own, zs, zr, xs, xr, stay)
 
     def far_of(n):
@@ -801,39 +845,39 @@
         far, b = far_of(n)
         return b, flow.level_entry(far)
 
-    def back(a, n, b, i, k):
+    def back(n, b, i, k):
         return remote(
-            sent.at[a, lax.rem(n, kept), k],
-            returned.at[a, i, b, e],
-            ys.at[a, i, b, k],
-            yr.at[a, i, b, k],
+            sent.at[lax.rem(n, kept), k],
+            returned.at[i, b, e],
+            ys.at[i, b, k],
+            yr.at[i, b, k],
             (lax.rem(e + E - k, E), c, d),
         )
 
-    def back_own(a, n, b, i):
+    def back_own(n, b, i):
         return pltpu.make_async_copy(
-            sent.at[a, lax.rem(n, kept), 0], returned.at[a, i, b, e], bs.at[a, i, b]
+            sent.at[lax.rem(n, kept), 0], returned.at[i, b, e], bs.at[i, b]
         )
 
-    def up(a, b, i):
+    def up(b, i):
         return remote(
-            sums.at[a, i, b],
-            outs[a].at[c, b],
-            us.at[a, i, b],
-            ur.at[a, i, b],
+            sums.at[i, b],
+            out.at[c, b],
+            us.at[i, b],
+            ur.at[i, b],
             (e, lax.rem(c + C - i, C), d),
         )
 
-    def keep(a, b):
-        return pltpu.make_async_copy(sums.at[a, 0, b], outs[a].at[c, b], ks.at[a, b])
+    def keep(b):
+        return pltpu.make_async_copy(sums.at[0, b], out.at[c, b], ks.at[b])
 
     def load(a, b, i):
         source, target = ((x_out, x), (u_in, u))[a]
         return pltpu.make_async_copy(source.at[i, b], target, loads.at[a])
 
     def store(j, b, i):
-        source = (pair, act, gate_back, up_back)[j]
-        target = (pair_out, act_out, gate_back_out, up_back_out)[j]
+        source = (pair, act, gate_back, up_back, gated)[j]
+        target = (pair_out, act_out, gate_back_out, up_back_out, y_out)[j]
         return pltpu.make_async_copy(source, target.at[i, b], stores.at[j])
 
     flow.begin()
@@ -862,15 +906,14 @@
         @pl.when(n > 0)
         def _():
             before = chunk_of(n - 1)
-            for j in range(4):
+            for j in range(5):
                 store(j, *before).wait()
 
         @pl.when(n >= kept)
         def _():
             before = chunk_of(n - kept)
-            for a in range(2):
-                for k in range(1, E):
-                    back(a, n - kept, *before, k).wait_send()
+            for k in range(1, E):
+                back(n - kept, *before, k).wait_send()
 
         holds, gate = [], []
         cells = lax.broadcasted_iota(jnp.int32, (cap, run), 0).astype(f32)
@@ -910,14 +953,14 @@
             gate_grad += jnp.sum(
                 out * u[:, :, at : at + 512].reshape(total, 512).astype(f32), axis=1, keepdims=True
             )
-            sent[0, place, :, :, at : at + 512] = (gate * out).astype(bf16).reshape(E, cap, 512)
+            gated[:, :, at : at + 512] = (gate * out).astype(bf16).reshape(E, cap, 512)
             back_rows = contract(gate_back[...], w_gate[at : at + 512, :], (1, 1))
             back_rows += contract(up_back[...], w_up[at : at + 512, :], (1, 1))
-            sent[1, place, :, :, at : at + 512] = back_rows.astype(bf16).reshape(E, cap, 512)
-        for a in (1, 0):
-            for k in range(1, E):
-                back(a, n, b, i, k).start()
-            back_own(a, n, b, i).start()
+            sent[place, :, :, at : at + 512] = back_rows.astype(bf16).reshape(E, cap, 512)
+        for k in range(1, E):
+            back(n, b, i, k).start()
+        back_own(n, b, i).start()
+        store(4, b, i).start()
         for k in range(E):
             scalars[k, i, b] = jnp.sum(
                 jnp.where(holds[k], gate_grad[k * cap : (k + 1) * cap], 0.0), axis=0, keepdims=True
@@ -926,21 +969,20 @@
     def combine(n):
         b, i = chunk_of(n)
         picks = choose(slots[i, b], cap)
-        for a in (1, 0):
-            for k in range(1, E):
-                back(a, n, b, i, k).wait_recv()
-            back_own(a, n, b, i).wait()
-            for at in range(0, width, 512):
-                part = returned[a, i, b, :, :, at : at + 512].reshape(total, 512)
-                sums[a, i, b, :, at : at + 512] = contract(picks, part, (0, 0)).astype(bf16)
-
-            @pl.when(i > 0)
-            def _():
-                up(a, b, i).start()
-
-            @pl.when(i == 0)
-            def _():
-                keep(a, b).start()
+        for k in range(1, E):
+            back(n, b, i, k).wait_recv()
+        back_own(n, b, i).wait()
+        for at in range(0, width, 512):
+            part = returned[i, b, :, :, at : at + 512].reshape(total, 512)
+            sums[i, b, :, at : at + 512] = contract(picks, part, (0, 0)).astype(bf16)
+
+        @pl.when(i > 0)
+        def _():
+            up(b, i).start()
+
+        @pl.when(i == 0)
+        def _():
+            keep(b).start()
 
     def step(s, carry):
         @pl.when(jnp.logical_and(s > 0, s <= batches * (C - 1)))
@@ -973,7 +1015,7 @@
         copy.start()
     for copy in small:
         copy.wait_send()
-    for j in range(4):
+    for j in range(5):
         store(j, *chunk_of(chunks - 1)).wait()
 
     def finish(n, carry):
@@ -984,20 +1026,18 @@
         def _():
             flow.crossed(n, b, i)
 
-        for a in range(2):
-
-            @pl.when(n >= chunks - kept)
-            def _():
-                for k in range(1, E):
-                    back(a, n, b, i, k).wait_send()
-
-            @pl.when(i > 0)
-            def _():
-                up(a, b, i).wait()
-
-            @pl.when(i == 0)
-            def _():
-                keep(a, b).wait()
+        @pl.when(n >= chunks - kept)
+        def _():
+            for k in range(1, E):
+                back(n, b, i, k).wait_send()
+
+        @pl.when(i > 0)
+        def _():
+            up(b, i).wait()
+
+        @pl.when(i == 0)
+        def _():
+            keep(b).wait()
 
         return carry
 
@@ -1019,7 +1059,7 @@
         (rows_x, u_in, slots, gates, w_gate, w_up, w_down),
         (
             by_token,
-            by_token,
+            by_slot,
             by_slot,
             by_slot,
             hidden,
@@ -1035,27 +1075,28 @@
         ]
         + Flow.scratch(E, C, batches, run, width, cap, kept)
         + [
-            pltpu.VMEM((2, C, batches, run, width), bf16),
-            pltpu.VMEM((2, C, batches, E, cap, width), bf16),
+            pltpu.VMEM((C, batches, run, width), bf16),
+            pltpu.VMEM((C, batches, E, cap, width), bf16),
             pltpu.VMEM((E, cap, width), bf16),
             pltpu.VMEM((E, cap, width), bf16),
             pltpu.VMEM((E, cap, width), bf16),
             pltpu.VMEM((total, units), bf16),
             pltpu.VMEM((total, units), bf16),
             pltpu.VMEM((total, units), bf16),
-            pltpu.VMEM((2, kept, E, cap, width), bf16),
+            pltpu.VMEM((E, cap, width), bf16),
+            pltpu.VMEM((kept, E, cap, width), bf16),
             DMA((E, C)),
             DMA((E, C)),
             DMA((E, C)),
             DMA((E, C)),
-            DMA((2, C, batches, E)),
-            DMA((2, C, batches, E)),
-            DMA((2, C, batches)),
-            DMA((2, C, batches)),
-            DMA((2, C, batches)),
-            DMA((2, batches)),
+            DMA((C, batches, E)),
+            DMA((C, batches, E)),
+            DMA((C, batches)),
+            DMA((C, batches)),
+            DMA((C, batches)),
+            DMA((batches,)),
             DMA((2,)),
-            DMA((4,)),
+            DMA((5,)),
         ],
         collective,
         name,
@@ -1067,6 +1108,7 @@
     E,
     C,
     G,
+    runs,
     rows,
     mixed,
     grads,
@@ -1075,6 +1117,8 @@
     gate_back,
     up_back,
     act,
+    y_rows,
+    slots,
     heads,
     proj,
     own_gate,
@@ -1083,6 +1127,7 @@
     other_gate,
     other_up,
     other_down,
+    out,
     hidden,
     wide,
     kept,
@@ -1106,6 +1151,7 @@
     ks,
     xs,
     xr,
+    *return_scratch,
 ):
     e, c, d = position()
     me, peers = column_peers(E, C, G)
@@ -1131,6 +1177,9 @@
     for copy in head_copies:
         copy.start()
 
+    way_back = Return(E, C, runs, y_rows, slots, out, *return_scratch)
+    way_back.begin()
+
     hidden_copies = [
         pltpu.make_async_copy(source, hidden.at[j], rs.at[j])
         for j, source in enumerate((gate_back, up_back, act))
@@ -1165,12 +1214,14 @@
             device,
         )
 
-    def give(level, carry):
+    def give(i, carry):
+        level = lax.rem(c + 1 + i, C)
         swap[level] = proj_part(1 - d, level).astype(bf16)
         chip_copy(level).start()
         return carry
 
-    def take(level, carry):
+    def take(i, carry):
+        level = lax.rem(c + 1 + i, C)
         part = proj_part(d, level)
         chip_copy(level).wait_recv()
         part = (part + swapped[level].astype(f32)).astype(bf16)
@@ -1182,13 +1233,20 @@
     lax.fori_loop(0, C, give, 0)
     lax.fori_loop(0, C, take, 0)
 
-    def plane_sum(level, carry):
+    def level_copy(i, level):
+        return remote(level_part.at[level], proj.at[c], zs.at[i], zr.at[i], (e, level, d))
+
+    def plane_sum(i):
+        level = lax.rem(c + i, C)
         total = chip[level, e].astype(f32)
         for k, _, device in planes:
             plane_copy(level, k, device).wait_recv()
             total = total + plane_parts[level, k].astype(f32)
         level_part[level] = total.astype(bf16)
-        return carry
+        if i > 0:
+            level_copy(i, level).start()
+        else:
+            proj[c] = level_part[c]
 
     def keep_copy(j, at, place):
         target = (own_gate, own_up, own_down)[j]
@@ -1200,7 +1258,9 @@
         where = target.at[:, pl.ds(at, step)] if j == 2 else target.at[pl.ds(at, step)]
         return remote(sent.at[place], where, xs.at[place], xr.at[place], sibling)
 
-    kept_copies, sent_copies = [], []
+    kept_copies, sent_copies, after = [], [], {}
+    for n in range(len(runs)):
+        after.setdefault(count + n * count // max(1, len(runs)), []).append(n)
     for copy in hidden_copies:
         copy.wait()
     for item in range(2 * count):
@@ -1226,19 +1286,18 @@
             kept_copies.append(copy)
         if item + 2 < 2 * count:
             wide_copy(item + 2).start()
-        if item == count - 1:
-            lax.fori_loop(0, C, plane_sum, 0)
-            level_copies = []
-            for i, level, device in levels:
-                copy = remote(level_part.at[level], proj.at[c], zs.at[i], zr.at[i], device)
-                copy.start()
-                level_copies.append(copy)
-            proj[c] = level_part[c]
+        for n in after.get(item, ()):
+            way_back.combine(n)
+    for i in list(range(1, C)) + [0]:
+        plane_sum(i)
 
     for copy in kept_copies[-2:]:
         copy.wait()
-    for copy in sent_copies + level_copies + head_copies:
+    for copy in sent_copies + head_copies:
         copy.wait()
+    for i, level, _ in levels:
+        level_copy(i, level).wait()
+    way_back.end()
 
     def done(level, carry):
         chip_copy(level).wait_send()
@@ -1249,7 +1308,9 @@
     lax.fori_loop(0, C, done, 0)
 
 
-def middle(E, C, G, rows, mixed, grads, x, pair, gate_back, up_back, act, collective, name):
+def middle(
+    E, C, G, runs, rows, mixed, grads, x, pair, gate_back, up_back, act, y_rows, slots, collective, name
+):
     batches, run, width = rows.shape
     count = C * G
     part = mixed.shape[3]
@@ -1261,8 +1322,8 @@
     tall = (width, half)
     flat = (half, width)
     return call(
-        functools.partial(middle_kernel, E, C, G),
-        (rows, mixed, grads, x, pair, gate_back, up_back, act),
+        functools.partial(middle_kernel, E, C, G, runs),
+        (rows, mixed, grads, x, pair, gate_back, up_back, act, y_rows, slots),
         (
             jax.ShapeDtypeStruct((batches, count, run, width // count), bf16),
             jax.ShapeDtypeStruct((C, part, width), bf16),
@@ -1272,9 +1333,10 @@
             jax.ShapeDtypeStruct(tall, bf16),
             jax.ShapeDtypeStruct(tall, bf16),
             jax.ShapeDtypeStruct(flat, bf16),
+            jax.ShapeDtypeStruct((len(runs), run, width), bf16),
         ),
-        [ANY, VMEM, VMEM] + [ANY] * 5,
-        (ANY, VMEM) + (ANY,) * 6,
+        [ANY, VMEM, VMEM] + [ANY] * 6 + [VMEM],
+        (ANY, VMEM) + (ANY,) * 7,
         [
             pltpu.VMEM((3, total, units), bf16),
             pltpu.VMEM((2, total, step), bf16),
@@ -1299,24 +1361,49 @@
             DMA((2,)),
             DMA((items,)),
             DMA((items,)),
-        ],
+        ]
+        + Return.scratch(E, C, len(runs), run, width, y_rows.shape[3]),
         collective,
         name,
         vmem=60,
     )
 
 
-def finish_kernel(
+def backward_kernel(
     E,
     C,
     G,
-    raw,
+    runs,
+    queries,
+    keys,
+    values,
+    grads,
+    row_ids,
+    key_ids,
+    log_total,
+    query_hat,
+    key_hat,
+    factors,
+    head_gains,
+    y_rows,
+    slots,
     w_qkv,
     normed,
     small,
     first,
     out_qkv,
     out_small,
+    out_gains,
+    out,
+    raw,
+    query_grad,
+    key_grad,
+    key_sum,
+    value_sum,
+    sums,
+    sum_parts,
+    gain_sum,
+    gain_parts,
     small_parts,
     small_sum,
     swap,
@@ -1340,23 +1427,36 @@
     sr,
     fs,
     fr,
+    ms,
+    mr,
+    hs,
+    hr,
+    gs,
+    gr,
+    *return_scratch,
 ):
     e, c, d = position()
     me, peers = column_peers(E, C, G)
     planes = plane_peers(E)
-    batches, _, run, columns = raw.shape
+    count = C * G
+    _, run, columns = raw.shape
+    every, size = queries.shape
+    batches, length = row_ids.shape[:2]
+    scale = HEAD**-0.5
     width = w_qkv.shape[0]
     rows = batches * run
     sibling = (e, c, 1 - d)
     meet([device for _, _, device in peers] + [device for _, _, device in planes])
-    block = tokens.shape[2]
-
-    def token_copy(item):
-        plane = lax.rem(e + 1 + item, E)
+    half = tokens.shape[2]
+    block = parts.shape[1]
+    cuts = block // half
+
+    def token_copy(part):
+        at = lax.rem(e + 1 + part // cuts, E) * block + part % cuts * half
         return pltpu.make_async_copy(
-            normed.at[:, pl.ds(pl.multiple_of(plane * block, block), block)],
-            tokens.at[item % 2],
-            ts.at[item % 2],
+            normed.at[:, pl.ds(pl.multiple_of(at, half), half)],
+            tokens.at[part % 2],
+            ts.at[part % 2],
         )
 
     token_copy(0).start()
@@ -1368,9 +1468,125 @@
     for copy in small_copies:
         copy.start()
 
-    def product(level, core, at, size):
-        left = jnp.concatenate([raw[b, level * G + core] for b in range(batches)], axis=0)
-        return contract(left, w_qkv[at : at + size, :], (1, 1))
+    way_back = Return(E, C, runs, y_rows, slots, out, *return_scratch)
+    way_back.begin()
+    heads = size // HEAD
+
+    def head_back(n, carry):
+        b, h = n // heads, lax.rem(n, heads)
+        lanes = pl.ds(pl.multiple_of(h * HEAD, HEAD), HEAD)
+        start = pl.multiple_of(b * length, length)
+        key_sum[...] = jnp.zeros_like(key_sum)
+        value_sum[...] = jnp.zeros_like(value_sum)
+        for at, many, seen in query_blocks(length):
+            rows_here = pl.ds(pl.multiple_of(start + at, many), many)
+            rows_seen = pl.ds(start, seen)
+            query, grad = queries[rows_here, lanes], grads[rows_here, lanes]
+            scores = contract(query, keys[rows_seen, lanes], (1, 1)) * scale
+            allowed = key_ids[b, :, :seen] <= row_ids[b, at : at + many]
+            scores = jnp.where(allowed, scores, MASKED)
+            probs = jnp.exp(scores - log_total[b, h, at : at + many])
+            prod = contract(grad, values[rows_seen, lanes], (1, 1))
+            delta = jnp.sum(probs * prod, axis=1, keepdims=True)
+            score_grad = (probs * (prod - delta)).astype(bf16)
+            query_grad[rows_here, lanes] = (
+                jnp.dot(score_grad, keys[rows_seen, lanes], preferred_element_type=f32) * scale
+            )
+            key_sum[:seen] += contract(score_grad, query, (0, 0)) * scale
+            value_sum[:seen] += contract(probs.astype(bf16), grad, (0, 0))
+        key_grad[pl.ds(start, length), lanes] = key_sum[...]
+        value_lanes = pl.ds(pl.multiple_of(2 * size + h * HEAD, HEAD), HEAD)
+        raw[pl.ds(b * count, count), :, value_lanes] = (
+            value_sum[...].astype(bf16).reshape(count, run, HEAD)
+        )
+        return carry
+
+    pending = iter(range(len(runs)))
+
+    def carry_on(many):
+        for _ in range(many):
+            n = next(pending, None)
+            if n is not None:
+                way_back.combine(n)
+
+    lax.fori_loop(0, batches * heads, head_back, 0)
+
+    chunk = min(2 * run, every)
+    per_chunk = chunk // run
+    ones = jnp.ones((8, size), f32)
+    gain_sum[...] = jnp.zeros_like(gain_sum)
+    pairs = ((query_grad, query_hat), (key_grad, key_hat))
+
+    def dots(j, carry):
+        rows_here = pl.ds(pl.multiple_of(j * chunk, chunk), chunk)
+        for kind, (grad, hat) in enumerate(pairs):
+            prod = grad[rows_here] * hat[rows_here]
+            gain_sum[kind] += jnp.sum(prod, axis=0, keepdims=True)
+            total = lax.dot_general(
+                ones,
+                prod * head_gains[kind : kind + 1],
+                (((1,), (1,)), ((), ())),
+                precision=lax.Precision.HIGHEST,
+                preferred_element_type=f32,
+            )
+            sums[kind, :, rows_here] = total[:1]
+        return carry
+
+    lax.fori_loop(0, every // chunk, dots, 0)
+    shares = [
+        remote(sums, sum_parts.at[me], ms.at[offset], mr.at[offset], device)
+        for offset, _, device in peers
+    ]
+    gain_copies = [
+        remote(gain_sum, gain_parts.at[i], hs.at[i], hr.at[i], device) for i, _, device in planes
+    ]
+    for copy in shares + gain_copies:
+        copy.start()
+    sum_parts[me] = sums[...]
+    carry_on(len(runs) // 2)
+    for copy in shares:
+        copy.wait()
+    total = sum_parts[0]
+    for index in range(1, count):
+        total = total + sum_parts[index]
+    sums[...] = total / width
+    rows_at = lax.broadcasted_iota(jnp.int32, (chunk, chunk), 0)
+    same = rows_at == lax.broadcasted_iota(jnp.int32, (chunk, chunk), 1)
+
+    def column_of(row):
+        return jnp.sum(jnp.where(same, row, 0.0), axis=1, keepdims=True)
+
+    def through_norm(j, carry):
+        rows_here = pl.ds(pl.multiple_of(j * chunk, chunk), chunk)
+        for kind, (grad, hat) in enumerate(pairs):
+            part = grad[rows_here] * head_gains[kind : kind + 1]
+            part = part - hat[rows_here] * column_of(sums[kind, :, rows_here])
+            part = (column_of(factors[kind, :, rows_here]) * part).astype(bf16)
+            raw[pl.ds(j * per_chunk, per_chunk), :, kind * size : (kind + 1) * size] = part.reshape(
+                per_chunk, run, size
+            )
+        return carry
+
+    lax.fori_loop(0, every // chunk, through_norm, 0)
+
+    def gain_copy(offset, device):
+        return remote(gain_sum, out_gains.at[me], gs.at[offset], gr.at[offset], device)
+
+    for copy in gain_copies:
+        copy.wait()
+    total = gain_sum[...]
+    for i in range(1, E):
+        total = total + gain_parts[i]
+    gain_sum[...] = total
+    out_gains[me] = total
+    for offset, _, device in peers:
+        gain_copy(offset, device).start()
+
+    def product(level, core, at, many):
+        left = jnp.concatenate(
+            [raw[b * count + level * G + core] for b in range(batches)], axis=0
+        )
+        return contract(left, w_qkv[at : at + many, :], (1, 1))
 
     def chip_copy(level):
         return remote(swap.at[level], swapped.at[level], cs.at[level], cr.at[level], sibling)
@@ -1428,17 +1644,18 @@
             (plane, c, d),
         )
 
-    raw_flat = raw[...].reshape(-1, columns)
-
     def weights(item):
-        token_copy(item).wait()
-        for at in range(0, columns, 256):
-            size = min(256, columns - at)
-            parts[item, :, at : at + size] = contract(
-                tokens[item % 2], raw_flat[:, at : at + size], (0, 0)
-            ).astype(bf16)
-        if item + 2 < E:
-            token_copy(item + 2).start()
+        for part in range(cuts * item, cuts * (item + 1)):
+            token_copy(part).wait()
+            for at in range(0, columns, 256):
+                many = min(256, columns - at)
+                piece = raw[:, :, at : at + many].reshape(every, many)
+                rows_here = pl.ds(part % cuts * half, half)
+                parts[item, rows_here, at : at + many] = contract(
+                    tokens[part % 2], piece, (0, 0)
+                ).astype(bf16)
+            if part + 2 < cuts * E:
+                token_copy(part + 2).start()
         if item < E - 1:
             plane_copy(item).start()
 
@@ -1456,7 +1673,9 @@
                 send(1, 0, False)
 
             weights(items.pop(0))
+            carry_on(1)
     weights(items.pop(0))
+    carry_on(len(runs))
     for turn in range(1, C - 1):
 
         @pl.when(c <= turn)
@@ -1552,38 +1771,96 @@
         plane_copy(item).wait_send()
     for copy in small_copies:
         copy.wait_send()
+    for offset, _, device in peers:
+        gain_copy(offset, device).wait()
+    way_back.end()
     for offset, index, device in peers:
         row_copy(offset, index, device).wait()
         small_copy(offset, index, device).wait()
 
 
-def finish(E, C, G, raw, w_qkv, normed, small, collective, name):
-    batches, count, run, columns = raw.shape
+def run_backward(
+    E,
+    C,
+    G,
+    runs,
+    queries,
+    keys,
+    values,
+    grads,
+    ids,
+    log_total,
+    query_hat,
+    key_hat,
+    factors,
+    head_gains,
+    y_rows,
+    slots,
+    w_qkv,
+    normed,
+    small,
+    collective,
+    name,
+):
+    every, size = queries.shape
+    batches, length = ids.shape
+    count = C * G
+    run = length // count
+    columns = 3 * size
     width = w_qkv.shape[0]
-    every = normed.shape[0]
     rows = batches * run
     block = width // E
     share = block // count
     lanes = small.shape[2]
     by_level = pltpu.VMEM((C, rows, width), bf16)
+    wide = pltpu.VMEM((every, size), f32)
+    head = pltpu.VMEM((length, HEAD), f32)
     return call(
-        functools.partial(finish_kernel, E, C, G),
-        (raw, w_qkv, normed, small),
+        functools.partial(backward_kernel, E, C, G, runs),
+        (
+            queries,
+            keys,
+            values,
+            grads,
+            ids[:, :, None],
+            ids[:, None, :],
+            log_total,
+            query_hat,
+            key_hat,
+            factors,
+            head_gains,
+            y_rows,
+            slots,
+            w_qkv,
+            normed,
+            small,
+        ),
         (
             jax.ShapeDtypeStruct((rows, width), f32),
             jax.ShapeDtypeStruct((count, share, columns), bf16),
             jax.ShapeDtypeStruct((count, share, lanes), f32),
+            jax.ShapeDtypeStruct((count, 2, 1, size), f32),
+            jax.ShapeDtypeStruct((len(runs), run, width), bf16),
         ),
-        [VMEM, VMEM, ANY, VMEM],
-        (VMEM, VMEM, VMEM),
+        [VMEM] * 11 + [ANY, VMEM, VMEM, ANY, VMEM],
+        (VMEM, VMEM, VMEM, VMEM, ANY),
         [
+            pltpu.VMEM((batches * count, run, columns), bf16),
+            wide,
+            wide,
+            head,
+            head,
+            pltpu.VMEM((2, 1, every), f32),
+            pltpu.VMEM((count, 2, 1, every), f32),
+            pltpu.VMEM((2, 1, size), f32),
+            pltpu.VMEM((E, 2, 1, size), f32),
             pltpu.VMEM((E, block, lanes), f32),
             pltpu.VMEM((block, lanes), f32),
             by_level,
             by_level,
             by_level,
             pltpu.VMEM((C + 1, rows, width), bf16),
-            pltpu.VMEM((2, every, block), bf16),
+            pltpu.VMEM((2, every, min(block, 256)), bf16),
             pltpu.VMEM((E, block, columns), bf16),
             pltpu.VMEM((E, block, columns), bf16),
             pltpu.VMEM((block, columns), bf16),
@@ -1600,10 +1877,17 @@
             DMA((E,)),
             DMA((count,)),
             DMA((count,)),
-        ],
+            DMA((count,)),
+            DMA((count,)),
+            DMA((E,)),
+            DMA((E,)),
+            DMA((count,)),
+            DMA((count,)),
+        ]
+        + Return.scratch(E, C, len(runs), run, width, y_rows.shape[3]),
         collective,
         name,
-        vmem=60,
+        vmem=62,
     )
 
 
@@ -1614,50 +1898,6 @@
 def query_blocks(length):
     size = min(256, length)
     return [(i, size, min(length, i + 2 * size)) for i in range(0, length, size)]
-
-
-def attend_back_kernel(
-    scale, queries, keys, values, grads, row_ids, key_ids, log_total, query_grad, key_grad, value_grad
-):
-    length = queries.shape[1]
-    key_grad[...] = jnp.zeros_like(key_grad)
-    value_grad[...] = jnp.zeros_like(value_grad)
-    for first, size, seen in query_blocks(length):
-        rows = pl.ds(first, size)
-        query, grad = queries[0, rows], grads[0, rows]
-        scores = contract(query, keys[0, :seen], (1, 1)) * scale
-        scores = jnp.where(key_ids[0, :, :seen] <= row_ids[0, rows], scores, MASKED)
-        probs = jnp.exp(scores - log_total[0, 0, rows])
-        prod = contract(grad, values[0, :seen], (1, 1))
-        delta = jnp.sum(probs * prod, axis=1, keepdims=True)
-        score_grad = (probs * (prod - delta)).astype(bf16)
-        query_grad[0, rows] = jnp.dot(score_grad, keys[0, :seen], preferred_element_type=f32) * scale
-        key_grad[0, :seen] += contract(score_grad, query, (0, 0)) * scale
-        value_grad[0, :seen] += contract(probs.astype(bf16), grad, (0, 0))
-
-
-def attention_specs(length):
-    head = pl.BlockSpec((1, length, HEAD), lambda b, h: (b, 0, h))
-    row_ids = pl.BlockSpec((1, length, 1), lambda b, h: (b, 0, 0))
-    key_ids = pl.BlockSpec((1, 1, length), lambda b, h: (b, 0, 0))
-    log_total = pl.BlockSpec((1, 1, length, 1), lambda b, h: (b, h, 0, 0))
-    return head, row_ids, key_ids, log_total
-
-
-def attend_back(queries, keys, values, grads, ids, totals):
-    batches, length, size = queries.shape
-    heads = size // HEAD
-    head, row_ids, key_ids, log_total = attention_specs(length)
-    grad = jax.ShapeDtypeStruct(queries.shape, f32)
-    return pl.pallas_call(
-        functools.partial(attend_back_kernel, HEAD**-0.5),
-        grid=(batches, heads),
-        out_shape=(grad, grad, grad),
-        in_specs=[head, head, head, head, row_ids, key_ids, log_total],
-        out_specs=(head, head, head),
-        compiler_params=pltpu.CompilerParams(vmem_limit_bytes=48 * MIB),
-        name="attend_back",
-    )(queries, keys, values, grads, ids[:, :, None], ids[:, None, :], totals)
 
 
 def rms_factor(values):
@@ -1759,11 +1999,6 @@
         "forward",
     )
     mixed_low = mixed_low.reshape(own, width)
-    query_factor, key_factor = factors[0, 0][:, None], factors[1, 0][:, None]
-    by_sequence = (batches, length, size)
-    query_low, key_low, value_low = (
-        low.reshape(by_sequence) for low in (query_low, key_low, value_low)
-    )
 
     inputs = tokens.reshape(own, width).astype(f32)
     resid = inputs + jnp.dot(mixed_low, full_output, preferred_element_type=f32)
@@ -1775,7 +2010,7 @@
     gate_table = jnp.transpose(router_probs.reshape(batches, run, E, C), (2, 3, 0, 1))
     table = jnp.concatenate([by_expert, gate_table], axis=2)[:, :, :, None, :]
 
-    mixture, second_grad, x, pair_grad, act, gate_pre_grad, up_pre_grad, gate_grad = run_experts(
+    second_grad, x, y_rows, pair_grad, act, gate_pre_grad, up_pre_grad, gate_grad = run_experts(
         E,
         C,
         second_low.reshape(batches, run, width),
@@ -1794,8 +2029,6 @@
         rows.reshape(slot_count, -1) for rows in (x, pair_grad, act, gate_pre_grad, up_pre_grad)
     )
     upstream = cotangent.reshape(own, width).astype(f32)
-    mixture = jnp.sum(mixture.astype(f32), axis=0).reshape(own, width)
-    activations = (resid + mixture).astype(bf16).reshape(tokens.shape)
     prob_grad = jnp.transpose(gate_grad[:, :, :, 0, :], (2, 3, 0, 1)).reshape(own, experts)
     logit_grad = router_probs * (
         prob_grad - jnp.sum(router_probs * prob_grad, axis=-1, keepdims=True)
@@ -1808,10 +2041,13 @@
     attn_grad = resid_grad.astype(bf16)
     mixed_grad = contract(attn_grad, full_output, (1, 1)).astype(bf16)
 
-    mixed_grad, grad_proj, *expert_grads = middle(
+    early = [(b, i) for b in range(batches // 2) for i in list(range(1, C)) + [0]]
+    late = [(b, i) for b in range(batches // 2, batches) for i in list(range(1, C)) + [0]]
+    mixed_grad, grad_proj, *expert_grads, early_mixture = middle(
         E,
         C,
         G,
+        early,
         mixed_grad.reshape(batches, run, width),
         jnp.swapaxes(mixed_low, 0, 1).reshape(E, C, G, rows, own),
         attn_grad,
@@ -1820,6 +2056,8 @@
         gate_pre_grad,
         up_pre_grad,
         act,
+        y_rows,
+        slots,
         6,
         "middle",
     )
@@ -1827,44 +2065,42 @@
         (mine + other.astype(f32))[None] for mine, other in zip(expert_grads[:3], expert_grads[3:])
     )
     grad_proj = jnp.sum(grad_proj.astype(f32), axis=0)
-    query_grad, key_grad, value_grad = (
-        grad.reshape(every, size)
-        for grad in attend_back(
-            query_low, key_low, value_low, mixed_grad.reshape(by_sequence), ids, log_total
-        )
-    )
-    query_back, key_back = query_grad * head_gains[:, 1], key_grad * head_gains[:, 2]
-    means = jnp.stack([jnp.sum(query_back * query_hat, axis=1), jnp.sum(key_back * key_hat, axis=1)])
-    means = column_sum(E, C, G, means, 7, "norm_means") / width
-    raw_grads = jnp.concatenate(
-        [
-            (query_factor * (query_back - query_hat * means[0][:, None])).astype(bf16),
-            (key_factor * (key_back - key_hat * means[1][:, None])).astype(bf16),
-            value_grad.astype(bf16),
-        ],
-        axis=1,
-    )
-    gain_heads = jnp.stack(
-        [jnp.sum(query_grad * query_hat, axis=0), jnp.sum(key_grad * key_hat, axis=0)], axis=1
-    )
-    gain_heads = lax.dynamic_update_slice(
-        jnp.zeros((width, 2), f32), gain_heads, (me * size, 0)
-    )
     sums = jnp.concatenate(
-        [gain_heads, gain_second[:, None], contract(second_low, logit_grad, (0, 0))], axis=1
+        [gain_second[:, None], contract(second_low, logit_grad, (0, 0))], axis=1
     )
     sums = jnp.pad(sums, ((0, 0), (0, small_width - sums.shape[1])))
-    first_grad, grad_qkv, sums = finish(
+    first_grad, grad_qkv, sums, gain_heads, late_mixture = run_backward(
         E,
         C,
         G,
-        raw_grads.reshape(batches, count, run, 3 * size),
+        late,
+        query_low,
+        key_low,
+        value_low,
+        mixed_grad.reshape(every, size),
+        ids,
+        log_total,
+        query_hat,
+        key_hat,
+        factors,
+        jnp.swapaxes(head_gains[:, 1:3], 0, 1),
+        y_rows,
+        slots,
         w_qkv,
         normed,
         sums.reshape(E, width // E, small_width),
         8,
-        "finish",
+        "backward",
     )
+    gain_heads = jnp.swapaxes(gain_heads[:, :, 0], 0, 1).reshape(2, width)
+    first_row = (lax.axis_index("expert") * count + me) * rows
+    gain_heads = lax.dynamic_slice(gain_heads, (0, first_row), (2, rows))
+    mixture = [0.0] * batches
+    for runs, parts in ((early, early_mixture), (late, late_mixture)):
+        for n, (b, _) in enumerate(runs):
+            mixture[b] = mixture[b] + parts[n].astype(f32)
+    mixture = jnp.stack(mixture)
+    activations = (resid.reshape(tokens.shape) + mixture).astype(bf16)
     sums = jnp.sum(sums, axis=0)
     first_factor = rms_factor(inputs)
     first_hat = inputs * first_factor
@@ -1879,7 +2115,7 @@
         for w, grad in ((w_query, grad_query), (w_key, grad_key), (w_value, grad_value))
     )
     gain_first = gain_first / norm_gains[:, 0].astype(f32)
-    grad_gains = jnp.concatenate([gain_first[:, None], sums[:, :3]], axis=1)
+    grad_gains = jnp.stack([gain_first, gain_heads[0], gain_heads[1], sums[:, 0]], axis=1)
     return (
         activations,
         input_grad.reshape(tokens.shape),
@@ -1888,7 +2124,7 @@
         grad_key,
         grad_value,
         grad_proj,
-        sums[:, 3 : 3 + experts],
+        sums[:, 1 : 1 + experts],
         grad_gate,
         grad_up,
         grad_down,

time: 895 us -> 833 us (0.931)
  Pallas kernels: 794 us -> 745 us
  other arithmetic: 43.8 us -> 30.5 us
    pallas_call x6 -> x5, Pallas kernels: 775 us -> 745 us  [call(): pl.pallas_call(kernel, out_shape=out_shapes, in_specs=in_specs, out_specs...]
    pallas_call x1 -> x0, Pallas kernels: 18.6 us -> none  [attend_back(): pl.pallas_call(functools.partial(attend_back_kernel, HEAD ** (-0.5)), gri...]
    unnamed x124 -> x79, local copies, waits for them, and re-layouts: 23.3 us -> 18.8 us
where the time goes in v5:
time: 833 us; the launch traced here: 823 us
  Pallas kernels  745 us (89%)
  other arithmetic  30.5 us (4%)
  local copies, waits for them, and re-layouts  28.3 us (3%)
  matrix products  17.5 us (2%)
    pallas_call x5, Pallas kernels, call(): pl.pallas_call(kernel, out_shape=out_shapes, in_specs=in_specs, out_specs...  745 us
    unnamed x79, local copies, waits for them, and re-layouts  18.8 us

profile of v5, /device:TPU:1, one launch (start us, length us, event | category | flops | bytes accessed | tf_op | source)
XLA Modules:
  0.0 823.1 jit_solution(6148212323189435094)
XLA Ops:
  0.7 1.6 multiply_reduce_fusion.1
  7.0 119.8 %start.1 = (bf16[2,8,128,2048]{3,2,1,0:T(8,128)(2,1)S(1)}, bf16[4,8,64,768]{3,2,1,0:T(8,128)(2,1)S(1)}, bf16[4,8,64,128]{3,2,1,0:T(8,128)(2,1)S(1)}, bf16[4,4,2,...) custom-call(bf16[2,128,2048]{2,1,0:T(8,128)(2,1)S(1)} %copy-done, ...), custom_call_target="tpu_custom_call" | custom-call | tf_op jit(solution)/shard_map/start/pallas_call | solution.py:25
  126.7 1.7 copy-done.1
  128.4 3.2 copy-done.2
  131.6 3.2 copy-done.6
  136.9 1.3 copy.76.row_ids
  138.3 108.7 %forward.1 = (bf16[2048,2048]{1,0:T(8,128)(2,1)}, bf16[2048,256]{1,0:T(8,128)(2,1)}, bf16[2048,256]{1,0:T(8,128)(2,1)}, bf16[2048,256]{1,0:T(8,128)(2,1)}, f32[2...) custom-call(bf16[2048,2048]{1,0:T(8,128)(2,1)} %bitcast.148, ...), custom_call_target="tpu_custom_call" | custom-call | tf_op jit(solution)/shard_map/forward/pallas_call | solution.py:25
  247.0 2.3 copy.77
  249.4 6.2 multiply_reduce_fusion.4
  257.9 231.4 %experts.1 = (bf16[4,2,128,2048]{3,2,1,0:T(8,128)(2,1)}, bf16[4,2,4,64,2048]{4,3,2,1,0:T(8,128)(2,1)}, bf16[4,2,4,64,2048]{4,3,2,1,0:T(8,128)(2,1)}, bf16[4,2,4,...) custom-call(bf16[2,128,2048]{2,1,0:T(8,128)(2,1)} %bitcast.157, ...), custom_call_target="tpu_custom_call" | custom-call | tf_op jit(solution)/shard_map/experts/pallas_call | solution.py:25
  489.4 3.4 convert_reduce_fusion
  493.1 2.3 multiply_reduce_fusion.2
  495.4 1.3 copy.88
  496.8 2.4 pad.9.clone
  499.2 2.2 fusion.19.grads
  501.5 7.1 convolution_convert_fusion
  508.6 108.9 %middle.1 = (bf16[2,8,128,256]{3,2,1,0:T(8,128)(2,1)}, bf16[4,64,2048]{2,1,0:T(8,128)(2,1)}, f32[2048,512]{1,0:T(8,128)}, f32[2048,512]{1,0:T(8,128)}, f32[512,2...) custom-call(bf16[2,128,2048]{2,1,0:T(8,128)(2,1)} %bitcast.177, ...), custom_call_target="tpu_custom_call" | custom-call | tf_op jit(solution)/shard_map/middle/pallas_call | solution.py:25
  617.5 2.8 convert_add_fusion.2
  620.3 176.7 %backward.1 = (f32[256,2048]{1,0:T(8,128)}, bf16[8,64,768]{2,1,0:T(8,128)(2,1)}, f32[8,64,128]{2,1,0:T(8,128)}, f32[8,2,1,256]{3,2,1,0:T(1,128)}, bf16[4,128,2048]{2,1,0:T(8,128)(2,1)}) custom-call(bf16[2048,256]{1,0:T(8,128)(2,1)} %get-tuple-element.66.queries, bf16[2048,256]{1,0:T(8,128)(2,1)} %get-tuple-element.67.keys, ...), custom_call_target="tpu_custom_call" | custom-call | tf_op jit(solution)/shard_map/backward/pallas_call | solution.py:25
  797.0 2.0 convert_add_fusion.1
  803.3 2.6 multiply_add_fusion
  811.5 2.9 add_bitcast_fusion.2
  815.9 2.9 add_bitcast_fusion.1
  820.2 2.7 add_bitcast_fusion
  (124 shorter events, 22.1 us)
Async XLA Ops:
  0.6 6.2 copy-start.31
  0.7 6.2 copy-start.30
  0.7 6.3 copy-start
  0.7 6.3 copy-start.4
  0.7 6.3 copy-start.5
  128.4 3.2 copy-start.2
  131.6 3.2 copy-start.6
  134.8 3.5 copy-start.3
  489.3 3.4 copy-start.34
  489.4 3.5 copy-start.13
  489.4 3.7 copy-start.8
  495.4 3.8 copy-start.14
  501.5 7.1 copy-start.21
  803.3 2.7 copy-start.35
  803.3 2.8 copy-start.33
  803.3 3.6 copy-start.28
  808.0 2.5 copy-start.24
  808.2 3.2 copy-start.20
  808.5 5.9 copy-start.26
  808.7 5.6 copy-start.27
  811.5 3.5 copy-start.19
  811.5 4.4 copy-start.23
  815.8 3.5 copy-start.18
  815.8 4.4 copy-start.22
  (13 other events, 23.8 us)

commit v6 on v5

--- a/solution.py
+++ b/solution.py
@@ -171,8 +171,19 @@
                     def _():
                         step(hop, landed, item, level, up).start()
 
+                if item == 0:
+                    for i, _, device in planes:
+                        output_copy(i, level, device).start()
                 if G > 1:
                     to_sibling(landed, item, level, hop if up else C - 1 + hop).start()
+
+    def output_copy(i, level, device):
+        mine = full_output.at[e, level, d]
+        return remote(mine, mine, fs.at[i, level], fr.at[i, level], device)
+
+    def output_sibling(i, level):
+        part = full_output.at[lax.rem(e + E - i, E), level, d]
+        return remote(part, part, gs.at[i, level], gr.at[i, level], sibling)
 
     for item in range(batches + 1):
 
@@ -205,26 +216,16 @@
             copy = remote(target.at[e], target.at[e], bs.at[j, i], br.at[j, i], device)
             copy.start()
             plane_copies.append(copy)
+    for i, _, device in planes:
+        output_copy(i, c, device).start()
     for hop in range(1, C):
-        relay(0, hop)
-
-    def output_copy(i, plane, device):
-        mine = full_output.at[e, :, d]
-        return remote(mine, mine, fs.at[i], fr.at[i], device)
-
-    def output_sibling(i):
-        part = full_output.at[lax.rem(e + E - i, E), :, d]
-        return remote(part, part, gs.at[i], gr.at[i], sibling)
-
-    for i, plane, device in planes:
-        output_copy(i, plane, device).start()
-    for hop in range(1, C):
-        for item in range(1, batches + 1):
+        for item in range(batches + 1):
             relay(item, hop)
-    for i, plane, device in planes:
-        output_copy(i, plane, device).wait_recv()
-        if G > 1:
-            output_sibling(i).start()
+    for level in range(C):
+        for i, _, device in planes:
+            output_copy(i, level, device).wait_recv()
+            if G > 1:
+                output_sibling(i, level).start()
 
     for item in range(batches + 1):
         if G > 1:
@@ -250,10 +251,11 @@
                     def _():
                         to_sibling(source_of(item), item, c, arrival).wait()
 
-    for i, plane, device in planes:
-        output_copy(i, plane, device).wait_send()
-        if G > 1:
-            output_sibling(i).wait()
+    for level in range(C):
+        for i, _, device in planes:
+            output_copy(i, level, device).wait_send()
+            if G > 1:
+                output_sibling(i, level).wait()
     for copy in weight_copies:
         copy.wait_send()
     for copy in plane_copies + small + local[3:]:
@@ -292,13 +294,14 @@
             DMA((count,)),
             DMA((C,)),
             DMA((C,)),
-            DMA((E,)),
-            DMA((E,)),
-            DMA((E,)),
-            DMA((E,)),
+            DMA((E, C)),
+            DMA((E, C)),
+            DMA((E, C)),
+            DMA((E, C)),
         ],
         1,
         "start",
+        vmem=62,
     )
 
 
@@ -467,17 +470,22 @@
             self.sums.at[n], self.out.at[n], self.sems[3].at[n], self.sems[4].at[n], to
         )
 
-    def begin(self):
-        for n in range(len(self.runs)):
+    def send(self, n):
+        if n < len(self.runs):
             for k in range(1, self.E):
                 self.back(n, k).start()
             self.own(n).start()
+
+    def begin(self):
+        self.send(0)
+        self.send(1)
 
     def combine(self, n):
         b, i = self.runs[n]
         for k in range(1, self.E):
             self.back(n, k).wait_recv()
         self.own(n).wait()
+        self.send(n + 2)
         cap, width = self.rows.shape[3:]
         picks = choose(self.slots[i, b], cap)
         for at in range(0, width, 512):
@@ -1109,9 +1117,15 @@
     C,
     G,
     runs,
-    rows,
+    parts,
+    resid,
+    factor,
+    upstream,
+    gain,
+    logit_grad,
+    router,
+    w_output,
     mixed,
-    grads,
     x,
     pair,
     gate_back,
@@ -1119,6 +1133,8 @@
     act,
     y_rows,
     slots,
+    resid_grad,
+    gain_grad,
     heads,
     proj,
     own_gate,
@@ -1128,6 +1144,9 @@
     other_up,
     other_down,
     out,
+    attn_grad,
+    stage,
+    blocks,
     hidden,
     wide,
     kept,
@@ -1140,6 +1159,7 @@
     hs,
     hr,
     hl,
+    block_sem,
     cs,
     cr,
     ps,
@@ -1156,36 +1176,30 @@
     e, c, d = position()
     me, peers = column_peers(E, C, G)
     planes, levels = plane_peers(E), level_peers(C)
-    batches = rows.shape[0]
-    size = heads.shape[3]
-    block, width = swap.shape[1:]
+    batches, run = parts.shape[1:3]
+    own, width = resid.shape
+    size = blocks.shape[1]
     step = wide.shape[2]
     half = own_gate.shape[1]
     sibling = (e, c, 1 - d)
     meet([device for _, _, device in peers] + [device for _, _, device in planes])
-
-    def head_part(b, index):
-        return rows.at[b, :, pl.ds(pl.multiple_of(index * size, size), size)]
-
-    head_copies = []
-    for b in range(batches):
-        for offset, index, device in peers:
-            head_copies.append(
-                remote(head_part(b, index), heads.at[b, me], hs.at[b, offset], hr.at[b, offset], device)
-            )
-        head_copies.append(pltpu.make_async_copy(head_part(b, me), heads.at[b, me], hl.at[b]))
-    for copy in head_copies:
-        copy.start()
-
     way_back = Return(E, C, runs, y_rows, slots, out, *return_scratch)
     way_back.begin()
 
+    turns = [index for _, index, _ in peers] + [me]
+
+    def block_copy(n):
+        at = pl.ds(pl.multiple_of(turns[n] * size, size), size)
+        return pltpu.make_async_copy(w_output.at[at], blocks.at[n % 2], block_sem.at[n % 2])
+
+    block_copy(0).start()
+    block_copy(1).start()
     hidden_copies = [
-        pltpu.make_async_copy(source, hidden.at[j], rs.at[j])
+        pltpu.make_async_copy(source, hidden.at[j % 2], rs.at[j % 2])
         for j, source in enumerate((gate_back, up_back, act))
     ]
-    for copy in hidden_copies:
-        copy.start()
+    hidden_copies[0].start()
+    hidden_copies[1].start()
     count = width // step
     sources = [x] * count + [pair] * count
 
@@ -1198,55 +1212,93 @@
     wide_copy(0).start()
     wide_copy(1).start()
 
-    def chip_copy(level):
-        return remote(swap.at[level], swapped.at[level], cs.at[level], cr.at[level], sibling)
-
-    def proj_part(core, level):
-        part = mixed[:, level, core].reshape(block, mixed.shape[4])
-        return jnp.dot(part, grads[...], preferred_element_type=f32)
-
-    def plane_copy(level, k, device):
+    total = jnp.zeros((own, 1), f32)
+    for at in range(0, width, 512):
+        lanes = pl.ds(at, 512)
+        grad = contract(logit_grad[...], router[lanes], (1, 1))
+        for level in range(C):
+            grad += parts[level, :, :, lanes].reshape(own, 512).astype(f32)
+        hat = resid[:, lanes] * factor[...]
+        gain_grad[:, lanes] = jnp.sum(grad * hat, axis=0, keepdims=True)
+        grad = grad * gain[:, lanes]
+        total += jnp.sum(grad * hat, axis=1, keepdims=True)
+        resid_grad[:, lanes] = grad
+    mean = total / width
+    for at in range(0, width, 512):
+        lanes = pl.ds(at, 512)
+        hat = resid[:, lanes] * factor[...]
+        grad = upstream[:, lanes].astype(f32) + factor[...] * (resid_grad[:, lanes] - hat * mean)
+        resid_grad[:, lanes] = grad
+        attn_grad[:, lanes] = grad.astype(bf16)
+
+    head_copies = []
+    for n in range(len(turns)):
+        block_copy(n).wait()
+        part = contract(attn_grad[...], blocks[n % 2], (1, 1))
+        stage[n] = part.astype(bf16).reshape(batches, run, size)
+        if n + 2 < len(turns):
+            block_copy(n + 2).start()
+        for b in range(batches):
+            if n < len(peers):
+                offset, _, device = peers[n]
+                copy = remote(
+                    stage.at[n, b], heads.at[b, me], hs.at[b, offset], hr.at[b, offset], device
+                )
+            else:
+                copy = pltpu.make_async_copy(stage.at[n, b], heads.at[b, me], hl.at[b])
+            copy.start()
+            head_copies.append(copy)
+
+    block = width // E
+
+    def chip_copy(plane):
+        return remote(swap.at[plane], swapped.at[plane], cs.at[plane], cr.at[plane], sibling)
+
+    def plane_copy(i, level):
+        plane = lax.rem(e + i, E)
         return remote(
-            chip.at[level, lax.rem(e + k, E)],
-            plane_parts.at[level, k],
-            ps.at[level, k],
-            pr.at[level, k],
-            device,
+            chip.at[plane, level],
+            plane_parts.at[i, level],
+            ps.at[i, level],
+            pr.at[i, level],
+            (plane, c, d),
         )
 
     def give(i, carry):
-        level = lax.rem(c + 1 + i, C)
-        swap[level] = proj_part(1 - d, level).astype(bf16)
-        chip_copy(level).start()
+        plane = lax.rem(e + 1 + i, E)
+        rows = pl.ds(pl.multiple_of(plane * block, block), block)
+        left = mixed[:, rows]
+        for at in range(0, width, 512):
+            lanes = pl.ds(at, 512)
+            part = contract(left, attn_grad[:, lanes], (0, 0)).astype(bf16)
+            part = part.reshape(C, G, block // (C * G), 512)
+            first, last = part[:, 0], part[:, G - 1]
+            chip[plane, :, :, lanes] = jnp.where(d == 0, first, last)
+            swap[plane, :, :, lanes] = jnp.where(d == 0, last, first)
+        chip_copy(plane).start()
         return carry
 
     def take(i, carry):
-        level = lax.rem(c + 1 + i, C)
-        part = proj_part(d, level)
-        chip_copy(level).wait_recv()
-        part = (part + swapped[level].astype(f32)).astype(bf16)
-        chip[level] = part.reshape(chip.shape[1:])
-        for k, _, device in planes:
-            plane_copy(level, k, device).start()
+        plane = lax.rem(e + 1 + i, E)
+        chip_copy(plane).wait_recv()
+        for at in range(0, width, 512):
+            lanes = pl.ds(at, 512)
+            part = chip[plane, :, :, lanes].astype(f32) + swapped[plane, :, :, lanes].astype(f32)
+            chip[plane, :, :, lanes] = part.astype(bf16)
         return carry
 
-    lax.fori_loop(0, C, give, 0)
-    lax.fori_loop(0, C, take, 0)
-
-    def level_copy(i, level):
-        return remote(level_part.at[level], proj.at[c], zs.at[i], zr.at[i], (e, level, d))
-
-    def plane_sum(i):
-        level = lax.rem(c + i, C)
-        total = chip[level, e].astype(f32)
-        for k, _, device in planes:
-            plane_copy(level, k, device).wait_recv()
-            total = total + plane_parts[level, k].astype(f32)
-        level_part[level] = total.astype(bf16)
-        if i > 0:
-            level_copy(i, level).start()
-        else:
-            proj[c] = level_part[c]
+    lax.fori_loop(0, E, give, 0)
+    lax.fori_loop(0, E, take, 0)
+    order = [lax.rem(c + i, C) for i in list(range(1, C)) + [0]]
+    levels_left = iter(order)
+
+    def level_send():
+        level = next(levels_left, None)
+        if level is not None:
+            for i in range(1, E):
+                plane_copy(i, level).start()
+
+    level_send()
 
     def keep_copy(j, at, place):
         target = (own_gate, own_up, own_down)[j]
@@ -1256,14 +1308,19 @@
     def send_copy(j, at, place):
         target = (other_gate, other_up, other_down)[j]
         where = target.at[:, pl.ds(at, step)] if j == 2 else target.at[pl.ds(at, step)]
-        return remote(sent.at[place], where, xs.at[place], xr.at[place], sibling)
-
+        return remote(sent.at[place % slots_sent], where, xs.at[place], xr.at[place], sibling)
+
+    slots_sent = sent.shape[0]
+    combine_at, combine_step, level_at = 0, 1, (2, 3, 4)
     kept_copies, sent_copies, after = [], [], {}
     for n in range(len(runs)):
-        after.setdefault(count + n * count // max(1, len(runs)), []).append(n)
-    for copy in hidden_copies:
-        copy.wait()
+        after.setdefault(combine_at + combine_step * n, []).append(n)
+    hidden_copies[0].wait()
+    hidden_copies[1].wait()
     for item in range(2 * count):
+        if item == count:
+            hidden_copies[2].start()
+            hidden_copies[2].wait()
         wide_copy(item).wait()
         at = (item % count) * step
         left = wide[item % 2]
@@ -1271,10 +1328,12 @@
             place = len(sent_copies)
 
             def product(core):
-                part = hidden[j, :, pl.ds(pl.multiple_of(core * half, half), half)]
+                part = hidden[j % 2, :, pl.ds(pl.multiple_of(core * half, half), half)]
                 return contract(part, left, (0, 0)) if j == 2 else contract(left, part, (0, 0))
 
-            sent[place] = product(1 - d).astype(bf16)
+            if place >= slots_sent:
+                sent_copies[place - slots_sent].wait_send()
+            sent[place % slots_sent] = product(1 - d).astype(bf16)
             copy = send_copy(j, at, place)
             copy.start()
             sent_copies.append(copy)
@@ -1288,44 +1347,105 @@
             wide_copy(item + 2).start()
         for n in after.get(item, ()):
             way_back.combine(n)
-    for i in list(range(1, C)) + [0]:
-        plane_sum(i)
+        if item in level_at:
+            level_send()
+    for _ in range(C):
+        level_send()
+
+    def level_copy(i, level):
+        return remote(level_part.at[level], proj.at[c], zs.at[i], zr.at[i], (e, level, d))
+
+    for i, level in zip(list(range(1, C)) + [0], order):
+        for k in range(1, E):
+            plane_copy(k, level).wait_recv()
+        total = chip[e, level].astype(f32)
+        for k in range(1, E):
+            total = total + plane_parts[k, level].astype(f32)
+        level_part[level] = total.astype(bf16)
+        if i > 0:
+            level_copy(i, level).start()
+        else:
+            proj[c] = level_part[c]
 
     for copy in kept_copies[-2:]:
         copy.wait()
-    for copy in sent_copies + head_copies:
+    for copy in sent_copies:
+        copy.wait_recv()
+    for copy in sent_copies[-slots_sent:]:
+        copy.wait_send()
+    for copy in head_copies:
         copy.wait()
     for i, level, _ in levels:
         level_copy(i, level).wait()
     way_back.end()
-
-    def done(level, carry):
-        chip_copy(level).wait_send()
-        for k, _, device in planes:
-            plane_copy(level, k, device).wait_send()
-        return carry
-
-    lax.fori_loop(0, C, done, 0)
+    for plane in range(E):
+        chip_copy(plane).wait_send()
+    for i in range(1, E):
+        for level in range(C):
+            plane_copy(i, level).wait_send()
 
 
 def middle(
-    E, C, G, runs, rows, mixed, grads, x, pair, gate_back, up_back, act, y_rows, slots, collective, name
+    E,
+    C,
+    G,
+    runs,
+    parts,
+    resid,
+    factor,
+    upstream,
+    gain,
+    logit_grad,
+    router,
+    w_output,
+    mixed,
+    x,
+    pair,
+    gate_back,
+    up_back,
+    act,
+    y_rows,
+    slots,
+    collective,
+    name,
 ):
-    batches, run, width = rows.shape
+    batches, run, width = parts.shape[1:]
+    own = resid.shape[0]
     count = C * G
-    part = mixed.shape[3]
-    block = E * part
+    size = width // count
+    block = width // E
+    part = block // count
     total, units = act.shape
     half = units // G
     step = min(512, width)
     items = 3 * (width // step)
     tall = (width, half)
     flat = (half, width)
+    by_plane = pltpu.VMEM((E, C, part, width), bf16)
     return call(
         functools.partial(middle_kernel, E, C, G, runs),
-        (rows, mixed, grads, x, pair, gate_back, up_back, act, y_rows, slots),
         (
-            jax.ShapeDtypeStruct((batches, count, run, width // count), bf16),
+            parts,
+            resid,
+            factor,
+            upstream,
+            gain,
+            logit_grad,
+            router,
+            w_output,
+            mixed,
+            x,
+            pair,
+            gate_back,
+            up_back,
+            act,
+            y_rows,
+            slots,
+        ),
+        (
+            jax.ShapeDtypeStruct((own, width), f32),
+            jax.ShapeDtypeStruct((1, width), f32),
+            jax.ShapeDtypeStruct((batches, count, run, size), bf16),
             jax.ShapeDtypeStruct((C, part, width), bf16),
             jax.ShapeDtypeStruct(tall, f32),
             jax.ShapeDtypeStruct(tall, f32),
@@ -1335,28 +1455,32 @@
             jax.ShapeDtypeStruct(flat, bf16),
             jax.ShapeDtypeStruct((len(runs), run, width), bf16),
         ),
-        [ANY, VMEM, VMEM] + [ANY] * 6 + [VMEM],
-        (ANY, VMEM) + (ANY,) * 7,
+        [VMEM] * 7 + [ANY, VMEM] + [ANY] * 6 + [VMEM],
+        (VMEM, VMEM, ANY, VMEM) + (ANY,) * 7,
         [
-            pltpu.VMEM((3, total, units), bf16),
+            pltpu.VMEM((own, width), bf16),
+            pltpu.VMEM((count, batches, run, size), bf16),
+            pltpu.VMEM((2, size, width), bf16),
+            pltpu.VMEM((2, total, units), bf16),
             pltpu.VMEM((2, total, step), bf16),
             pltpu.VMEM((2, step, half), f32),
-            pltpu.VMEM((items, step, half), bf16),
-            pltpu.VMEM((C, block, width), bf16),
-            pltpu.VMEM((C, block, width), bf16),
-            pltpu.VMEM((C, E, part, width), bf16),
-            pltpu.VMEM((C, E, part, width), bf16),
+            pltpu.VMEM((4, step, half), bf16),
+            by_plane,
+            by_plane,
+            by_plane,
+            by_plane,
             pltpu.VMEM((C, part, width), bf16),
             DMA((batches, count)),
             DMA((batches, count)),
             DMA((batches,)),
+            DMA((2,)),
+            DMA((E,)),
+            DMA((E,)),
+            DMA((E, C)),
+            DMA((E, C)),
             DMA((C,)),
             DMA((C,)),
-            DMA((C, E)),
-            DMA((C, E)),
-            DMA((C,)),
-            DMA((C,)),
-            DMA((3,)),
+            DMA((2,)),
             DMA((2,)),
             DMA((2,)),
             DMA((items,)),
@@ -1365,7 +1489,7 @@
         + Return.scratch(E, C, len(runs), run, width, y_rows.shape[3]),
         collective,
         name,
-        vmem=60,
+        vmem=62,
     )
 
 
@@ -1499,9 +1623,16 @@
         raw[pl.ds(b * count, count), :, value_lanes] = (
             value_sum[...].astype(bf16).reshape(count, run, HEAD)
         )
+        for q in range(min(beside, len(runs))):
+
+            @pl.when(n == batches * heads - beside + q)
+            def _():
+                way_back.combine(q)
+
         return carry
 
-    pending = iter(range(len(runs)))
+    beside = 2
+    pending = iter(range(beside, len(runs)))
 
     def carry_on(many):
         for _ in range(many):
@@ -1543,7 +1674,7 @@
     for copy in shares + gain_copies:
         copy.start()
     sum_parts[me] = sums[...]
-    carry_on(len(runs) // 2)
+    carry_on(1)
     for copy in shares:
         copy.wait()
     total = sum_parts[0]
@@ -1633,6 +1764,7 @@
     order = [C - 1, 0] + list(range(C - 2, 0, -1))
     for level in order:
         give(level)
+    carry_on(1)
 
     def plane_copy(item):
         plane = lax.rem(e + 1 + item, E)
@@ -2028,29 +2160,29 @@
     x, pair_grad, act, gate_pre_grad, up_pre_grad = (
         rows.reshape(slot_count, -1) for rows in (x, pair_grad, act, gate_pre_grad, up_pre_grad)
     )
-    upstream = cotangent.reshape(own, width).astype(f32)
     prob_grad = jnp.transpose(gate_grad[:, :, :, 0, :], (2, 3, 0, 1)).reshape(own, experts)
     logit_grad = router_probs * (
         prob_grad - jnp.sum(router_probs * prob_grad, axis=-1, keepdims=True)
     )
-    logit_grad = logit_grad.astype(bf16)
-    second_grad = jnp.sum(second_grad.astype(f32), axis=0).reshape(own, width)
-    second_grad = second_grad + contract(logit_grad, full_router, (1, 1))
-    gain_second = jnp.sum(second_grad * second_hat, axis=0)
-    resid_grad = upstream + norm_back(second_grad * gains[:, 3], second_hat, second_factor)
-    attn_grad = resid_grad.astype(bf16)
-    mixed_grad = contract(attn_grad, full_output, (1, 1)).astype(bf16)
+    logit_grad = jnp.pad(logit_grad.astype(bf16), ((0, 0), (0, small_width - experts)))
+    router_wide = jnp.pad(full_router, ((0, 0), (0, small_width - experts)))
 
     early = [(b, i) for b in range(batches // 2) for i in list(range(1, C)) + [0]]
     late = [(b, i) for b in range(batches // 2, batches) for i in list(range(1, C)) + [0]]
-    mixed_grad, grad_proj, *expert_grads, early_mixture = middle(
+    resid_grad, gain_second, mixed_grad, grad_proj, *expert_grads, early_mixture = middle(
         E,
         C,
         G,
         early,
-        mixed_grad.reshape(batches, run, width),
-        jnp.swapaxes(mixed_low, 0, 1).reshape(E, C, G, rows, own),
-        attn_grad,
+        second_grad,
+        resid,
+        second_factor,
+        cotangent.reshape(own, width),
+        jnp.swapaxes(gains[:, 3:4], 0, 1),
+        logit_grad,
+        router_wide,
+        full_output,
+        mixed_low,
         x,
         pair_grad,
         gate_pre_grad,
@@ -2065,10 +2197,8 @@
         (mine + other.astype(f32))[None] for mine, other in zip(expert_grads[:3], expert_grads[3:])
     )
     grad_proj = jnp.sum(grad_proj.astype(f32), axis=0)
-    sums = jnp.concatenate(
-        [gain_second[:, None], contract(second_low, logit_grad, (0, 0))], axis=1
-    )
-    sums = jnp.pad(sums, ((0, 0), (0, small_width - sums.shape[1])))
+    sums = contract(second_low, logit_grad, (0, 0))
+    sums = jnp.where(jnp.arange(small_width) == experts, gain_second.reshape(width, 1), sums)
     first_grad, grad_qkv, sums, gain_heads, late_mixture = run_backward(
         E,
         C,
@@ -2115,7 +2245,7 @@
         for w, grad in ((w_query, grad_query), (w_key, grad_key), (w_value, grad_value))
     )
     gain_first = gain_first / norm_gains[:, 0].astype(f32)
-    grad_gains = jnp.stack([gain_first, gain_heads[0], gain_heads[1], sums[:, 0]], axis=1)
+    grad_gains = jnp.stack([gain_first, gain_heads[0], gain_heads[1], sums[:, experts]], axis=1)
     return (
         activations,
         input_grad.reshape(tokens.shape),
@@ -2124,7 +2254,7 @@
         grad_key,
         grad_value,
         grad_proj,
-        sums[:, 1 : 1 + experts],
+        sums[:, :experts],
         grad_gate,
         grad_up,
         grad_down,

time: 833 us -> 810 us (0.972)
    unnamed x79 -> x59, local copies, waits for them, and re-layouts: 18.8 us -> 9.34 us
where the time goes in v6:
time: 810 us; the launch traced here: 806 us
  Pallas kernels  751 us (93%)
  other arithmetic  23.6 us (3%)
  local copies, waits for them, and re-layouts  20.5 us (3%)
  matrix products  9.51 us (1%)
    pallas_call x5, Pallas kernels, call(): pl.pallas_call(kernel, out_shape=out_shapes, in_specs=in_specs, out_specs...  751 us

profile of v6, /device:TPU:1, one launch (start us, length us, event | category | flops | bytes accessed | tf_op | source)
XLA Modules:
  0.0 806.0 jit_solution(9571423553775175775)
XLA Ops:
  1.6 1.0 fusion.3
  3.9 1.1 copy_bitcast_fusion
  5.0 1.0 copy.131
  6.0 0.9 maximum_bitcast_fusion.weights
  7.7 118.5 %start.1 = (bf16[2,8,128,2048]{3,2,1,0:T(8,128)(2,1)}, bf16[4,8,64,768]{3,2,1,0:T(8,128)(2,1)}, bf16[4,8,64,128]{3,2,1,0:T(8,128)(2,1)}, bf16[4,4,2,64,2048]{4,3...) custom-call(bf16[2,128,2048]{2,1,0:T(8,128)(2,1)} %tokens.1, ...), custom_call_target="tpu_custom_call" | custom-call | tf_op jit(solution)/shard_map/start/pallas_call | solution.py:25
  126.2 1.3 copy.119
  128.7 2.0 copy.104.row_ids
  130.7 1.3 copy.103
  132.0 113.4 %forward.1 = (bf16[2048,2048]{1,0:T(8,128)(2,1)}, bf16[2048,256]{1,0:T(8,128)(2,1)}, bf16[2048,256]{1,0:T(8,128)(2,1)}, bf16[2048,256]{1,0:T(8,128)(2,1)}, f32[2...) custom-call(bf16[2048,2048]{1,0:T(8,128)(2,1)} %bitcast.132, ...), custom_call_target="tpu_custom_call" | custom-call | tf_op jit(solution)/shard_map/forward/pallas_call | solution.py:25
  245.4 6.2 multiply_reduce_fusion.2
  251.9 1.1 copy-done.7
  254.9 231.8 %experts.1 = (bf16[4,2,128,2048]{3,2,1,0:T(8,128)(2,1)}, bf16[4,2,4,64,2048]{4,3,2,1,0:T(8,128)(2,1)}, bf16[4,2,4,64,2048]{4,3,2,1,0:T(8,128)(2,1)}, bf16[4,2,4,...) custom-call(bf16[2,128,2048]{2,1,0:T(8,128)(2,1)} %bitcast.128, ...), custom_call_target="tpu_custom_call" | custom-call | tf_op jit(solution)/shard_map/experts/pallas_call | solution.py:25
  490.5 103.2 %middle.1 = (f32[256,2048]{1,0:T(8,128)}, f32[1,2048]{1,0:T(1,128)}, bf16[2,8,128,256]{3,2,1,0:T(8,128)(2,1)}, bf16[4,64,2048]{2,1,0:T(8,128)(2,1)}, f32[2048,51...) custom-call(bf16[4,2,128,2048]{3,2,1,0:T(8,128)(2,1)} %get-tuple-ele, ...), custom_call_target="tpu_custom_call" | custom-call | tf_op jit(solution)/shard_map/middle/pallas_call | solution.py:25
  593.7 5.9 add_bitcast_fusion
  599.6 2.9 add_bitcast_fusion.1
  603.0 0.9 copy-done.11
  604.0 2.9 add_bitcast_fusion.2
  606.9 1.6 convolution_select_fusion
  608.5 184.2 %backward.1 = (f32[256,2048]{1,0:T(8,128)}, bf16[8,64,768]{2,1,0:T(8,128)(2,1)}, f32[8,64,128]{2,1,0:T(8,128)}, f32[8,2,1,256]{3,2,1,0:T(1,128)}, bf16[4,128,2048]{2,1,0:T(8,128)(2,1)}) custom-call(bf16[2048,256]{1,0:T(8,128)(2,1)} %get-tuple-element.68.queries, bf16[2048,256]{1,0:T(8,128)(2,1)} %get-tuple-element.69.keys, ...), custom_call_target="tpu_custom_call" | custom-call | tf_op jit(solution)/shard_map/backward/pallas_call | solution.py:25
  792.7 1.3 convert_bitcast_fusion
  798.7 1.9 multiply_add_fusion
  801.0 1.2 copy-done.13
  803.0 1.2 fusion
  804.9 0.9 convert_reduce_fusion
  (104 shorter events, 17.1 us)
Async XLA Ops:
  0.6 6.3 copy-start.26
  0.7 6.3 copy-start.25
  132.0 113.4 %copy-start.4 = (bf16[2,128,2048]{2,1,0:T(8,128)(2,1)S(1)}, bf16[2,128,2048]{2,1,0:T(8,128)(2,1)}, u32[]{:S(2)}) copy-start(bf16[2,128,2048]{2,1,0:T(8,128)(2,1)} %tokens.1) | copy-start | bytes 3145732
  251.6 2.0 copy-start
  251.6 1.4 copy-start.7
  253.0 1.8 copy-start.2
  593.6 5.9 copy-start.9
  593.7 5.9 copy-start.12
  599.6 3.5 copy-start.8
  599.6 4.4 copy-start.11
  604.0 2.9 copy-start.3
  604.0 2.9 copy-start.24
  794.1 1.0 copy-start.21
  794.2 1.4 copy-start.15
  794.2 1.2 copy-start.19
  794.9 1.3 copy-start.22
  795.1 1.3 copy-start.23
  795.1 2.0 copy-start.5
  795.2 2.3 copy-start.6
  797.1 1.7 copy-start.10
  798.7 1.9 copy-start.14
  800.6 1.6 copy-start.13
  801.0 2.0 copy-start.1
  802.9 1.9 copy-start.18
  (3 other events, 2.5 us)

commit v7 on v6

--- a/solution.py
+++ b/solution.py
@@ -356,28 +356,30 @@
             return jnp.logical_and(i <= self.c, self.c < self.C - 1)
         return jnp.logical_and(lax.rem(self.C - i, self.C) + self.c < self.C, self.c > 0)
 
-    def begin(self):
+    def pass_on(self, far, b):
+        for way in range(2):
+            i = far if way == 0 else lax.rem(self.C - far, self.C)
+            here = (far <= self.c) if way == 0 else (far + self.c < self.C)
+
+            @pl.when(jnp.logical_and(here, self.onward(i, way)))
+            def _():
+                self.hop(b, i, way).start()
+
+    def begin(self, count):
         for b in range(self.batches):
             self.own(b).start()
         for b in range(self.batches):
             self.own(b).wait()
-            for way in range(2):
-
-                @pl.when(self.onward(0, way))
-                def _():
-                    self.hop(b, 0, way).start()
-
-    def relay(self, far, b):
+        for b in range(count):
+            self.pass_on(0, b)
+
+    def receive(self, far, b):
         for way in range(2):
             i = far if way == 0 else self.C - far
 
             @pl.when((far <= self.c) if way == 0 else (far + self.c < self.C))
             def _():
                 self.arrival(b, i).wait_recv()
-
-                @pl.when(self.onward(i, way))
-                def _():
-                    self.hop(b, i, way).start()
 
     def hops_sent(self, b, i):
         for way in range(2):
@@ -592,12 +594,13 @@
                 flow.crossed(*before)
                 flow.stay(*before).wait()
             if n >= batches:
-                flow.relay(n // batches, n % batches)
+                flow.receive(n // batches, n % batches)
+                flow.pass_on(n // batches, n % batches)
             flow.compact(n, *chunk_of(n))
 
     load(0).start()
     load(1).start()
-    flow.begin()
+    flow.begin(batches)
     carry_on(batches)
     ones = jnp.ones((8, size), f32)
 
@@ -777,7 +780,7 @@
         ],
         collective,
         name,
-        vmem=56,
+        vmem=46,
     )
 
 
@@ -788,9 +791,9 @@
     u_in,
     slots,
     gates,
-    w_gate,
-    w_up,
-    w_down,
+    gate_in,
+    up_in,
+    down_in,
     out,
     x_out,
     y_out,
@@ -799,6 +802,9 @@
     gate_back_out,
     up_back_out,
     scalars_out,
+    w_gate,
+    w_up,
+    w_down,
     table,
     scalars,
     landed,
@@ -831,6 +837,7 @@
     ks,
     loads,
     stores,
+    weight_sem,
 ):
     e, c, d = position()
     batches, run, width = rows_x.shape
@@ -888,7 +895,16 @@
         target = (pair_out, act_out, gate_back_out, up_back_out, y_out)[j]
         return pltpu.make_async_copy(source, target.at[i, b], stores.at[j])
 
-    flow.begin()
+    weight_copies = [
+        pltpu.make_async_copy(source, target, weight_sem.at[j])
+        for j, (source, target) in enumerate(
+            ((gate_in, w_gate), (up_in, w_up), (down_in, w_down))
+        )
+    ]
+    for copy in weight_copies:
+        copy.start()
+
+    flow.begin(1)
     small = [
         remote(gates.at[device[0], device[1]], table.at[k, i], gs.at[k, i], gr.at[k, i], device)
         for k, i, device in ahead
@@ -910,6 +926,11 @@
         flow.arrived(n, b, i)
         flow.stay(n, b, i).wait()
         load(0, b, i).start()
+
+        @pl.when(n == 0)
+        def _():
+            for copy in weight_copies:
+                copy.wait()
 
         @pl.when(n > 0)
         def _():
@@ -995,7 +1016,8 @@
     def step(s, carry):
         @pl.when(jnp.logical_and(s > 0, s <= batches * (C - 1)))
         def _():
-            flow.relay(*far_of(s))
+            flow.receive(*far_of(s))
+            flow.pass_on(s // batches, lax.rem(s, batches))
 
         @pl.when(s < chunks)
         def _():
@@ -1075,9 +1097,12 @@
             hidden,
             jax.ShapeDtypeStruct((E, C, batches, 1, run), f32),
         ),
-        [ANY, ANY, VMEM, VMEM, VMEM, VMEM, VMEM],
+        [ANY, ANY, VMEM, VMEM, ANY, ANY, ANY],
         (ANY,) * 7 + (VMEM,),
         [
+            pltpu.VMEM(w_gate.shape, bf16),
+            pltpu.VMEM(w_up.shape, bf16),
+            pltpu.VMEM(w_down.shape, bf16),
             pltpu.VMEM(gates.shape, f32),
             pltpu.VMEM((E, C, batches, 1, run), f32),
         ]
@@ -1105,6 +1130,7 @@
             DMA((batches,)),
             DMA((2,)),
             DMA((5,)),
+            DMA((3,)),
         ],
         collective,
         name,
@@ -1852,10 +1878,10 @@
 
     for copy in small_copies:
         copy.wait_recv()
-    total = small[e]
+    total = small[e].astype(f32)
     for i in range(1, E):
-        total = total + small_parts[i]
-    small_sum[...] = total
+        total = total + small_parts[i].astype(f32)
+    small_sum[...] = total.astype(bf16)
     for offset, index, device in peers:
         small_copy(offset, index, device).start()
         row_copy(offset, index, device).start()
@@ -1970,7 +1996,7 @@
         (
             jax.ShapeDtypeStruct((rows, width), f32),
             jax.ShapeDtypeStruct((count, share, columns), bf16),
-            jax.ShapeDtypeStruct((count, share, lanes), f32),
+            jax.ShapeDtypeStruct((count, share, lanes), bf16),
             jax.ShapeDtypeStruct((count, 2, 1, size), f32),
             jax.ShapeDtypeStruct((len(runs), run, width), bf16),
         ),
@@ -1986,8 +2012,8 @@
             pltpu.VMEM((count, 2, 1, every), f32),
             pltpu.VMEM((2, 1, size), f32),
             pltpu.VMEM((E, 2, 1, size), f32),
-            pltpu.VMEM((E, block, lanes), f32),
-            pltpu.VMEM((block, lanes), f32),
+            pltpu.VMEM((E, block, lanes), bf16),
+            pltpu.VMEM((block, lanes), bf16),
             by_level,
             by_level,
             by_level,
@@ -2199,6 +2225,7 @@
     grad_proj = jnp.sum(grad_proj.astype(f32), axis=0)
     sums = contract(second_low, logit_grad, (0, 0))
     sums = jnp.where(jnp.arange(small_width) == experts, gain_second.reshape(width, 1), sums)
+    sums = sums.astype(bf16)
     first_grad, grad_qkv, sums, gain_heads, late_mixture = run_backward(
         E,
         C,
@@ -2231,7 +2258,7 @@
             mixture[b] = mixture[b] + parts[n].astype(f32)
     mixture = jnp.stack(mixture)
     activations = (resid.reshape(tokens.shape) + mixture).astype(bf16)
-    sums = jnp.sum(sums, axis=0)
+    sums = jnp.sum(sums.astype(f32), axis=0)
     first_factor = rms_factor(inputs)
     first_hat = inputs * first_factor
     input_grad = resid_grad + norm_back(first_grad * gains[:, 0], first_hat, first_factor)

time: 810 us -> 785 us (0.969)
  Pallas kernels: 751 us -> 730 us
    pallas_call x5, Pallas kernels: 751 us -> 730 us  [call(): pl.pallas_call(kernel, out_shape=out_shapes, in_specs=in_specs, out_specs...]
where the time goes in v7:
time: 785 us; the launch traced here: 781 us
  Pallas kernels  730 us (93%)
  other arithmetic  23.6 us (3%)
  local copies, waits for them, and re-layouts  20.4 us (3%)
    pallas_call x5, Pallas kernels, call(): pl.pallas_call(kernel, out_shape=out_shapes, in_specs=in_specs, out_specs...  730 us

profile of v7, /device:TPU:1, one launch (start us, length us, event | category | flops | bytes accessed | tf_op | source)
XLA Modules:
  0.0 780.8 jit_solution(16229371298880101966)
XLA Ops:
  1.6 1.0 fusion.4
  3.9 1.1 copy_bitcast_fusion
  5.0 1.0 copy.131
  6.0 0.9 maximum_bitcast_fusion.weights
  7.7 118.5 %start.1 = (bf16[2,8,128,2048]{3,2,1,0:T(8,128)(2,1)}, bf16[4,8,64,768]{3,2,1,0:T(8,128)(2,1)}, bf16[4,8,64,128]{3,2,1,0:T(8,128)(2,1)}, bf16[4,4,2,64,2048]{4,3...) custom-call(bf16[2,128,2048]{2,1,0:T(8,128)(2,1)} %tokens.1, ...), custom_call_target="tpu_custom_call" | custom-call | tf_op jit(solution)/shard_map/start/pallas_call | solution.py:25
  126.2 1.3 copy.119
  128.1 1.1 copy.104.row_ids
  129.9 1.2 copy-done.1
  131.8 111.2 %forward.1 = (bf16[2048,2048]{1,0:T(8,128)(2,1)}, bf16[2048,256]{1,0:T(8,128)(2,1)S(1)}, bf16[2048,256]{1,0:T(8,128)(2,1)S(1)}, bf16[2048,256]{1,0:T(8,128)(2,1)...) custom-call(bf16[2048,2048]{1,0:T(8,128)(2,1)} %bitcast.137, ...), custom_call_target="tpu_custom_call" | custom-call | tf_op jit(solution)/shard_map/forward/pallas_call | solution.py:25
  243.2 2.6 multiply_reduce_fusion.2
  246.1 1.1 copy-done.18
  249.0 220.4 %experts.1 = (bf16[4,2,128,2048]{3,2,1,0:T(8,128)(2,1)}, bf16[4,2,4,64,2048]{4,3,2,1,0:T(8,128)(2,1)}, bf16[4,2,4,64,2048]{4,3,2,1,0:T(8,128)(2,1)}, bf16[4,2,4,...) custom-call(bf16[2,128,2048]{2,1,0:T(8,128)(2,1)} %bitcast.136, ...), custom_call_target="tpu_custom_call" | custom-call | tf_op jit(solution)/shard_map/experts/pallas_call | solution.py:25
  473.2 103.1 %middle.1 = (f32[256,2048]{1,0:T(8,128)}, f32[1,2048]{1,0:T(1,128)}, bf16[2,8,128,256]{3,2,1,0:T(8,128)(2,1)}, bf16[4,64,2048]{2,1,0:T(8,128)(2,1)}, f32[2048,51...) custom-call(bf16[4,2,128,2048]{3,2,1,0:T(8,128)(2,1)} %get-tuple-ele, ...), custom_call_target="tpu_custom_call" | custom-call | tf_op jit(solution)/shard_map/middle/pallas_call | solution.py:25
  576.4 5.9 add_bitcast_fusion
  582.3 2.9 add_bitcast_fusion.1
  585.7 0.9 copy-done.22
  586.7 2.9 add_bitcast_fusion.2
  589.6 1.4 fusion
  591.0 176.4 %backward.1 = (f32[256,2048]{1,0:T(8,128)}, bf16[8,64,768]{2,1,0:T(8,128)(2,1)}, bf16[8,64,128]{2,1,0:T(8,128)(2,1)}, f32[8,2,1,256]{3,2,1,0:T(1,128)}, bf16[4,128,2048]{2,1,0:T(8,128)(2,1)}) custom-call(bf16[2048,256]{1,0:T(8,128)(2,1)} %copy-done.2, bf16[2048,256]{1,0:T(8,128)(2,1)} %copy-done.3, bf16[2048,256]{1,0:T(8,128)(2,1)} %copy-done.4, ...), custom_call_target="tpu_custom_call" | custom-call | tf_op jit(solution)/shard_map/backward/pallas_call | solution.py:25
  767.4 1.3 convert_bitcast_fusion
  773.5 1.9 multiply_add_fusion
  775.7 1.2 copy-done.24
  777.7 1.2 fusion.1
  779.6 0.9 convert_reduce_fusion
  (126 shorter events, 18.0 us)
Async XLA Ops:
  0.6 6.3 copy-start.36
  0.7 6.3 copy-start.35
  127.5 115.5 %copy-start.8 = (f32[2,256]{1,0:T(2,128)}, f32[2,256]{1,0:T(2,128)S(1)}, u32[]{:S(2)}) copy-start(f32[2,256]{1,0:T(2,128)S(1)} %dynamic-slice_bitcast_fusion.head_gains) | copy-start | bytes 6148
  129.2 113.9 %copy-start = (s32[2,1024,1]{2,1,0:T(8,128)}, s32[2,1024,1]{2,1,0:T(8,128)S(1)}, u32[]{:S(2)}) copy-start(s32[2,1024,1]{2,1,0:T(8,128)S(1)} %copy.104.row_ids) | copy-start | bytes 24580
  129.9 113.2 %copy-start.7 = (s32[2,8,128]{2,1,0:T(8,128)}, s32[2,8,128]{2,1,0:T(8,128)S(1)}, u32[]{:S(2)}) copy-start(s32[2,8,128]{2,1,0:T(8,128)S(1)} %copy.103) | copy-start | bytes 24580
  131.8 111.3 %copy-start.12 = (bf16[2,128,2048]{2,1,0:T(8,128)(2,1)S(1)}, bf16[2,128,2048]{2,1,0:T(8,128)(2,1)}, u32[]{:S(2)}) copy-start(bf16[2,128,2048]{2,1,0:T(8,128)(2,1)} %tokens.1) | copy-start | bytes 3145732
  131.8 111.3 %copy-start.17 = (bf16[4,4,2,64,2048]{4,3,2,1,0:T(8,128)(2,1)S(1)}, bf16[4,4,2,64,2048]{4,3,2,1,0:T(8,128)(2,1)}, u32[]{:S(2)}) copy-start(bf16[4,4,2,64,2048]{4,3,2,1,0:T(8,128)(2,1)} %get-tuple-element.57) | copy-start | bytes 25165828
  243.1 2.7 copy-start.2
  243.1 2.6 copy-start.3
  243.1 2.6 copy-start.4
  243.1 2.6 copy-start.5
  243.1 2.6 copy-start.9
  245.8 2.1 copy-start.10
  576.4 5.9 copy-start.20
  576.4 5.9 copy-start.23
  582.3 3.5 copy-start.19
  582.3 4.4 copy-start.22
  586.7 2.9 copy-start.15
  586.7 2.9 copy-start.37
  769.8 2.0 copy-start.13
  769.9 2.3 copy-start.16
  773.5 1.9 copy-start.25
  775.7 2.0 copy-start.11
  777.7 1.9 copy-start.29
  (14 other events, 17.1 us)

commit v8 on v7

--- a/solution.py
+++ b/solution.py
@@ -478,10 +478,6 @@
                 self.back(n, k).start()
             self.own(n).start()
 
-    def begin(self):
-        self.send(0)
-        self.send(1)
-
     def combine(self, n):
         b, i = self.runs[n]
         for k in range(1, self.E):
@@ -528,15 +524,20 @@
     slots,
     upstream,
     normed,
+    queries_out,
+    keys_out,
+    values_out,
+    query_hat_out,
+    key_hat_out,
+    log_total,
+    factors,
+    mixed,
+    u_out,
     queries,
     keys,
     values,
     query_hat,
     key_hat,
-    log_total,
-    factors,
-    mixed,
-    u_out,
     raw,
     low,
     squares,
@@ -557,6 +558,7 @@
     ms,
     mr,
     ml,
+    out_sem,
 ):
     me, peers = column_peers(E, C, G)
     planes = plane_peers(E)
@@ -678,6 +680,20 @@
         return carry
 
     lax.fori_loop(0, blocks, scaled, 0)
+    out_copies = [
+        pltpu.make_async_copy(source, target, out_sem.at[j])
+        for j, (source, target) in enumerate(
+            (
+                (queries, queries_out),
+                (keys, keys_out),
+                (values, values_out),
+                (query_hat, query_hat_out),
+                (key_hat, key_hat_out),
+            )
+        )
+    ]
+    for copy in out_copies:
+        copy.start()
     carry_on(1)
 
     def mixed_copy(b, offset, index, device):
@@ -717,6 +733,8 @@
         carry_on(1)
     carry_on(flow.chunks)
 
+    for copy in out_copies:
+        copy.wait()
     for copy in shares:
         copy.wait_send()
     for j in (blocks - 2, blocks - 1):
@@ -760,8 +778,13 @@
             jax.ShapeDtypeStruct((C, batches, E, cap, width), bf16),
         ),
         [ANY] + [VMEM] * 6 + [ANY],
-        (ANY,) + (VMEM,) * 7 + (ANY, ANY),
+        (ANY,) * 6 + (VMEM,) * 2 + (ANY, ANY),
         [
+            pltpu.VMEM(low.shape, bf16),
+            pltpu.VMEM(low.shape, bf16),
+            pltpu.VMEM(low.shape, bf16),
+            pltpu.VMEM(wide.shape, f32),
+            pltpu.VMEM(wide.shape, f32),
             pltpu.VMEM((2, block, width), bf16),
             pltpu.VMEM((2, block, width), bf16),
             pltpu.VMEM((2, 1, every), f32),
@@ -777,6 +800,7 @@
             DMA((batches, count)),
             DMA((batches, count)),
             DMA((batches,)),
+            DMA((5,)),
         ],
         collective,
         name,
@@ -1210,7 +1234,7 @@
     sibling = (e, c, 1 - d)
     meet([device for _, _, device in peers] + [device for _, _, device in planes])
     way_back = Return(E, C, runs, y_rows, slots, out, *return_scratch)
-    way_back.begin()
+    way_back.send(0)
 
     turns = [index for _, index, _ in peers] + [me]
 
@@ -1256,6 +1280,8 @@
         grad = upstream[:, lanes].astype(f32) + factor[...] * (resid_grad[:, lanes] - hat * mean)
         resid_grad[:, lanes] = grad
         attn_grad[:, lanes] = grad.astype(bf16)
+
+    way_back.send(1)
 
     head_copies = []
     for n in range(len(turns)):
@@ -1531,13 +1557,13 @@
     row_ids,
     key_ids,
     log_total,
-    query_hat,
-    key_hat,
+    query_hat_in,
+    key_hat_in,
     factors,
     head_gains,
     y_rows,
     slots,
-    w_qkv,
+    w_qkv_in,
     normed,
     small,
     first,
@@ -1545,6 +1571,9 @@
     out_small,
     out_gains,
     out,
+    query_hat,
+    key_hat,
+    w_qkv,
     raw,
     query_grad,
     key_grad,
@@ -1583,6 +1612,7 @@
     hr,
     gs,
     gr,
+    in_sem,
     *return_scratch,
 ):
     e, c, d = position()
@@ -1619,7 +1649,15 @@
         copy.start()
 
     way_back = Return(E, C, runs, y_rows, slots, out, *return_scratch)
-    way_back.begin()
+    way_back.send(0)
+    in_copies = [
+        pltpu.make_async_copy(source, target, in_sem.at[j])
+        for j, (source, target) in enumerate(
+            ((query_hat_in, query_hat), (key_hat_in, key_hat), (w_qkv_in, w_qkv))
+        )
+    ]
+    for copy in in_copies:
+        copy.start()
     heads = size // HEAD
 
     def head_back(n, carry):
@@ -1649,16 +1687,20 @@
         raw[pl.ds(b * count, count), :, value_lanes] = (
             value_sum[...].astype(bf16).reshape(count, run, HEAD)
         )
-        for q in range(min(beside, len(runs))):
-
-            @pl.when(n == batches * heads - beside + q)
+        @pl.when(n == 0)
+        def _():
+            way_back.send(1)
+
+        for q, turn in enumerate(beside):
+
+            @pl.when(n == turn)
             def _():
                 way_back.combine(q)
 
         return carry
 
-    beside = 2
-    pending = iter(range(beside, len(runs)))
+    beside = (1, 3)[: len(runs)]
+    pending = iter(range(len(beside), len(runs)))
 
     def carry_on(many):
         for _ in range(many):
@@ -1667,6 +1709,8 @@
                 way_back.combine(n)
 
     lax.fori_loop(0, batches * heads, head_back, 0)
+    for copy in in_copies:
+        copy.wait()
 
     chunk = min(2 * run, every)
     per_chunk = chunk // run
@@ -2000,9 +2044,12 @@
             jax.ShapeDtypeStruct((count, 2, 1, size), f32),
             jax.ShapeDtypeStruct((len(runs), run, width), bf16),
         ),
-        [VMEM] * 11 + [ANY, VMEM, VMEM, ANY, VMEM],
+        [VMEM] * 7 + [ANY, ANY, VMEM, VMEM, ANY, VMEM, ANY, ANY, VMEM],
         (VMEM, VMEM, VMEM, VMEM, ANY),
         [
+            wide,
+            wide,
+            pltpu.VMEM(w_qkv.shape, bf16),
             pltpu.VMEM((batches * count, run, columns), bf16),
             wide,
             wide,
@@ -2041,6 +2088,7 @@
             DMA((E,)),
             DMA((count,)),
             DMA((count,)),
+            DMA((3,)),
         ]
         + Return.scratch(E, C, len(runs), run, width, y_rows.shape[3]),
         collective,

time: 785 us -> 781 us (level)
  no operation moved by 1% of the time
where the time goes in v8:
time: 781 us; the launch traced here: 777 us
  Pallas kernels  726 us (93%)
  other arithmetic  23.6 us (3%)
  local copies, waits for them, and re-layouts  20.4 us (3%)
    pallas_call x5, Pallas kernels, call(): pl.pallas_call(kernel, out_shape=out_shapes, in_specs=in_specs, out_specs...  726 us

profile of v8, /device:TPU:1, one launch (start us, length us, event | category | flops | bytes accessed | tf_op | source)
XLA Modules:
  0.0 777.2 jit_solution(4240448065977752191)
XLA Ops:
  1.6 1.0 fusion.4
  3.9 1.1 copy_bitcast_fusion
  5.0 1.0 copy.131
  6.0 0.9 maximum_bitcast_fusion.weights
  7.7 118.5 %start.1 = (bf16[2,8,128,2048]{3,2,1,0:T(8,128)(2,1)}, bf16[4,8,64,768]{3,2,1,0:T(8,128)(2,1)}, bf16[4,8,64,128]{3,2,1,0:T(8,128)(2,1)}, bf16[4,4,2,64,2048]{4,3...) custom-call(bf16[2,128,2048]{2,1,0:T(8,128)(2,1)} %tokens.1, ...), custom_call_target="tpu_custom_call" | custom-call | tf_op jit(solution)/shard_map/start/pallas_call | solution.py:25
  126.2 1.3 copy.119
  128.1 1.1 copy.104.row_ids
  129.9 1.2 copy-done.1
  131.8 109.8 %forward.1 = (bf16[2048,2048]{1,0:T(8,128)(2,1)}, bf16[2048,256]{1,0:T(8,128)(2,1)S(1)}, bf16[2048,256]{1,0:T(8,128)(2,1)S(1)}, bf16[2048,256]{1,0:T(8,128)(2,1)...) custom-call(bf16[2048,2048]{1,0:T(8,128)(2,1)} %bitcast.137, ...), custom_call_target="tpu_custom_call" | custom-call | tf_op jit(solution)/shard_map/forward/pallas_call | solution.py:25
  241.8 2.6 multiply_reduce_fusion.2
  244.7 1.1 copy-done.18
  247.7 220.5 %experts.1 = (bf16[4,2,128,2048]{3,2,1,0:T(8,128)(2,1)}, bf16[4,2,4,64,2048]{4,3,2,1,0:T(8,128)(2,1)}, bf16[4,2,4,64,2048]{4,3,2,1,0:T(8,128)(2,1)}, bf16[4,2,4,...) custom-call(bf16[2,128,2048]{2,1,0:T(8,128)(2,1)} %bitcast.136, ...), custom_call_target="tpu_custom_call" | custom-call | tf_op jit(solution)/shard_map/experts/pallas_call | solution.py:25
  471.9 103.1 %middle.1 = (f32[256,2048]{1,0:T(8,128)}, f32[1,2048]{1,0:T(1,128)}, bf16[2,8,128,256]{3,2,1,0:T(8,128)(2,1)}, bf16[4,64,2048]{2,1,0:T(8,128)(2,1)}, f32[2048,51...) custom-call(bf16[4,2,128,2048]{3,2,1,0:T(8,128)(2,1)} %get-tuple-ele, ...), custom_call_target="tpu_custom_call" | custom-call | tf_op jit(solution)/shard_map/middle/pallas_call | solution.py:25
  575.0 5.9 add_bitcast_fusion
  580.9 2.9 add_bitcast_fusion.1
  584.4 0.9 copy-done.22
  585.3 2.9 add_bitcast_fusion.2
  588.2 1.4 fusion
  589.6 174.2 %backward.1 = (f32[256,2048]{1,0:T(8,128)}, bf16[8,64,768]{2,1,0:T(8,128)(2,1)}, bf16[8,64,128]{2,1,0:T(8,128)(2,1)}, f32[8,2,1,256]{3,2,1,0:T(1,128)}, bf16[4,128,2048]{2,1,0:T(8,128)(2,1)}) custom-call(bf16[2048,256]{1,0:T(8,128)(2,1)} %copy-done.2, bf16[2048,256]{1,0:T(8,128)(2,1)} %copy-done.3, bf16[2048,256]{1,0:T(8,128)(2,1)} %copy-done.4, ...), custom_call_target="tpu_custom_call" | custom-call | tf_op jit(solution)/shard_map/backward/pallas_call | solution.py:25
  763.8 1.3 convert_bitcast_fusion
  769.9 1.9 multiply_add_fusion
  772.1 1.2 copy-done.24
  774.1 1.2 fusion.1
  776.0 0.9 convert_reduce_fusion
  (126 shorter events, 18.0 us)
Async XLA Ops:
  0.6 6.3 copy-start.36
  0.7 6.3 copy-start.35
  127.5 114.2 %copy-start.8 = (f32[2,256]{1,0:T(2,128)}, f32[2,256]{1,0:T(2,128)S(1)}, u32[]{:S(2)}) copy-start(f32[2,256]{1,0:T(2,128)S(1)} %dynamic-slice_bitcast_fusion.head_gains) | copy-start | bytes 6148
  129.2 112.5 %copy-start = (s32[2,1024,1]{2,1,0:T(8,128)}, s32[2,1024,1]{2,1,0:T(8,128)S(1)}, u32[]{:S(2)}) copy-start(s32[2,1024,1]{2,1,0:T(8,128)S(1)} %copy.104.row_ids) | copy-start | bytes 24580
  129.9 111.8 %copy-start.7 = (s32[2,8,128]{2,1,0:T(8,128)}, s32[2,8,128]{2,1,0:T(8,128)S(1)}, u32[]{:S(2)}) copy-start(s32[2,8,128]{2,1,0:T(8,128)S(1)} %copy.103) | copy-start | bytes 24580
  131.8 109.9 %copy-start.12 = (bf16[2,128,2048]{2,1,0:T(8,128)(2,1)S(1)}, bf16[2,128,2048]{2,1,0:T(8,128)(2,1)}, u32[]{:S(2)}) copy-start(bf16[2,128,2048]{2,1,0:T(8,128)(2,1)} %tokens.1) | copy-start | bytes 3145732
  131.8 110.0 %copy-start.17 = (bf16[4,4,2,64,2048]{4,3,2,1,0:T(8,128)(2,1)S(1)}, bf16[4,4,2,64,2048]{4,3,2,1,0:T(8,128)(2,1)}, u32[]{:S(2)}) copy-start(bf16[4,4,2,64,2048]{4,3,2,1,0:T(8,128)(2,1)} %get-tuple-element.57) | copy-start | bytes 25165828
  241.7 2.7 copy-start.2
  241.7 2.6 copy-start.3
  241.8 2.6 copy-start.4
  241.8 2.6 copy-start.5
  241.8 2.6 copy-start.9
  244.4 2.1 copy-start.10
  575.0 5.9 copy-start.20
  575.0 5.9 copy-start.23
  580.9 3.5 copy-start.19
  580.9 4.4 copy-start.22
  585.3 2.9 copy-start.15
  585.3 2.9 copy-start.37
  766.2 2.0 copy-start.13
  766.3 2.3 copy-start.16
  769.9 1.9 copy-start.25
  772.1 2.0 copy-start.11
  774.1 1.9 copy-start.29
  (14 other events, 17.1 us)

commit v9 on v8

--- a/solution.py
+++ b/solution.py
@@ -1391,7 +1391,7 @@
             sent_copies.append(copy)
             if place >= 2:
                 kept_copies[place - 2].wait()
-            kept[place % 2] = product(d)
+            kept[place % 2] = product(d).astype(bf16)
             copy = keep_copy(j, at, place % 2)
             copy.start()
             kept_copies.append(copy)
@@ -1499,9 +1499,9 @@
             jax.ShapeDtypeStruct((1, width), f32),
             jax.ShapeDtypeStruct((batches, count, run, size), bf16),
             jax.ShapeDtypeStruct((C, part, width), bf16),
-            jax.ShapeDtypeStruct(tall, f32),
-            jax.ShapeDtypeStruct(tall, f32),
-            jax.ShapeDtypeStruct(flat, f32),
+            jax.ShapeDtypeStruct(tall, bf16),
+            jax.ShapeDtypeStruct(tall, bf16),
+            jax.ShapeDtypeStruct(flat, bf16),
             jax.ShapeDtypeStruct(tall, bf16),
             jax.ShapeDtypeStruct(tall, bf16),
             jax.ShapeDtypeStruct(flat, bf16),
@@ -1515,7 +1515,7 @@
             pltpu.VMEM((2, size, width), bf16),
             pltpu.VMEM((2, total, units), bf16),
             pltpu.VMEM((2, total, step), bf16),
-            pltpu.VMEM((2, step, half), f32),
+            pltpu.VMEM((2, step, half), bf16),
             pltpu.VMEM((4, step, half), bf16),
             by_plane,
             by_plane,
@@ -2268,7 +2268,7 @@
         "middle",
     )
     grad_gate, grad_up, grad_down = (
-        (mine + other.astype(f32))[None] for mine, other in zip(expert_grads[:3], expert_grads[3:])
+        (mine.astype(f32) + other.astype(f32))[None] for mine, other in zip(expert_grads[:3], expert_grads[3:])
     )
     grad_proj = jnp.sum(grad_proj.astype(f32), axis=0)
     sums = contract(second_low, logit_grad, (0, 0))

time: 781 us -> 780 us (level)
  no operation moved by 1% of the time
where the time goes in v9:
time: 780 us; the launch traced here: 776 us
  Pallas kernels  726 us (93%)
  other arithmetic  22.8 us (3%)
  local copies, waits for them, and re-layouts  19.8 us (3%)
    pallas_call x5, Pallas kernels, call(): pl.pallas_call(kernel, out_shape=out_shapes, in_specs=in_specs, out_specs...  726 us

profile of v9, /device:TPU:1, one launch (start us, length us, event | category | flops | bytes accessed | tf_op | source)
XLA Modules:
  0.0 775.7 jit_solution(2365877492477218007)
XLA Ops:
  1.6 1.0 fusion.4
  3.9 1.1 copy_bitcast_fusion
  5.0 1.0 copy.131
  6.0 0.9 maximum_bitcast_fusion.weights
  7.7 118.5 %start.1 = (bf16[2,8,128,2048]{3,2,1,0:T(8,128)(2,1)}, bf16[4,8,64,768]{3,2,1,0:T(8,128)(2,1)}, bf16[4,8,64,128]{3,2,1,0:T(8,128)(2,1)}, bf16[4,4,2,64,2048]{4,3...) custom-call(bf16[2,128,2048]{2,1,0:T(8,128)(2,1)} %tokens.1, ...), custom_call_target="tpu_custom_call" | custom-call | tf_op jit(solution)/shard_map/start/pallas_call | solution.py:25
  126.2 1.3 copy.119
  128.1 1.1 copy.104.row_ids
  129.9 1.2 copy-done.1
  131.8 109.8 %forward.1 = (bf16[2048,2048]{1,0:T(8,128)(2,1)}, bf16[2048,256]{1,0:T(8,128)(2,1)S(1)}, bf16[2048,256]{1,0:T(8,128)(2,1)S(1)}, bf16[2048,256]{1,0:T(8,128)(2,1)...) custom-call(bf16[2048,2048]{1,0:T(8,128)(2,1)} %bitcast.137, ...), custom_call_target="tpu_custom_call" | custom-call | tf_op jit(solution)/shard_map/forward/pallas_call | solution.py:25
  241.8 2.6 multiply_reduce_fusion.2
  244.7 1.1 copy-done.18
  247.7 220.8 %experts.1 = (bf16[4,2,128,2048]{3,2,1,0:T(8,128)(2,1)}, bf16[4,2,4,64,2048]{4,3,2,1,0:T(8,128)(2,1)}, bf16[4,2,4,64,2048]{4,3,2,1,0:T(8,128)(2,1)}, bf16[4,2,4,...) custom-call(bf16[2,128,2048]{2,1,0:T(8,128)(2,1)} %bitcast.136, ...), custom_call_target="tpu_custom_call" | custom-call | tf_op jit(solution)/shard_map/experts/pallas_call | solution.py:25
  472.2 102.7 %middle.1 = (f32[256,2048]{1,0:T(8,128)}, f32[1,2048]{1,0:T(1,128)}, bf16[2,8,128,256]{3,2,1,0:T(8,128)(2,1)}, bf16[4,64,2048]{2,1,0:T(8,128)(2,1)}, bf16[2048,5...) custom-call(bf16[4,2,128,2048]{3,2,1,0:T(8,128)(2,1)} %get-tuple-ele, ...), custom_call_target="tpu_custom_call" | custom-call | tf_op jit(solution)/shard_map/middle/pallas_call | solution.py:25
  575.0 5.2 add_bitcast_fusion
  580.2 2.8 add_bitcast_fusion.1
  583.0 1.0 copy-done.26
  584.0 2.8 add_bitcast_fusion.2
  586.8 1.4 fusion
  588.2 174.1 %backward.1 = (f32[256,2048]{1,0:T(8,128)}, bf16[8,64,768]{2,1,0:T(8,128)(2,1)}, bf16[8,64,128]{2,1,0:T(8,128)(2,1)}, f32[8,2,1,256]{3,2,1,0:T(1,128)}, bf16[4,128,2048]{2,1,0:T(8,128)(2,1)}) custom-call(bf16[2048,256]{1,0:T(8,128)(2,1)} %copy-done.2, bf16[2048,256]{1,0:T(8,128)(2,1)} %copy-done.3, bf16[2048,256]{1,0:T(8,128)(2,1)} %copy-done.4, ...), custom_call_target="tpu_custom_call" | custom-call | tf_op jit(solution)/shard_map/backward/pallas_call | solution.py:25
  762.4 1.3 convert_bitcast_fusion
  768.4 1.9 multiply_add_fusion
  770.7 1.2 copy-done.20
  772.6 1.2 fusion.1
  774.5 0.9 convert_reduce_fusion
  (126 shorter events, 17.4 us)
Async XLA Ops:
  0.6 6.3 copy-start.36
  0.7 6.3 copy-start.35
  127.5 114.2 %copy-start.8 = (f32[2,256]{1,0:T(2,128)}, f32[2,256]{1,0:T(2,128)S(1)}, u32[]{:S(2)}) copy-start(f32[2,256]{1,0:T(2,128)S(1)} %dynamic-slice_bitcast_fusion.head_gains) | copy-start | bytes 6148
  129.2 112.5 %copy-start = (s32[2,1024,1]{2,1,0:T(8,128)}, s32[2,1024,1]{2,1,0:T(8,128)S(1)}, u32[]{:S(2)}) copy-start(s32[2,1024,1]{2,1,0:T(8,128)S(1)} %copy.104.row_ids) | copy-start | bytes 24580
  129.9 111.8 %copy-start.7 = (s32[2,8,128]{2,1,0:T(8,128)}, s32[2,8,128]{2,1,0:T(8,128)S(1)}, u32[]{:S(2)}) copy-start(s32[2,8,128]{2,1,0:T(8,128)S(1)} %copy.103) | copy-start | bytes 24580
  131.8 109.9 %copy-start.12 = (bf16[2,128,2048]{2,1,0:T(8,128)(2,1)S(1)}, bf16[2,128,2048]{2,1,0:T(8,128)(2,1)}, u32[]{:S(2)}) copy-start(bf16[2,128,2048]{2,1,0:T(8,128)(2,1)} %tokens.1) | copy-start | bytes 3145732
  131.8 110.0 %copy-start.17 = (bf16[4,4,2,64,2048]{4,3,2,1,0:T(8,128)(2,1)S(1)}, bf16[4,4,2,64,2048]{4,3,2,1,0:T(8,128)(2,1)}, u32[]{:S(2)}) copy-start(bf16[4,4,2,64,2048]{4,3,2,1,0:T(8,128)(2,1)} %get-tuple-element.57) | copy-start | bytes 25165828
  241.7 2.7 copy-start.2
  241.7 2.6 copy-start.3
  241.7 2.6 copy-start.4
  241.8 2.6 copy-start.5
  241.8 2.6 copy-start.9
  244.4 2.1 copy-start.10
  575.0 5.2 copy-start.27
  575.0 5.2 copy-start.28
  580.2 2.8 copy-start.25
  580.2 3.7 copy-start.26
  584.0 2.8 copy-start.15
  584.0 2.8 copy-start.37
  764.8 2.0 copy-start.13
  764.8 2.3 copy-start.16
  768.4 1.9 copy-start.21
  770.7 2.0 copy-start.11
  772.6 1.9 copy-start.29
  (14 other events, 17.1 us)
